TPU v7x, 128 devices: a whole 4x4x4 slice. The times are simulated.
128 devices in a mesh: old: 8 (over z, core), new: 16 (over y, x).
Axes of the slice: x: 4, y: 4, z: 4, core: 2. Of those that a mesh axis runs over, the one named last changes fastest.
Arguments:
- old_values: float32 [32, 1048576], P(None, ('old', 'new')), may hold values from -6 to 6
- pair_rows: int32 [128, 128, 128], P(('old', 'new')), may hold values from 0 to 8191
- pair_targets: int32 [128, 128, 128], P(('old', 'new')), may hold values from 0 to 65535
- pair_weights: float32 [128, 128, 128], P(('old', 'new')), may hold values from 0.1 to 1
- pair_counts: int32 [128, 128], P(('old', 'new')), may hold values from 0 to 128, as said below
- cell_area: float32 [2, 512, 8192], P(None, 'new', 'old'), may hold values from 0.5 to 2
- thickness: float32 [2, 512, 8192], P(None, 'new', 'old'), may hold values from 0.5 to 2
- displacement: float32 [3, 512, 8192], P(None, 'new', 'old'), may hold values from -0.05 to 0.05
- velocity: float32 [3, 512, 8192], P(None, 'new', 'old'), may hold values from -3 to 3
Outputs:
- projected: float32 [32, 512, 8192], P(None, 'new', 'old')
- velocity_next: float32 [3, 512, 8192], P(None, 'new', 'old')
Inputs may be any that keep to these rules, and one draw needn't show every extreme that they name: `pair_counts`: at most 128 live slots for every pair; some owner receives 128 from every source, and every source sends 128 to some owner. `pair_targets`: triangle id local to the owner; ids of cells outside the sheet may occur and take nothing.
All inputs are finite; a program needn't handle non-finite values.
Results may differ from a plain program's by a relative error of at most 0.000023.
Values sent between devices are 32-bit elements; how exact they have to be, the bound alone decides.
A program may use at most 128 MiB of HBM per device.

v0:
```python
import jax
import jax.numpy as jnp
from jax import lax
from jax.sharding import PartitionSpec as P

POINTS = 4
COMP = 8
ITERS = 3


MU_BASE = 10.0
LAMBDA_BULK = 20.0
PRESTRESS = 4.0
TIME_STEP = 1.0
GRAVITY = -1.0
EIG_LOW = 0.5
EIG_HIGH = 2.0


def from_behind(block, axis, distance):
    devices = range(lax.axis_size(axis))
    route = [(i - distance, i) for i in devices if i - distance in devices]
    return lax.ppermute(block, axis, route)


def padded_2(block, sides, width):
    for axis, dim in sides:
        count = lax.axis_size(axis)
        forward = [(i, i + 1) for i in range(count - 1)]
        backward = [(target, source) for source, target in forward]
        low = lax.ppermute(
            lax.slice_in_dim(block, block.shape[dim] - width, None, axis=dim), axis, forward
        )
        high = lax.ppermute(lax.slice_in_dim(block, 0, width, axis=dim), axis, backward)
        block = jnp.concatenate([low, block, high], axis=dim)
    return block


def corners(padded):
    return (padded[..., :-1, :-1], padded[..., :-1, 1:], padded[..., 1:, :-1], padded[..., 1:, 1:])


def node_sum(lower_part, upper_part):
    summed = lower_part + upper_part
    return (
        summed[..., 1:, 1:]
        + lower_part[..., 1:, :-1]
        + upper_part[..., :-1, 1:]
        + summed[..., :-1, :-1]
    )


def mass_terms(padded, area_cells):
    anchor, beside, upward, across = corners(padded)
    lower_tri = area_cells[0] / 12.0 * (anchor + beside + across)
    upper_tri = area_cells[1] / 12.0 * (anchor + across + upward)
    return node_sum(lower_tri, upper_tri)


def chebyshev(rhs, weight_diag, apply_mass):
    centre = 0.5 * (EIG_HIGH + EIG_LOW)
    half_width = 0.5 * (EIG_HIGH - EIG_LOW)
    ratio_eig = centre / half_width
    rho_now = 1.0 / ratio_eig
    inv_diag = 1.0 / (2.0 * weight_diag)
    residual = rhs
    direction = inv_diag * residual / centre
    solution = direction
    for sweep in range(ITERS):
        residual = residual - apply_mass(direction)
        rho_next = 1.0 / (2.0 * ratio_eig - rho_now)
        direction = rho_next * rho_now * direction + 2.0 * rho_next / half_width * (
            inv_diag * residual
        )
        solution = solution + direction
        rho_now = rho_next
    return solution


def membrane_fields(projected):
    through = jnp.mean(
        projected.reshape(POINTS, COMP, projected.shape[1], projected.shape[2]), axis=0
    )
    return jnp.stack([through[0], through[1], through[5], through[7]], 0)


def first_piola(stretch_x, stretch_y, fields):
    gram_xx = jnp.sum(stretch_x * stretch_x, axis=0)
    gram_xy = jnp.sum(stretch_x * stretch_y, axis=0)
    gram_yy = jnp.sum(stretch_y * stretch_y, axis=0)
    determinant = gram_xx * gram_yy - gram_xy * gram_xy
    inv_xx = gram_yy / determinant
    inv_xy = -gram_xy / determinant
    inv_yy = gram_xx / determinant
    push_x = stretch_x * inv_xx + stretch_y * inv_xy
    push_y = stretch_x * inv_xy + stretch_y * inv_yy
    shear_mod = MU_BASE * (1.5 + jnp.tanh(fields[3]))
    log_jacobian = 0.5 * jnp.log(determinant)
    piola_x = (
        shear_mod * (stretch_x - push_x)
        + LAMBDA_BULK * log_jacobian * push_x
        + PRESTRESS * (stretch_x * fields[0] + stretch_y * fields[2])
    )
    piola_y = (
        shear_mod * (stretch_y - push_y)
        + LAMBDA_BULK * log_jacobian * push_y
        + PRESTRESS * (stretch_x * fields[2] + stretch_y * fields[1])
    )
    return (piola_x, piola_y)


def triangle_forces(padded, volume):
    anchor, beside, upward, across = corners(padded)
    unit_x = jnp.array([1.0, 0.0, 0.0], jnp.float32)[:, None, None]
    unit_y = jnp.array([0.0, 1.0, 0.0], jnp.float32)[:, None, None]
    lower_x = unit_x + beside[:3] - anchor[:3]
    lower_y = unit_y + across[:3] - beside[:3]
    lower_fields = (anchor[3:] + beside[3:] + across[3:]) / 3.0
    upper_x = unit_x + across[:3] - upward[:3]
    upper_y = unit_y + upward[:3] - anchor[:3]
    upper_fields = (anchor[3:] + across[3:] + upward[3:]) / 3.0
    piola_lx, piola_ly = first_piola(lower_x, lower_y, lower_fields)
    piola_ux, piola_uy = first_piola(upper_x, upper_y, upper_fields)
    force_beside = -volume[0] * (piola_lx - piola_ly)
    force_across_low = -volume[0] * piola_ly
    force_across_up = -volume[1] * piola_ux
    force_upward = -volume[1] * (piola_uy - piola_ux)
    force_anchor = -(force_beside + force_across_low) - (force_across_up + force_upward)
    return (force_anchor, force_beside, force_upward, force_across_low + force_across_up)


def force_sum(force_anchor, force_beside, force_upward, force_across):
    return (
        force_anchor[..., 1:, 1:]
        + force_beside[..., 1:, :-1]
        + force_upward[..., :-1, 1:]
        + force_across[..., :-1, :-1]
    )


def local(
    old_values,
    pair_rows,
    pair_targets,
    pair_weights,
    pair_counts,
    cell_area,
    thickness,
    displacement,
    velocity,
):
    channels = old_values.shape[0]
    slots = pair_rows.shape[2]
    rows_dev = cell_area.shape[1]
    cols_dev = cell_area.shape[2]
    rows_here = pair_rows[0]
    is_live = jnp.arange(slots, dtype=jnp.int32)[None, :] < pair_counts[0][:, None]
    slot_weight = jnp.where(is_live, pair_weights[0], 0.0)
    slot_target = jnp.where(is_live, pair_targets[0], 0)
    picked = old_values[:, rows_here] * slot_weight[None]
    arrived, arrived_ids = (
        lax.all_to_all(picked, ("old", "new"), split_axis=1, concat_axis=1, tiled=True),
        lax.all_to_all(slot_target[None], ("old", "new"), split_axis=1, concat_axis=1, tiled=True),
    )
    empty = jnp.zeros((channels, 2 * rows_dev * cols_dev), jnp.float32)
    element_sums = empty.at[:, arrived_ids.reshape(-1)].add(arrived.reshape(channels, -1))
    element_sums = element_sums.reshape(channels, 2, rows_dev, cols_dev)
    total_rows = rows_dev * lax.axis_size("new")
    total_cols = cols_dev * lax.axis_size("old")
    row_global = lax.axis_index("new") * rows_dev + jnp.arange(rows_dev, dtype=jnp.int32)
    col_global = lax.axis_index("old") * cols_dev + jnp.arange(cols_dev, dtype=jnp.int32)
    valid = (
        (row_global < total_rows - 1)[:, None] & (col_global < total_cols - 1)[None, :]
    ).astype(jnp.float32)
    element_sums = element_sums * valid
    area_valid = cell_area * valid
    volume = thickness * area_valid
    cell_stack = jnp.concatenate([element_sums, area_valid[None], volume[None]], 0)
    lower_row = from_behind(cell_stack[..., -1:, :], "new", 1)
    with_rows = jnp.concatenate([lower_row, cell_stack], 2)
    left_col = from_behind(with_rows[..., -1:], "old", 1)
    cell_data = jnp.concatenate([left_col, with_rows], 3)
    area_cells = cell_data[channels]
    volume_cells = cell_data[channels + 1]
    rhs = node_sum(cell_data[:channels, 0], cell_data[:channels, 1]) / 3.0
    weight_diag = node_sum(area_cells[0] / 12.0, area_cells[1] / 12.0)
    node_mass = node_sum(volume_cells[0] / 3.0, volume_cells[1] / 3.0)

    def apply_mass(field):
        padded = padded_2(field, (("old", 2), ("new", 1)), 1)
        return weight_diag * field + mass_terms(padded, area_cells)

    projected = chebyshev(rhs, weight_diag, apply_mass)
    nodal = jnp.concatenate([displacement, membrane_fields(projected)], 0)
    padded = padded_2(nodal, (("old", 2), ("new", 1)), 1)
    force_anchor, force_beside, force_upward, force_across = triangle_forces(padded, volume_cells)
    forces = force_sum(force_anchor, force_beside, force_upward, force_across)
    gravity_vec = jnp.array([0.0, 0.0, GRAVITY], jnp.float32)[:, None, None]
    velocity_next = velocity + TIME_STEP * (forces / node_mass + gravity_vec)
    return (projected, velocity_next)


def solution(mesh):
    return jax.shard_map(
        local,
        mesh=mesh,
        in_specs=(
            P(None, ("old", "new")),
            P(("old", "new"), None, None),
            P(("old", "new"), None, None),
            P(("old", "new"), None, None),
            P(("old", "new"), None),
            P(None, "new", "old"),
            P(None, "new", "old"),
            P(None, "new", "old"),
            P(None, "new", "old"),
        ),
        out_specs=(P(None, "new", "old"), P(None, "new", "old")),
        check_vma=False,
    )
```

profile of v0, /device:TPU:1, one launch (start us, length us, event | category | flops | bytes accessed | tf_op | source)
XLA Modules:
  0.0 541.1 jit_solution(3534178734056960933)
XLA Ops:
  2.3 11.5 %all-to-all-start = ((s32[1,128,128]{2,0,1:T(1,128)}), s32[1,128,128]{2,0,1:T(1,128)S(1)}, u32[]{:S(2)}, u32[]{:S(2)}) async-start(s32[1,128,128]{2,0,1:T(1,128)} %compare_select_fusion.3), calls=%async_computation | async-start | bytes 131072 | tf_op jit(solution)/shard_map/all_to_all | solution.py:163
  14.9 3.7 copy.48
  18.6 56.7 %gather_fusion = f32[16384,32]{1,0:T(8,128)} fusion(f32[32,8192]{0,1:T(8,128)} %copy.48, s32[16384]{0:T(1024)S(1)} %fusion.53), kind=kCustom, calls=%fused_computation | custom fusion | bytes 4259840 | tf_op jit(solution)/shard_map/gather | solution.py:160
  75.3 5.2 copy.50
  82.9 10.2 %all-to-all-start.1 = ((f32[32,128,128]{2,0,1:T(8,128)}), f32[32,128,128]{2,0,1:T(8,128)}, u32[]{:S(2)}, u32[]{:S(2)}) async-start(f32[32,128,128]{2,0,1:T(8,128)} %multiply_bitcast_fusion), calls=%async_computation.1 | async-start | bytes 4194304 | tf_op jit(solution)/shard_map/all_to_all | solution.py:162
  93.2 29.3 %all-to-all-done.1 = f32[32,128,128]{2,0,1:T(8,128)} async-done(((f32[32,128,128]{2,0,1:T(8,128)}), f32[32,128,128]{2,0,1:T(8,128)}, u32[]{:S(2)}, u32[]{:S(2)}) %all-to-all-start.1) | async-done | bytes 2097184 | tf_op jit(solution)/shard_map/all_to_all | solution.py:162
  122.5 3.0 bitcast_bitcast_fusion
  125.5 6.3 %copy.52 = f32[16384,32]{1,0:T(8,128)} copy(f32[16384,32]{0,1:T(8,128)} %bitcast_bitcast_fusion) | data formatting | bytes 4194304 | tf_op jit(solution)/shard_map/reshape | solution.py:166
  131.8 111.6 %scatter_custom_fusion = f32[32,65536]{0,1:T(8,128)} fusion(s32[16384]{0:T(1024)S(1)} %bitcast.92, f32[16384,32]{1,0:T(8,128)} %copy.52, f32[]{:T(128)} %constant.29.clone.1), kind=kCustom, calls=%fused_computation.2 | custom fusion | flops 524288 | bytes 8389120 | tf_op jit(solution)/shard_map/scatter-add | solution.py:166
  243.4 21.7 %copy.53 = f32[32,2,32,1024]{3,0,2,1:T(8,128)} copy(f32[32,2,32,1024]{0,3,2,1:T(8,128)} %bitcast.79) | data formatting | bytes 16777216 | tf_op jit(solution)/shard_map/reshape | solution.py:167
  265.1 4.5 broadcast_multiply_fusion
  269.7 5.5 %collective-permute-start = (f32[34,2,1,1024]{3,0,2,1:T(8,128)S(1)}, f32[34,2,1,1024]{3,0,2,1:T(8,128)S(1)}, u32[]{:S(2)}, u32[]{:S(2)}) collective-permute-start(f32[34,2,1,1024]{3,0,2,1:T(8,128)S(1)} %pad_maximum_fusion.12), channel_id=1, source_target_pairs={{0,1},{1,2},{2,3},{3,4},{4,5},{5,6},{6,7},{7,8},{8,9},{9,10},{10,1... | collective-permute-start | bytes 835592 | tf_op jit(solution)/shard_map/ppermute | solution.py:23
  275.2 4.4 collective-permute-done
  280.7 10.5 %collective-permute-start.1 = (f32[34,2,33,1]{0,1,3,2:T(2,128)S(1)}, f32[34,2,33,1]{0,1,3,2:T(2,128)S(1)}, u32[]{:S(2)}, u32[]{:S(2)}) collective-permute-start(f32[34,2,33,1]{0,1,3,2:T(2,128)S(1)} %copy.56), channel_id=1, source_target_pairs={{0,16},{16,32},{32,48},{48,64},{64,80},{80,96},{96,112},{1,17},{17... | collective-permute-start | bytes 26936 | tf_op jit(solution)/shard_map/ppermute | solution.py:23
  292.8 11.9 %maximum_maximum_fusion = f32[34,2,33,1025]{3,0,2,1:T(8,128)} fusion(f32[1,2,32,1024]{3,0,2,1:T(1,128)S(1)} %copy.55, f32[1,2,32,1024]{3,0,2,1:T(1,128)S(1)} %copy.54, f32[32,2,32,1024]{3,0,2,1:T(8,128)} %copy-done, f32[34,2,1,1024]{3,0,2,1:T(8,128)S(1)} %collective-permute-done, f32[34,2,33,1]{3,0,2,1:T(8,128)S(1)} %copy.57), kind=kLoop, calls=%fused_computation.4 | loop fusion | flops 9200400 | bytes 18400800 | tf_op jit(solution)/shard_map/concatenate | solution.py:182
  304.7 6.9 %slice_bitcast_fusion.1 = (f32[32,33,1025]{2,0,1:T(8,128)S(1)}, f32[32,33,1025]{2,0,1:T(8,128)}) fusion(f32[34,2,33,1025]{3,0,2,1:T(8,128)} %maximum_maximum_fusion), kind=kLoop, calls=%fused_computation.33 | loop fusion | bytes 17318400 | tf_op jit(solution)/shard_map/squeeze | solution.py:185
  311.5 4.4 fusion.56
  316.0 2.8 broadcast_multiply_fusion.3
  321.8 5.6 %multiply_multiply_fusion = (f32[32,32,1024]{2,0,1:T(8,128)S(1)}, f32[32,32,1024]{2,0,1:T(8,128)}) fusion(f32[32,1024]{1,0:T(8,128)S(1)} %get-tuple-element.91, f32[32,33,1025]{2,0,1:T(8,128)S(1)} %fusion.56, f32[32,33,1025]{2,0,1:T(8,128)} %get-tuple-element.42, f32[32,33,1025]{2,0,1:T(8,128)S(1)} %get-tuple-element.41), kind=kLoop, calls=%fused_computation.59 | loop fusion | flops 5242880 | bytes 25296896 | tf_op jit(solution)/shard_map/div | solution.py:67
  329.7 4.2 collective-permute-start.2
  335.8 4.2 collective-permute-done.2
  340.0 4.4 collective-permute-done.3
  344.4 6.4 %concatenate.64 = f32[32,32,1026]{2,0,1:T(8,128)} concatenate(f32[32,32,1]{2,0,1:T(8,128)S(1)} %collective-permute-done.2, f32[32,32,1024]{2,0,1:T(8,128)} %copy-done.4, f32[32,32,1]{2,0,1:T(8,128)S(1)} %collective-permute-done.3), dimensions={2} | concatenate | bytes 8404992 | tf_op jit(solution)/shard_map/concatenate | solution.py:35
  351.8 4.1 collective-permute-start.4
  358.0 4.1 collective-permute-done.5
  362.1 16.9 %fusion.67 = (f32[32,33,1025]{2,0,1:T(8,128)S(1)}, f32[32,33,1025]{2,0,1:T(8,128)S(1)}, f32[32,33,1025]{2,0,1:T(8,128)S(1)}) fusion(f32[32,1,1026]{2,0,1:T(8,128)S(1)} %collective-permute-done.5, f32[32,32,1026]{2,0,1:T(8,128)} %concatenate.64, f32[32,1,1026]{2,0,1:T(8,128)S(1)} %collective-permute-done.4, f32[33,1025]{1,0:T(8,128)S(1)} %get-tuple-element.93, ...), kind=kLoop, calls=%fused_computation.180 | loop fusion | flops 14071200 | bytes 17724552 | tf_op jit(solution)/shard_map/add | solution.py:44
  379.0 4.7 multiply_add_fusion.1
  385.9 3.2 collective-permute-start.6
  391.0 4.2 collective-permute-done.6
  395.2 4.4 collective-permute-done.7
  399.6 6.4 %concatenate.67 = f32[32,32,1026]{2,0,1:T(8,128)} concatenate(f32[32,32,1]{2,0,1:T(8,128)S(1)} %collective-permute-done.6, f32[32,32,1024]{2,0,1:T(8,128)} %copy-done.1, f32[32,32,1]{2,0,1:T(8,128)S(1)} %collective-permute-done.7), dimensions={2} | concatenate | bytes 8404992 | tf_op jit(solution)/shard_map/concatenate | solution.py:35
  406.9 2.8 collective-permute-start.8
  411.9 6.9 %collective-permute-done.9 = f32[32,1,1026]{2,0,1:T(8,128)S(1)} collective-permute-done((f32[32,1,1026]{2,0,1:T(8,128)S(1)}, f32[32,1,1026]{2,0,1:T(8,128)S(1)}, u32[]{:S(2)}, u32[]{:S(2)}) %collective-permute-start.9) | collective-permute-done | bytes 131360 | tf_op jit(solution)/shard_map/ppermute | solution.py:34
  418.8 18.5 %fusion.63 = (f32[32,33,1025]{2,0,1:T(8,128)S(1)}, f32[32,33,1025]{2,0,1:T(8,128)S(1)}, f32[32,33,1025]{2,0,1:T(8,128)}) fusion(f32[32,1,1026]{2,0,1:T(8,128)S(1)} %collective-permute-done.9, f32[32,32,1026]{2,0,1:T(8,128)} %concatenate.67, f32[32,1,1026]{2,0,1:T(8,128)S(1)} %collective-permute-done.8, f32[33,1025]{1,0:T(8,128)S(1)} %get-tuple-element.93, ...), kind=kLoop, calls=%fused_computation.179 | loop fusion | flops 14071200 | bytes 17724552 | tf_op jit(solution)/shard_map/add | solution.py:44
  437.3 6.6 %multiply_add_fusion = (f32[32,32,1024]{2,0,1:T(8,128)S(1)}, f32[32,32,1024]{2,0,1:T(8,128)}) fusion(f32[32,32,1024]{2,0,1:T(8,128)S(1)} %copy-done.2, f32[32,1024]{1,0:T(8,128)S(1)} %get-tuple-element.34, f32[32,32,1024]{2,0,1:T(8,128)} %get-tuple-element.33, f32[32,33,1025]{2,0,1:T(8,128)S(1)} %get-tuple-element.29, ...), kind=kLoop, calls=%fused_computation.56 | loop fusion | flops 10485760 | bytes 33816576 | tf_op jit(solution)/shard_map/add | solution.py:72
  446.0 4.1 collective-permute-start.10
  452.1 4.2 collective-permute-done.10
  456.3 4.4 collective-permute-done.11
  460.7 6.4 %concatenate.70 = f32[32,32,1026]{2,0,1:T(8,128)} concatenate(f32[32,32,1]{2,0,1:T(8,128)S(1)} %collective-permute-done.10, f32[32,32,1024]{2,0,1:T(8,128)} %copy-done.6, f32[32,32,1]{2,0,1:T(8,128)S(1)} %collective-permute-done.11), dimensions={2} | concatenate | bytes 8404992 | tf_op jit(solution)/shard_map/concatenate | solution.py:35
  468.1 5.5 %collective-permute-start.12 = (f32[32,1,1026]{2,0,1:T(8,128)S(1)}, f32[32,1,1026]{2,0,1:T(8,128)S(1)}, u32[]{:S(2)}, u32[]{:S(2)}) collective-permute-start(f32[32,1,1026]{2,0,1:T(8,128)S(1)} %get-tuple-element.45), channel_id=1, source_target_pairs={{0,1},{1,2},{2,3},{3,4},{4,5},{5,6},{6,7},{7,8},{8,9},{9,10},{10,1... | collective-permute-start | bytes 393992 | tf_op jit(solution)/shard_map/ppermute | solution.py:31
  475.6 4.2 collective-permute-done.13
  479.9 18.5 %fusion.59 = (f32[32,33,1025]{2,0,1:T(8,128)S(1)}, f32[32,33,1025]{2,0,1:T(8,128)S(1)}, f32[32,33,1025]{2,0,1:T(8,128)}) fusion(f32[32,1,1026]{2,0,1:T(8,128)S(1)} %collective-permute-done.13, f32[32,32,1026]{2,0,1:T(8,128)} %concatenate.70, f32[32,1,1026]{2,0,1:T(8,128)S(1)} %collective-permute-done.12, f32[33,1025]{1,0:T(8,128)S(1)} %get-tuple-element.93, ...), kind=kLoop, calls=%fused_computation.178 | loop fusion | flops 14071200 | bytes 17724552 | tf_op jit(solution)/shard_map/add | solution.py:44
  498.3 7.4 %fusion.22 = f32[32,32,1024]{2,0,1:T(8,128)} fusion(f32[32,32,1024]{2,0,1:T(8,128)} %get-tuple-element.28, f32[32,33,1025]{2,0,1:T(8,128)S(1)} %get-tuple-element.24, f32[32,33,1025]{2,0,1:T(8,128)S(1)} %get-tuple-element.25, f32[32,33,1025]{2,0,1:T(8,128)} %get-tuple-element.26, f32[32,32,1024]{2,0,1:T(8,128)S(1)} %copy-done.5, ...), kind=kLoop, calls=%fused_computation.40 | loop fusion | flops 17825792 | bytes 33816576 | tf_op jit(solution)/shard_map/add | solution.py:75
  505.7 6.6 %copy.59 = f32[32,32,1024]{2,1,0:T(8,128)} copy(f32[32,32,1024]{2,0,1:T(8,128)} %fusion.22) | data formatting | bytes 8388608
  512.4 2.7 reduce_sum.63
  516.5 3.5 collective-permute-start.14
  522.0 4.3 collective-permute-done.15
  527.8 4.0 collective-permute-start.16
  (108 shorter events, 46.1 us)
Async XLA Ops:
  0.6 18.0 %copy-start.14 = (s32[1,128,128]{2,1,0:T(8,128)S(1)}, s32[1,128,128]{2,1,0:T(8,128)}, u32[]{:S(2)}) copy-start(s32[1,128,128]{2,1,0:T(8,128)} %param.13) | copy-start | bytes 196612
  2.3 80.5 %all-to-all-start = ((s32[1,128,128]{2,0,1:T(1,128)}), s32[1,128,128]{2,0,1:T(1,128)S(1)}, u32[]{:S(2)}, u32[]{:S(2)}) async-start(s32[1,128,128]{2,0,1:T(1,128)} %compare_select_fusion.3), calls=%async_computation | async-start | bytes 131072 | tf_op jit(solution)/shard_map/all_to_all | solution.py:163
  75.3 6.9 %copy-start.12 = (f32[2,32,1024]{2,1,0:T(8,128)S(1)}, f32[2,32,1024]{2,1,0:T(8,128)}, u32[]{:S(2)}) copy-start(f32[2,32,1024]{2,1,0:T(8,128)} %param.17) | copy-start | bytes 786436
  75.3 6.9 %copy-start.13 = (f32[2,32,1024]{2,1,0:T(8,128)S(1)}, f32[2,32,1024]{2,1,0:T(8,128)}, u32[]{:S(2)}) copy-start(f32[2,32,1024]{2,1,0:T(8,128)} %param.18) | copy-start | bytes 786436
  82.9 39.6 %all-to-all-start.1 = ((f32[32,128,128]{2,0,1:T(8,128)}), f32[32,128,128]{2,0,1:T(8,128)}, u32[]{:S(2)}, u32[]{:S(2)}) async-start(f32[32,128,128]{2,0,1:T(8,128)} %multiply_bitcast_fusion), calls=%async_computation.1 | async-start | bytes 4194304 | tf_op jit(solution)/shard_map/all_to_all | solution.py:162
  269.6 10.0 %copy-start = (f32[32,2,32,1024]{3,0,2,1:T(8,128)}, f32[32,2,32,1024]{3,0,2,1:T(8,128)S(1)}, u32[]{:S(2)}) copy-start(f32[32,2,32,1024]{3,0,2,1:T(8,128)S(1)} %broadcast_multiply_fusion) | copy-start | bytes 25165828
  269.7 9.9 %collective-permute-start = (f32[34,2,1,1024]{3,0,2,1:T(8,128)S(1)}, f32[34,2,1,1024]{3,0,2,1:T(8,128)S(1)}, u32[]{:S(2)}, u32[]{:S(2)}) collective-permute-start(f32[34,2,1,1024]{3,0,2,1:T(8,128)S(1)} %pad_maximum_fusion.12), channel_id=1, source_target_pairs={{0,1},{1,2},{2,3},{3,4},{4,5},{5,6},{6,7},{7,8},{8,9},{9,10},{10,1... | collective-permute-start | bytes 835592 | tf_op jit(solution)/shard_map/ppermute | solution.py:23
  280.7 11.5 %collective-permute-start.1 = (f32[34,2,33,1]{0,1,3,2:T(2,128)S(1)}, f32[34,2,33,1]{0,1,3,2:T(2,128)S(1)}, u32[]{:S(2)}, u32[]{:S(2)}) collective-permute-start(f32[34,2,33,1]{0,1,3,2:T(2,128)S(1)} %copy.56), channel_id=1, source_target_pairs={{0,16},{16,32},{32,48},{48,64},{64,80},{80,96},{96,112},{1,17},{17... | collective-permute-start | bytes 26936 | tf_op jit(solution)/shard_map/ppermute | solution.py:23
  292.8 23.2 %slice-start = ((s8[8388608]{0:T(1024)(128)(4,1)}), s8[4194304]{0:T(1024)(128)(4,1)S(1)}, s32[]{:S(2)}) async-start(s8[8388608]{0:T(1024)(128)(4,1)} %bitcast.77), calls=%async_computation.2 | async-start | bytes 8388608
  304.7 11.3 %slice-start.1 = ((s8[8388608]{0:T(1024)(128)(4,1)}), s8[4194304]{0:T(1024)(128)(4,1)S(1)}, s32[]{:S(2)}) async-start(s8[8388608]{0:T(1024)(128)(4,1)} %bitcast.77), calls=%async_computation.3 | async-start | bytes 8388608
  327.4 2.1 copy-start.4
  329.7 10.3 %collective-permute-start.2 = (f32[32,32,1]{2,0,1:T(8,128)S(1)}, f32[32,32,1]{2,0,1:T(8,128)S(1)}, u32[]{:S(2)}, u32[]{:S(2)}) collective-permute-start(f32[32,32,1]{2,0,1:T(8,128)S(1)} %get-tuple-element.56), channel_id=1, source_target_pairs={{0,16},{16,32},{32,48},{48,64},{64,80},{80,96},{96,112},{1,17},{17... | collective-permute-start | bytes 12296 | tf_op jit(solution)/shard_map/ppermute | solution.py:31
  333.9 10.5 %collective-permute-start.3 = (f32[32,32,1]{2,0,1:T(8,128)S(1)}, f32[32,32,1]{2,0,1:T(8,128)S(1)}, u32[]{:S(2)}, u32[]{:S(2)}) collective-permute-start(f32[32,32,1]{2,0,1:T(8,128)S(1)} %get-tuple-element.55), channel_id=1, source_target_pairs={{16,0},{32,16},{48,32},{64,48},{80,64},{96,80},{112,96},{17,1},{33... | collective-permute-start | bytes 12296 | tf_op jit(solution)/shard_map/ppermute | solution.py:34
  351.8 6.2 %collective-permute-start.4 = (f32[32,1,1026]{2,0,1:T(8,128)S(1)}, f32[32,1,1026]{2,0,1:T(8,128)S(1)}, u32[]{:S(2)}, u32[]{:S(2)}) collective-permute-start(f32[32,1,1026]{2,0,1:T(8,128)S(1)} %get-tuple-element.49), channel_id=1, source_target_pairs={{0,1},{1,2},{2,3},{3,4},{4,5},{5,6},{6,7},{7,8},{8,9},{9,10},{10,1... | collective-permute-start | bytes 393992 | tf_op jit(solution)/shard_map/ppermute | solution.py:31
  355.9 23.0 %copy-start.7 = (f32[32,32,1024]{2,0,1:T(8,128)S(1)}, f32[32,32,1024]{2,0,1:T(8,128)}, u32[]{:S(2)}) copy-start(f32[32,32,1024]{2,0,1:T(8,128)} %get-tuple-element.40) | copy-start | bytes 12582916
  355.9 6.2 %collective-permute-start.5 = (f32[32,1,1026]{2,0,1:T(8,128)S(1)}, f32[32,1,1026]{2,0,1:T(8,128)S(1)}, u32[]{:S(2)}, u32[]{:S(2)}) collective-permute-start(f32[32,1,1026]{2,0,1:T(8,128)S(1)} %get-tuple-element.50), channel_id=1, source_target_pairs={{1,0},{2,1},{3,2},{4,3},{5,4},{6,5},{7,6},{8,7},{9,8},{10,9},{11,1... | collective-permute-start | bytes 393992 | tf_op jit(solution)/shard_map/ppermute | solution.py:34
  383.7 2.0 copy-start.1
  385.9 9.3 %collective-permute-start.6 = (f32[32,32,1]{2,0,1:T(8,128)S(1)}, f32[32,32,1]{2,0,1:T(8,128)S(1)}, u32[]{:S(2)}, u32[]{:S(2)}) collective-permute-start(f32[32,32,1]{2,0,1:T(8,128)S(1)} %get-tuple-element.54), channel_id=1, source_target_pairs={{0,16},{16,32},{32,48},{48,64},{64,80},{80,96},{96,112},{1,17},{17... | collective-permute-start | bytes 12296 | tf_op jit(solution)/shard_map/ppermute | solution.py:31
  389.1 10.5 %collective-permute-start.7 = (f32[32,32,1]{2,0,1:T(8,128)S(1)}, f32[32,32,1]{2,0,1:T(8,128)S(1)}, u32[]{:S(2)}, u32[]{:S(2)}) collective-permute-start(f32[32,32,1]{2,0,1:T(8,128)S(1)} %get-tuple-element.53), channel_id=1, source_target_pairs={{16,0},{32,16},{48,32},{64,48},{80,64},{96,80},{112,96},{17,1},{33... | collective-permute-start | bytes 12296 | tf_op jit(solution)/shard_map/ppermute | solution.py:34
  406.9 4.9 collective-permute-start.8
  409.8 27.5 %copy-start.2 = (f32[32,32,1024]{2,0,1:T(8,128)S(1)}, f32[32,32,1024]{2,0,1:T(8,128)}, u32[]{:S(2)}) copy-start(f32[32,32,1024]{2,0,1:T(8,128)} %copy-done.1) | copy-start | bytes 12582916
  409.8 9.0 %collective-permute-start.9 = (f32[32,1,1026]{2,0,1:T(8,128)S(1)}, f32[32,1,1026]{2,0,1:T(8,128)S(1)}, u32[]{:S(2)}, u32[]{:S(2)}) collective-permute-start(f32[32,1,1026]{2,0,1:T(8,128)S(1)} %get-tuple-element.48), channel_id=1, source_target_pairs={{1,0},{2,1},{3,2},{4,3},{5,4},{6,5},{7,6},{8,7},{9,8},{10,9},{11,1... | collective-permute-start | bytes 393992 | tf_op jit(solution)/shard_map/ppermute | solution.py:34
  443.8 2.0 copy-start.6
  446.0 10.2 %collective-permute-start.10 = (f32[32,32,1]{2,0,1:T(8,128)S(1)}, f32[32,32,1]{2,0,1:T(8,128)S(1)}, u32[]{:S(2)}, u32[]{:S(2)}) collective-permute-start(f32[32,32,1]{2,0,1:T(8,128)S(1)} %get-tuple-element.52), channel_id=1, source_target_pairs={{0,16},{16,32},{32,48},{48,64},{64,80},{80,96},{96,112},{1,17},{17... | collective-permute-start | bytes 12296 | tf_op jit(solution)/shard_map/ppermute | solution.py:31
  450.2 10.5 %collective-permute-start.11 = (f32[32,32,1]{2,0,1:T(8,128)S(1)}, f32[32,32,1]{2,0,1:T(8,128)S(1)}, u32[]{:S(2)}, u32[]{:S(2)}) collective-permute-start(f32[32,32,1]{2,0,1:T(8,128)S(1)} %get-tuple-element.51), channel_id=1, source_target_pairs={{16,0},{32,16},{48,32},{64,48},{80,64},{96,80},{112,96},{17,1},{33... | collective-permute-start | bytes 12296 | tf_op jit(solution)/shard_map/ppermute | solution.py:34
  468.1 7.6 %collective-permute-start.12 = (f32[32,1,1026]{2,0,1:T(8,128)S(1)}, f32[32,1,1026]{2,0,1:T(8,128)S(1)}, u32[]{:S(2)}, u32[]{:S(2)}) collective-permute-start(f32[32,1,1026]{2,0,1:T(8,128)S(1)} %get-tuple-element.45), channel_id=1, source_target_pairs={{0,1},{1,2},{2,3},{3,4},{4,5},{5,6},{6,7},{7,8},{8,9},{9,10},{10,1... | collective-permute-start | bytes 393992 | tf_op jit(solution)/shard_map/ppermute | solution.py:31
  473.5 24.8 %copy-start.3 = (f32[32,32,1024]{2,0,1:T(8,128)S(1)}, f32[32,32,1024]{2,0,1:T(8,128)}, u32[]{:S(2)}) copy-start(f32[32,32,1024]{2,0,1:T(8,128)} %copy-done.1) | copy-start | bytes 12582916
  473.6 24.8 %copy-start.5 = (f32[32,32,1024]{2,0,1:T(8,128)S(1)}, f32[32,32,1024]{2,0,1:T(8,128)}, u32[]{:S(2)}) copy-start(f32[32,32,1024]{2,0,1:T(8,128)} %copy-done.4) | copy-start | bytes 12582916
  473.6 6.3 %collective-permute-start.13 = (f32[32,1,1026]{2,0,1:T(8,128)S(1)}, f32[32,1,1026]{2,0,1:T(8,128)S(1)}, u32[]{:S(2)}, u32[]{:S(2)}) collective-permute-start(f32[32,1,1026]{2,0,1:T(8,128)S(1)} %get-tuple-element.46), channel_id=1, source_target_pairs={{1,0},{2,1},{3,2},{4,3},{5,4},{6,5},{7,6},{8,7},{9,8},{10,9},{11,1... | collective-permute-start | bytes 393992 | tf_op jit(solution)/shard_map/ppermute | solution.py:34
  515.1 18.3 %copy-start.10 = (f32[33,1025]{1,0:T(8,128)S(1)}, f32[33,1025]{1,0:T(8,128)}, u32[]{:S(2)}) copy-start(f32[33,1025]{1,0:T(8,128)} %get-tuple-element.92) | copy-start | bytes 405904
  515.1 18.5 %copy-start.8 = (f32[1,1,33,1025]{3,0,2,1:T(1,128)S(1)}, f32[1,1,33,1025]{3,0,2,1:T(1,128)}, u32[]{:S(2)}) copy-start(f32[1,1,33,1025]{3,0,2,1:T(1,128)} %get-tuple-element.15) | copy-start | bytes 405904
  515.1 18.6 %copy-start.9 = (f32[1,1,33,1025]{3,0,2,1:T(1,128)S(1)}, f32[1,1,33,1025]{3,0,2,1:T(1,128)}, u32[]{:S(2)}) copy-start(f32[1,1,33,1025]{3,0,2,1:T(1,128)} %get-tuple-element.13) | copy-start | bytes 405904
  515.1 21.4 %copy-start.16 = (f32[3]{0:T(128)S(1)}, f32[3]{0:T(128)}, u32[]{:S(2)}) copy-start(f32[3]{0:T(128)} %constant.80.clone) | copy-start | bytes 40
  515.1 21.4 %copy-start.17 = (f32[3]{0:T(128)S(1)}, f32[3]{0:T(128)}, u32[]{:S(2)}) copy-start(f32[3]{0:T(128)} %constant.81.clone) | copy-start | bytes 40
  516.5 5.5 %collective-permute-start.14 = (f32[7,32,1]{2,1,0:T(8,128)S(1)}, f32[7,32,1]{2,1,0:T(8,128)S(1)}, u32[]{:S(2)}, u32[]{:S(2)}) collective-permute-start(f32[7,32,1]{2,1,0:T(8,128)S(1)} %get-tuple-element.73), channel_id=1, source_target_pairs={{0,16},{16,32},{32,48},{48,64},{64,80},{80,96},{96,112},{1,17},{17... | collective-permute-start | bytes 2696 | tf_op jit(solution)/shard_map/ppermute | solution.py:31
  520.1 6.2 %collective-permute-start.15 = (f32[7,32,1]{2,1,0:T(8,128)S(1)}, f32[7,32,1]{2,1,0:T(8,128)}, u32[]{:S(2)}, u32[]{:S(2)}) collective-permute-start(f32[7,32,1]{2,1,0:T(8,128)S(1)} %get-tuple-element.72), channel_id=1, source_target_pairs={{16,0},{32,16},{48,32},{64,48},{80,64},{96,80},{112,96},{17,1},{33... | collective-permute-start | bytes 2696 | tf_op jit(solution)/shard_map/ppermute | solution.py:34
  527.8 6.1 %collective-permute-start.16 = (f32[7,1,1026]{2,1,0:T(1,128)S(1)}, f32[7,1,1026]{2,1,0:T(1,128)S(1)}, u32[]{:S(2)}, u32[]{:S(2)}) collective-permute-start(f32[7,1,1026]{2,1,0:T(1,128)S(1)} %get-tuple-element.70), channel_id=1, source_target_pairs={{0,1},{1,2},{2,3},{3,4},{4,5},{5,6},{6,7},{7,8},{8,9},{9,10},{10,1... | collective-permute-start | bytes 86192 | tf_op jit(solution)/shard_map/ppermute | solution.py:31
  531.9 4.7 collective-permute-start.17
  538.3 1.1 copy-start.11
  538.3 1.1 copy-start.15
where the time goes:
time: 552 us; the launch traced here: 541 us
  other arithmetic  229 us (41%)
  local copies, waits for them, and re-layouts  143 us (26%)
  waiting for transfers between devices  83.6 us (15%)
  starting transfers between devices  83.5 us (15%)
    scatter-add x1, other arithmetic, local(): empty.at[:, arrived_ids.reshape(-1)].add(arrived.reshape(channels, -1))  112 us
    gather x2, local copies, waits for them, and re-layouts, local(): picked = old_values[:, rows_here] * slot_weight[None]  61.8 us
    add x5, other arithmetic, node_sum(): summed = lower_part + upper_part  58.3 us
    ppermute x8, waiting for transfers between devices, padded_2(): lax.ppermute(lax.slice_in_dim(block, 0, width, axis=dim), axis, backward)  35.3 us
    ppermute x8, starting transfers between devices, padded_2(): lax.ppermute(lax.slice_in_dim(block, block.shape[dim] - width, None, axis...  31.5 us
    all_to_all x1, waiting for transfers between devices, local(): lax.all_to_all(picked, ('old', 'new'), split_axis=1, concat_axis=1, tiled...  29.3 us
    reshape x1, local copies, waits for them, and re-layouts, local(): element_sums = element_sums.reshape(channels, 2, rows_dev, cols_dev)  21.7 us
    concatenate x4, local copies, waits for them, and re-layouts, padded_2(): block = jnp.concatenate([low, block, high], axis=dim)  20.6 us
  transfers between devices with their start and end apart: 20, of which 17 were waited for; matrix products, arithmetic and copies ran while one was open for 13% of the time, Pallas kernels for 0%

commit v1 on v0

v1 whole, which is shorter than its diff:
```python
import functools

import jax
import jax.numpy as jnp
from jax import lax
from jax.experimental import pallas as pl
from jax.experimental.pallas import tpu as pltpu
from jax.sharding import PartitionSpec as P

POINTS = 4
COMP = 8
ITERS = 3
MU_BASE = 10.0
LAMBDA_BULK = 20.0
PRESTRESS = 4.0
TIME_STEP = 1.0
GRAVITY = -1.0
EIG_LOW = 0.5
EIG_HIGH = 2.0

LANE = 128
FRONT = 8
BATCH = 4
HALO = 4
MESH = pl.DeviceIdType.MESH
MIB = 1024 * 1024

VMEM = pl.BlockSpec(memory_space=pltpu.VMEM)
SMEM = pl.BlockSpec(memory_space=pltpu.SMEM)
ANY = pl.BlockSpec(memory_space=pl.ANY)


def lane_ids(shape):
    return lax.broadcasted_iota(jnp.int32, shape, len(shape) - 1)


def gather_kernel(counts, rows, weights, values, out, table):
    ranks = out.shape[0]
    per = out.shape[1] * 4
    channels, total = values.shape

    def flip(step, _):
        start = pl.multiple_of(step * LANE, LANE)
        part = values[:, pl.ds(start, LANE)]
        table[pl.ds(start, LANE), :] = jnp.concatenate([part] * 4, axis=0).T
        return 0

    lax.fori_loop(0, total // LANE, flip, 0)
    lane = lane_ids((1, LANE))
    first, second, third = lane < 32, lane < 64, lane < 96

    def one_owner(owner, _):
        blocks = (counts[owner] + 31) // 32
        for block in range(per // 32):

            @pl.when(block < blocks)
            def _():
                for row in range(8):
                    base = owner * per + block * 32 + row * 4
                    part = [
                        table[pl.ds(rows[base + g], 1), :] * weights[base + g] for g in range(4)
                    ]
                    merged = jnp.where(
                        first,
                        part[0],
                        jnp.where(second, part[1], jnp.where(third, part[2], part[3])),
                    )
                    out[owner, pl.ds(block * 8 + row, 1), :] = merged

            @pl.when(block >= blocks)
            def _():
                out[owner, pl.ds(block * 8, 8), :] = jnp.zeros((8, LANE), jnp.float32)

        return 0

    lax.fori_loop(0, ranks, one_owner, 0)


def gather(counts, rows, weights, values):
    ranks, per = rows.shape
    return pl.pallas_call(
        gather_kernel,
        out_shape=jax.ShapeDtypeStruct((ranks, per // 4, LANE), jnp.float32),
        in_specs=[SMEM, SMEM, SMEM, VMEM],
        out_specs=VMEM,
        scratch_shapes=[pltpu.VMEM((values.shape[1], LANE), jnp.float32)],
        compiler_params=pltpu.CompilerParams(vmem_limit_bytes=24 * MIB),
        name="gather",
    )(counts, rows.reshape(-1), weights.reshape(-1), values)


def scatter_kernel(rows_dev, cols_dev, ids, clash, data, part, right_tile, acc):
    width = cols_dev + LANE
    ranks, payload, _ = data.shape
    per = payload * 4
    size = acc.shape[0]
    chunk = width // 8
    zeros = jnp.zeros((chunk, LANE), jnp.float32)
    acc[pl.ds(0, FRONT), :] = jnp.zeros((FRONT, LANE), jnp.float32)

    def clear(step, _):
        acc[pl.ds(pl.multiple_of(FRONT + step * chunk, 8), chunk), :] = zeros
        return 0

    lax.fori_loop(0, (size - FRONT) // chunk, clear, 0)

    lane = lane_ids((1, LANE))
    masks = [(lane >= 32 * g) & (lane < 32 * g + 32) for g in range(4)]

    def add_rows(source, first, count):
        slots = [(r, g) for r in range(count) for g in range(4)]
        where_to = [ids[source * per + (first + r) * 4 + g] for r, g in slots]
        new = [data[source, pl.ds(first + r, 1), :] for r in range(count)]
        old = [acc[pl.ds(row, 1), :] for row in where_to]
        for (r, g), row, have in zip(slots, where_to, old):
            pltpu.store(acc.at[pl.ds(row, 1), :], have + new[r], mask=masks[g])

    def one_source(source, _):
        @pl.when(clash[source] == 0)
        def _():
            for first in range(0, payload, BATCH):
                add_rows(source, first, BATCH)

        @pl.when(clash[source] != 0)
        def _():
            def slow(row, _):
                add_rows(source, row, 1)
                return 0

            lax.fori_loop(0, payload, slow, 0)

        return 0

    lax.fori_loop(0, ranks, one_source, 0)

    def fold(total):
        flipped = total.T
        return flipped[0:32] + flipped[32:64] + flipped[64:96] + flipped[96:128]

    upper_base = rows_dev * width
    for tile in range(width // LANE):

        def one_row(i, carry, tile=tile):
            base = i * width + tile * LANE + FRONT
            lower = acc[pl.ds(base, LANE), :]
            upper = acc[pl.ds(base + upper_base, LANE), :]
            lower_left = acc[pl.ds(base - 1, LANE), :]
            upper_left = acc[pl.ds(base + upper_base - 1, LANE), :]
            shared = upper + lower_left
            part[i, :, tile * LANE : (tile + 1) * LANE] = fold(lower + shared + carry)
            return shared + upper_left

        last = lax.fori_loop(0, rows_dev, one_row, jnp.zeros((LANE, LANE), jnp.float32))
        part[rows_dev, :, tile * LANE : (tile + 1) * LANE] = fold(last)

    edge = lane_ids((part.shape[1], LANE))

    def pack(i, _):
        own = part[i, :, cols_dev - LANE : cols_dev]
        ghost = part[i, :, cols_dev:width]
        right_tile[i] = jnp.where(edge >= 64, own, jnp.where(edge == 0, ghost, 0.0))
        return 0

    lax.fori_loop(0, rows_dev + 1, pack, 0)


def scatter(ids, clash, data, rows_dev, cols_dev):
    channels = LANE // 4
    width = cols_dev + LANE
    return pl.pallas_call(
        functools.partial(scatter_kernel, rows_dev, cols_dev),
        out_shape=(
            jax.ShapeDtypeStruct((rows_dev + 1, channels, width), jnp.float32),
            jax.ShapeDtypeStruct((rows_dev + 1, channels, LANE), jnp.float32),
        ),
        in_specs=[SMEM, SMEM, VMEM],
        out_specs=(VMEM, VMEM),
        scratch_shapes=[pltpu.VMEM((FRONT + 2 * rows_dev * width, LANE), jnp.float32)],
        compiler_params=pltpu.CompilerParams(vmem_limit_bytes=56 * MIB),
        name="scatter",
    )(ids.reshape(-1), clash, data)


def exchange_kernel(pick, body, edge, *refs):
    outs, send_sem, recv_sem = refs[:-2], refs[-2], refs[-1]
    n_old, n_new = lax.axis_size("old"), lax.axis_size("new")
    old, new = lax.axis_index("old"), lax.axis_index("new")
    left, right = lax.rem(old + n_old - 1, n_old), lax.rem(old + 1, n_old)
    below, above = lax.rem(new + n_new - 1, n_new), lax.rem(new + 1, n_new)
    around = [
        (old, above),
        (old, below),
        (right, new),
        (left, new),
        (right, above),
        (left, above),
        (right, below),
        (left, below),
    ]
    barrier = pltpu.get_barrier_semaphore()
    for device in around:
        pl.semaphore_signal(barrier, inc=1, device_id=device, device_id_type=MESH)
    pl.semaphore_wait(barrier, len(around))
    copies = [
        pltpu.make_async_remote_copy(
            src_ref=source,
            dst_ref=target,
            send_sem=send_sem.at[at],
            recv_sem=recv_sem.at[at],
            device_id=device,
            device_id_type=MESH,
        )
        for at, (source, target, device) in enumerate(zip(pick(body, edge), outs, around))
    ]
    for copy in copies:
        copy.start()
    for copy in copies:
        copy.wait()


def pick_partial(body, edge):
    top, low = pl.ds(body.shape[0] - HALO - 1, HALO + 1), pl.ds(0, HALO)
    near = pl.ds(0, LANE)
    return [
        body.at[top],
        body.at[low],
        edge,
        body.at[:, :, near],
        edge.at[top],
        body.at[top, :, near],
        edge.at[low],
        body.at[low, :, near],
    ]


def pick_fields(body, edge):
    rows, cols = body.shape[1:]
    top, low = pl.ds(rows - 8, 8), pl.ds(0, 8)
    near, far = pl.ds(0, LANE), pl.ds(cols - LANE, LANE)
    return [
        body.at[:, top, :],
        body.at[:, low, :],
        body.at[:, :, far],
        body.at[:, :, near],
        body.at[:, top, far],
        body.at[:, top, near],
        body.at[:, low, far],
        body.at[:, low, near],
    ]


def exchange(pick, shapes, body, edge, ident):
    return pl.pallas_call(
        functools.partial(exchange_kernel, pick),
        out_shape=tuple(jax.ShapeDtypeStruct(shape, jnp.float32) for shape in shapes),
        in_specs=[ANY, ANY],
        out_specs=(ANY,) * len(shapes),
        scratch_shapes=[pltpu.SemaphoreType.DMA((8,)), pltpu.SemaphoreType.DMA((8,))],
        compiler_params=pltpu.CompilerParams(collective_id=ident, has_side_effects=True),
        name="exchange",
    )(body, edge)


def first_piola(stretch_x, stretch_y, fields):
    gram_xx = sum(x * x for x in stretch_x)
    gram_xy = sum(x * y for x, y in zip(stretch_x, stretch_y))
    gram_yy = sum(y * y for y in stretch_y)
    determinant = gram_xx * gram_yy - gram_xy * gram_xy
    inverse = 1.0 / determinant
    inv_xx = gram_yy * inverse
    inv_xy = -gram_xy * inverse
    inv_yy = gram_xx * inverse
    shear_mod = MU_BASE * (1.5 + jnp.tanh(fields[3]))
    bulk = LAMBDA_BULK * 0.5 * jnp.log(determinant)
    piola_x, piola_y = [], []
    for along_x, along_y in zip(stretch_x, stretch_y):
        push_x = along_x * inv_xx + along_y * inv_xy
        push_y = along_x * inv_xy + along_y * inv_yy
        piola_x.append(
            shear_mod * (along_x - push_x)
            + bulk * push_x
            + PRESTRESS * (along_x * fields[0] + along_y * fields[2])
        )
        piola_y.append(
            shear_mod * (along_y - push_y)
            + bulk * push_y
            + PRESTRESS * (along_x * fields[2] + along_y * fields[1])
        )
    return piola_x, piola_y


def sheet_kernel(n_rows, n_cols, *refs):
    (part, p_dn, p_up, p_l, p_r, p_dl, p_dr, p_ul, p_ur) = refs[:9]
    (body, s_dn, s_up, s_l, s_r, s_dl, s_dr, s_ul, s_ur) = refs[9:18]
    velocity, out, vel_out = refs[18:21]
    resid, dir_a, dir_b, total, field, mem, mass, coef = refs[21:]
    rows_dev, cols_dev = body.shape[1:]
    channels, width = part.shape[1:]
    tall = rows_dev + 16

    edge8, edge_mid = lane_ids((8, LANE)), lane_ids((rows_dev, LANE))
    for f in range(body.shape[0]):
        field[f, 0:8, 0:cols_dev] = s_dn[f]
        field[f, 8 : 8 + rows_dev, 0:cols_dev] = body[f]
        field[f, 8 + rows_dev : tall, 0:cols_dev] = s_up[f]
        field[f, 0:8, cols_dev:width] = jnp.where(edge8 < 64, s_dr[f], s_dl[f])
        field[f, 8 : 8 + rows_dev, cols_dev:width] = jnp.where(edge_mid < 64, s_r[f], s_l[f])
        field[f, 8 + rows_dev : tall, cols_dev:width] = jnp.where(edge8 < 64, s_ur[f], s_ul[f])

    shape = (tall, width)
    row = lax.broadcasted_iota(jnp.int32, shape, 0) - 8 + lax.axis_index("new") * rows_dev
    lane = lax.broadcasted_iota(jnp.int32, shape, 1)
    col = jnp.where(lane < cols_dev + 64, lane, lane - width) + lax.axis_index("old") * cols_dev
    valid = (row >= 0) & (row < n_rows - 1) & (col >= 0) & (col < n_cols - 1)

    def from_left(x):
        return pltpu.roll(x, 1, 1)

    def from_right(x):
        return pltpu.roll(x, width - 1, 1)

    def from_below(x):
        return pltpu.roll(x, 1, 0)

    def from_above(x):
        return pltpu.roll(x, tall - 1, 0)

    area_low = jnp.where(valid, field[0], 0.0)
    area_up = jnp.where(valid, field[1], 0.0)
    field[2] = field[2] * area_low
    field[3] = field[3] * area_up
    low, high = area_low / 12.0, area_up / 12.0
    both = low + high
    low_left, high_below = from_left(low), from_below(high)
    weight = both + low_left + high_below + from_below(from_left(both))
    inv = jnp.where(weight > 0.0, 1.0 / (2.0 * weight), 0.0)
    inv_right = from_right(inv)
    east, north = low + high_below, high + low_left
    coef[0] = inv * (1.0 / 3.0)
    coef[1] = inv * north
    coef[2] = inv * from_below(north)
    coef[3] = from_left(inv * east)
    coef[4] = from_left(inv * both)
    coef[5] = inv_right * east
    coef[6] = inv_right * from_below(both)
    vol_low, vol_up = field[2], field[3]
    mass[...] = (
        vol_low
        + vol_up
        + from_left(vol_low)
        + from_below(vol_up)
        + from_below(from_left(vol_low + vol_up))
    ) * (1.0 / 3.0)

    centre = 0.5 * (EIG_HIGH + EIG_LOW)
    half_width = 0.5 * (EIG_HIGH - EIG_LOW)
    ratio_eig = centre / half_width
    rho = 1.0 / ratio_eig
    edge = lane_ids((channels, LANE))

    def widen(middle, left, right):
        first = middle[:, 0:LANE] + jnp.where(edge == 0, left, 0.0)
        last = middle[:, cols_dev:width] + jnp.where(edge >= 64, left, right)
        return jnp.concatenate([first, middle[:, LANE:cols_dev], last], axis=1)

    def begin(e, rhs):
        scaled = rhs * coef[0, pl.ds(e + 4, 1), :]
        start = scaled * (1.0 / centre)
        resid[e] = scaled
        dir_a[e] = start
        total[e] = start

    def own(i):
        return widen(part[i], p_l[i], p_r[i])

    def lower(i):
        return widen(p_dn[i], p_dl[i], p_dr[i])

    def upper(i):
        return widen(p_up[i], p_ul[i], p_ur[i])

    for e in range(HALO):
        begin(e, lower(e))
    begin(HALO, own(0) + lower(HALO))

    def inner(i, _):
        begin(i + HALO, own(i))
        return 0

    lax.fori_loop(1, rows_dev, inner, 0)
    begin(rows_dev + HALO, own(rows_dev) + upper(0))
    for e in range(1, HALO):
        begin(rows_dev + HALO + e, upper(e))

    mem[...] = jnp.zeros_like(mem)
    source, target = dir_a, dir_b
    for sweep in range(ITERS):
        rho_next = 1.0 / (2.0 * ratio_eig - rho)
        keep, gain = rho_next * rho, 2.0 * rho_next / half_width
        rho = rho_next
        final = sweep == ITERS - 1

        def step(e, _, source=source, target=target, keep=keep, gain=gain, final=final):
            k = [coef[c, pl.ds(e + 4, 1), :] for c in range(1, 7)]
            through = None
            for group in range(0, channels, 8):
                at = slice(group, group + 8)
                here, over, under = source[e, at, :], source[e + 1, at, :], source[e - 1, at, :]
                to_left = k[2] * here + k[3] * over
                to_right = k[4] * here + k[5] * under
                left = resid[e, at, :] - (
                    here
                    + k[0] * over
                    + k[1] * under
                    + pltpu.roll(to_left, width - 1, 1)
                    + pltpu.roll(to_right, 1, 1)
                )
                new = keep * here + gain * left
                summed = total[e, at, :] + new
                total[e, at, :] = summed
                if final:
                    through = summed if through is None else through + summed
                else:
                    resid[e, at, :] = left
                    target[e, at, :] = new
            if final:
                through = through * (1.0 / POINTS)
                for at, value in enumerate((0, 1, 5, 7)):
                    mem[at, pl.ds(e + 4, 1), :] = through[value : value + 1, :]
            return 0

        lax.fori_loop(1 + sweep, rows_dev + 2 * HALO - 1 - sweep, step, 0)
        source, target = target, source

    for channel in range(channels):
        for block in range(0, rows_dev, 8):
            out[channel, block : block + 8, :] = total[
                HALO + block : HALO + block + 8, channel, 0:cols_dev
            ]

    anchor = [field[4 + c] for c in range(3)]
    beside = [from_right(x) for x in anchor]
    upward = [from_above(x) for x in anchor]
    across = [from_above(x) for x in beside]
    m_anchor = [mem[c] for c in range(4)]
    m_beside = [from_right(x) for x in m_anchor]
    m_upward = [from_above(x) for x in m_anchor]
    m_across = [from_above(x) for x in m_beside]
    third = 1.0 / 3.0
    m_low = [(a + b + x) * third for a, b, x in zip(m_anchor, m_beside, m_across)]
    m_up = [(a + x + u) * third for a, x, u in zip(m_anchor, m_across, m_upward)]
    low_x = [b - a for a, b in zip(anchor, beside)]
    low_y = [x - b for b, x in zip(beside, across)]
    up_x = [x - u for u, x in zip(upward, across)]
    up_y = [u - a for a, u in zip(anchor, upward)]
    low_x[0], up_x[0] = 1.0 + low_x[0], 1.0 + up_x[0]
    low_y[1], up_y[1] = 1.0 + low_y[1], 1.0 + up_y[1]
    piola_lx, piola_ly = first_piola(low_x, low_y, m_low)
    piola_ux, piola_uy = first_piola(up_x, up_y, m_up)
    vol_low, vol_up = field[2], field[3]
    node_mass = mass[8 : 8 + rows_dev, 0:cols_dev]
    for c in range(3):
        f_beside = -vol_low * (piola_lx[c] - piola_ly[c])
        f_across_low = -vol_low * piola_ly[c]
        f_across_up = -vol_up * piola_ux[c]
        f_upward = -vol_up * (piola_uy[c] - piola_ux[c])
        f_anchor = -(f_beside + f_across_low) - (f_across_up + f_upward)
        force = (
            f_anchor
            + from_left(f_beside)
            + from_below(f_upward)
            + from_below(from_left(f_across_low + f_across_up))
        )
        speed_up = force[8 : 8 + rows_dev, 0:cols_dev] / node_mass
        if c == 2:
            speed_up = speed_up + GRAVITY
        vel_out[c] = velocity[c] + TIME_STEP * speed_up


def sheet(part, part_halo, body, body_halo, velocity, n_rows, n_cols):
    channels, width = part.shape[1:]
    rows_dev, cols_dev = body.shape[1:]
    tall, long = rows_dev + 16, rows_dev + 2 * HALO
    block = pltpu.VMEM((long, channels, width), jnp.float32)

    def plane(count):
        return pltpu.VMEM((count, tall, width), jnp.float32)

    return pl.pallas_call(
        functools.partial(sheet_kernel, n_rows, n_cols),
        out_shape=(
            jax.ShapeDtypeStruct((channels, rows_dev, cols_dev), jnp.float32),
            jax.ShapeDtypeStruct(velocity.shape, jnp.float32),
        ),
        in_specs=[VMEM] * 19,
        out_specs=(VMEM, VMEM),
        scratch_shapes=[
            block,
            block,
            block,
            block,
            plane(body.shape[0]),
            plane(4),
            pltpu.VMEM((tall, width), jnp.float32),
            plane(7),
        ],
        compiler_params=pltpu.CompilerParams(vmem_limit_bytes=56 * MIB),
        name="sheet",
    )(part, *part_halo, body, *body_halo, velocity)


def local(
    old_values,
    pair_rows,
    pair_targets,
    pair_weights,
    pair_counts,
    cell_area,
    thickness,
    displacement,
    velocity,
):
    channels = old_values.shape[0]
    ranks, slots = pair_rows.shape[1:]
    rows_dev, cols_dev = cell_area.shape[1:]
    n_old, n_new = lax.axis_size("old"), lax.axis_size("new")
    width = cols_dev + LANE

    slot = jnp.arange(slots, dtype=jnp.int32)[None, :]
    owner = jnp.arange(ranks, dtype=jnp.int32)[:, None]
    cell = pair_targets[0] // cols_dev
    col = pair_targets[0] % cols_dev
    outside = ((owner % n_new == n_new - 1) & (cell % rows_dev == rows_dev - 1)) | (
        (owner // n_new == n_old - 1) & (col == cols_dev - 1)
    )
    used = (slot < pair_counts[0][:, None]) & ~outside
    slot_weight = jnp.where(used, pair_weights[0], 0.0)
    slot_row = jnp.where(used, FRONT + cell * width + col, FRONT + cols_dev + slot)

    picked = gather(pair_counts[0], pair_rows[0], slot_weight, old_values)
    ids = lax.all_to_all(slot_row, ("old", "new"), split_axis=0, concat_axis=0, tiled=True)
    arrived = lax.all_to_all(picked, ("old", "new"), split_axis=0, concat_axis=0, tiled=True)

    batches = ids.reshape(ranks, slots // (4 * BATCH), BATCH, 4)
    clash = jnp.zeros((ranks,), jnp.bool_)
    for a in range(BATCH):
        for b in range(a):
            clash = clash | jnp.any(batches[:, :, a] == batches[:, :, b], axis=(1, 2))

    body = jnp.concatenate([cell_area, thickness, displacement], axis=0)
    fields = body.shape[0]
    body_halo = exchange(
        pick_fields,
        [(fields, 8, cols_dev)] * 2 + [(fields, rows_dev, LANE)] * 2 + [(fields, 8, LANE)] * 4,
        body,
        body,
        1,
    )
    part, edge = scatter(ids, clash.astype(jnp.int32), arrived, rows_dev, cols_dev)
    part_halo = exchange(
        pick_partial,
        [(HALO + 1, channels, width), (HALO, channels, width)]
        + [(rows_dev + 1, channels, LANE)] * 2
        + [(HALO + 1, channels, LANE)] * 2
        + [(HALO, channels, LANE)] * 2,
        part,
        edge,
        2,
    )
    return sheet(
        part, part_halo, body, body_halo, velocity, n_new * rows_dev, n_old * cols_dev
    )


def solution(mesh):
    return jax.shard_map(
        local,
        mesh=mesh,
        in_specs=(
            P(None, ("old", "new")),
            P(("old", "new"), None, None),
            P(("old", "new"), None, None),
            P(("old", "new"), None, None),
            P(("old", "new"), None),
            P(None, "new", "old"),
            P(None, "new", "old"),
            P(None, "new", "old"),
            P(None, "new", "old"),
        ),
        out_specs=(P(None, "new", "old"), P(None, "new", "old")),
        check_vma=False,
    )
```

time: 552 us -> 210 us (0.38); the launches traced: 541 us -> 209 us
  other arithmetic: 229 us -> 4.17 us
  Pallas kernels: 0 us -> 176 us
  local copies, waits for them, and re-layouts: 143 us -> 7.06 us
  waiting for transfers between devices: 83.6 us -> 0.01 us
  starting transfers between devices: 83.5 us -> 21.4 us
    pallas_call x0 -> x5, Pallas kernels: none -> 176 us  [the longest x1 62 us: scatter(): pl.pallas_call(functools.partial(scatter_kernel, rows_dev, cols_dev), out...]
    scatter-add x1 -> x0, other arithmetic: 112 us -> none  [local(): empty.at[:, arrived_ids.reshape(-1)].add(arrived.reshape(channels, -1))]
    add x10 -> x1, other arithmetic: 78.5 us -> 0.01 us  [local(): FRONT + cols_dev + slot]
    gather x2 -> x0, local copies, waits for them, and re-layouts: 61.8 us -> none  [local(): picked = old_values[:, rows_here] * slot_weight[None]]
    ppermute x18 -> x0, starting transfers between devices: 61.8 us -> none  [the longest x8 31.5 us: padded_2(): lax.ppermute(lax.slice_in_dim(block, block.shape[dim] - width, None, axis...]
    ppermute x18 -> x0, waiting for transfers between devices: 54.3 us -> none  [the longest x8 35.3 us: padded_2(): lax.ppermute(lax.slice_in_dim(block, 0, width, axis=dim), axis, backward)]
    reshape x3 -> x0, local copies, waits for them, and re-layouts: 31 us -> none  [the longest x1 21.7 us: local(): element_sums = element_sums.reshape(channels, 2, rows_dev, cols_dev)]
    all_to_all x2, waiting for transfers between devices: 29.3 us -> 0.01 us  [the longest x1 0.01 us: local(): lax.all_to_all(slot_row, ('old', 'new'), split_axis=0, concat_axis=0, til...]
  transfers between devices with their start and end apart: 20 -> 2, of which waited for: 17 -> 0; matrix products, arithmetic and copies ran while one was open for 13% -> 2% of each run, Pallas kernels for 0% -> 28%
where the time goes in v1:
time: 210 us; the launch traced here: 209 us
  Pallas kernels  176 us (84%)
  starting transfers between devices  21.4 us (10%)
  local copies, waits for them, and re-layouts  7.06 us (3%)
  other arithmetic  4.17 us (2%)
    pallas_call x1, Pallas kernels, scatter(): pl.pallas_call(functools.partial(scatter_kernel, rows_dev, cols_dev), out...  62 us
    pallas_call x2, Pallas kernels, exchange(): pl.pallas_call(functools.partial(exchange_kernel, pick), out_shape=tuple(...  59.2 us
    pallas_call x1, Pallas kernels, sheet(): pl.pallas_call(functools.partial(sheet_kernel, n_rows, n_cols), out_shape...  29 us
    pallas_call x1, Pallas kernels, gather(): pl.pallas_call(gather_kernel, out_shape=jax.ShapeDtypeStruct((ranks, per...  25.9 us
    all_to_all x1, starting transfers between devices, local(): lax.all_to_all(slot_row, ('old', 'new'), split_axis=0, concat_axis=0, til...  11.5 us
    all_to_all x1, starting transfers between devices, local(): lax.all_to_all(picked, ('old', 'new'), split_axis=0, concat_axis=0, tiled...  9.85 us
    unnamed x16, local copies, waits for them, and re-layouts  6.95 us
  transfers between devices with their start and end apart: 2, of which 0 were waited for; matrix products, arithmetic and copies ran while one was open for 2% of the time, Pallas kernels for 28%

profile of v1, /device:TPU:1, one launch (start us, length us, event | category | flops | bytes accessed | tf_op | source)
XLA Modules:
  0.0 209.5 jit_solution(16397932329391936567)
XLA Ops:
  0.7 2.5 %and_select_fusion = s32[128,1,128]{2,1,0:T(1,128)} fusion(pred[128]{0:T(512)(128)(4,1)S(1)} %get-tuple-element.45, pred[128]{0:T(512)(128)(4,1)S(1)} %get-tuple-element.44, s32[128,1,128]{2,1,0:T(1,128)} %bitcast.44, s32[128]{0:T(128)} %bitcast.40, s32[128]{0:T(128)S(1)} %iota_add_fusion), kind=kLoop, calls=%fused_computation.2 | loop fusion | flops 688128 | bytes 132352 | tf_op jit(solution)/shard_map/jit(_where)/select_n | solution.py:538
  3.2 11.5 %all-to-all-start = ((s32[128,1,128]{2,1,0:T(1,128)}), s32[128,1,128]{2,1,0:T(1,128)S(1)}, u32[]{:S(2)}, u32[]{:S(2)}) async-start(s32[128,1,128]{2,1,0:T(1,128)} %and_select_fusion), calls=%async_computation | async-start | bytes 131072 | tf_op jit(solution)/shard_map/all_to_all | solution.py:541
  14.7 1.0 bitcast_select_fusion.weights
  15.7 0.0 copy-start
  15.7 1.2 copy-done
  16.9 0.0 copy-start.1
  16.9 0.8 copy-done.1
  17.8 0.0 copy-start.2
  17.8 0.7 copy-done.2
  18.4 0.0 copy-start.6
  18.4 25.9 %gather.1 = f32[128,32,128]{2,1,0:T(8,128)} custom-call(s32[128]{0:T(128)S(1)} %bitcast.42, s32[16384]{0:T(1024)S(1)} %bitcast.39, f32[16384]{0:T(1024)S(1)} %bitcast_select_fusion.weights, f32[32,8192]{1,0:T(8,128)S(1)} %copy-done), custom_call_target="tpu_custom_call" | custom-call | tf_op jit(solution)/shard_map/gather/pallas_call | solution.py:81
  44.3 0.0 all-to-all-done
  44.3 0.0 copy-start.5
  44.3 9.9 %all-to-all-start.1 = ((f32[128,32,128]{2,1,0:T(8,128)}), f32[128,32,128]{2,1,0:T(8,128)S(1)}, u32[]{:S(2)}, u32[]{:S(2)}) async-start(f32[128,32,128]{2,1,0:T(8,128)} %gather.1), calls=%async_computation.1 | async-start | bytes 4194304 | tf_op jit(solution)/shard_map/all_to_all | solution.py:542
  54.1 1.0 constant_dynamic-update-slice_fusion.2
  55.1 1.0 constant_dynamic-update-slice_fusion.1
  56.1 0.0 copy-done.6
  56.1 0.0 copy-start.3
  56.1 1.0 copy-done.3
  57.1 32.2 %exchange.3 = (f32[7,8,1024]{2,1,0:T(8,128)}, f32[7,8,1024]{2,1,0:T(8,128)}, f32[7,32,128]{2,1,0:T(8,128)}, f32[7,32,128]{2,1,0:T(8,128)}, f32[7,8,128]{2,1,0:T(...) custom-call(f32[7,32,1024]{2,1,0:T(8,128)} %copy-done.3, f32[7,32,1024]{2,1,0:T(8,128)} %copy-done.3), custom_call_target="tpu_custom_call" | custom-call | tf_op jit(solution)/shard_map/exchange/pallas_call | solution.py:253
  89.3 0.1 copy.13
  89.4 0.6 or_convert_fusion.clash
  90.0 0.0 all-to-all-done.1.data
  90.0 0.0 copy-start.4
  90.0 0.0 copy-done.5
  90.0 1.3 copy-done.4
  91.3 62.0 %scatter.1 = (f32[33,32,1152]{2,1,0:T(8,128)}, f32[33,32,128]{2,1,0:T(8,128)}) custom-call(s32[16384]{0:T(1024)} %bitcast.43, s32[128]{0:T(128)} %or_convert_fusion.clash, f32[128,32,128]{2,1,0:T(8,128)} %copy-done.4), custom_call_target="tpu_custom_call" | custom-call | tf_op jit(solution)/shard_map/scatter/pallas_call | solution.py:170
  153.4 27.1 %exchange.2 = (f32[5,32,1152]{2,1,0:T(8,128)}, f32[4,32,1152]{2,1,0:T(8,128)}, f32[33,32,128]{2,1,0:T(8,128)}, f32[33,32,128]{2,1,0:T(8,128)}, f32[5,32,128]{2,1...) custom-call(f32[33,32,1152]{2,1,0:T(8,128)} %get-tuple-element.20.body.refs_0_, ...), custom_call_target="tpu_custom_call" | custom-call | tf_op jit(solution)/shard_map/exchange/pallas_call | solution.py:253
  180.5 29.0 %sheet.1 = (f32[32,32,1024]{2,1,0:T(8,128)}, f32[3,32,1024]{2,1,0:T(8,128)}) custom-call(f32[33,32,1152]{2,1,0:T(8,128)} %get-tuple-element.20.body.refs_0_, f32[5,32,1152]{2,1,0:T(8,128)} %get-tuple-element.22.refs_1_, f32[4,32,1152]{2,1,0:T(8,128)} %get-tuple-element.23.refs_2_, f32[33,32,128]{2,1,0:T(8,128)} %get-tuple-element.24.refs_3_, ...), custom_call_target="tpu_custom_call" | custom-call | tf_op jit(solution)/shard_map/sheet/pallas_call | solution.py:489
  (4 shorter events, 0.1 us)
Async XLA Ops:
  3.2 41.1 %all-to-all-start = ((s32[128,1,128]{2,1,0:T(1,128)}), s32[128,1,128]{2,1,0:T(1,128)S(1)}, u32[]{:S(2)}, u32[]{:S(2)}) async-start(s32[128,1,128]{2,1,0:T(1,128)} %and_select_fusion), calls=%async_computation | async-start | bytes 131072 | tf_op jit(solution)/shard_map/all_to_all | solution.py:541
  15.7 1.2 copy-start
  16.9 0.8 copy-start.1
  17.8 0.7 copy-start.2
  18.4 37.7 %copy-start.6 = (f32[3,32,1024]{2,1,0:T(8,128)S(1)}, f32[3,32,1024]{2,1,0:T(8,128)}, u32[]{:S(2)}) copy-start(f32[3,32,1024]{2,1,0:T(8,128)} %param.16) | copy-start | bytes 1179652
  44.3 45.7 %copy-start.5 = (s32[128,1,128]{2,1,0:T(1,128)}, s32[128,1,128]{2,1,0:T(1,128)S(1)}, u32[]{:S(2)}) copy-start(s32[128,1,128]{2,1,0:T(1,128)S(1)} %all-to-all-done) | copy-start | bytes 196612
  44.3 45.7 %all-to-all-start.1 = ((f32[128,32,128]{2,1,0:T(8,128)}), f32[128,32,128]{2,1,0:T(8,128)S(1)}, u32[]{:S(2)}, u32[]{:S(2)}) async-start(f32[128,32,128]{2,1,0:T(8,128)} %gather.1), calls=%async_computation.1 | async-start | bytes 4194304 | tf_op jit(solution)/shard_map/all_to_all | solution.py:542
  56.1 1.0 copy-start.3
  90.0 1.3 copy-start.4

commit v2 on v1

--- a/solution.py
+++ b/solution.py
@@ -22,6 +22,7 @@
 FRONT = 8
 BATCH = 4
 HALO = 4
+STRIDE = 37
 MESH = pl.DeviceIdType.MESH
 MIB = 1024 * 1024
 
@@ -34,94 +35,246 @@
     return lax.broadcasted_iota(jnp.int32, shape, len(shape) - 1)
 
 
-def gather_kernel(counts, rows, weights, values, out, table):
-    ranks = out.shape[0]
-    per = out.shape[1] * 4
-    channels, total = values.shape
+def send_kernel(
+    rows_dev,
+    cols_dev,
+    counts,
+    rows_in,
+    targets,
+    weights_in,
+    values,
+    body,
+    arrived,
+    arrived_ids,
+    s_dn,
+    s_up,
+    s_l,
+    s_r,
+    s_dl,
+    s_dr,
+    s_ul,
+    s_ur,
+    table,
+    picked,
+    ids,
+    notes,
+    weights_flat,
+    rows,
+    weights,
+    local_sem,
+    pair_sem,
+    near_send,
+    near_recv,
+):
+    n_old, n_new = lax.axis_size("old"), lax.axis_size("new")
+    old, new = lax.axis_index("old"), lax.axis_index("new")
+    ranks, payload, _ = picked.shape
+    slots = payload * 4
+    width = cols_dev + LANE
+    total = values.shape[1]
+    me = old * n_new + new
+
+    load_rows = pltpu.make_async_copy(rows_in, rows, local_sem.at[0])
+    load_rows.start()
+
+    barrier = pltpu.get_barrier_semaphore()
+
+    def greet(step, _):
+        other = lax.rem(me + step, ranks)
+        pl.semaphore_signal(
+            barrier, inc=1, device_id=(other // n_new, other % n_new), device_id_type=MESH
+        )
+        return 0
+
+    lax.fori_loop(1, ranks, greet, 0)
+
+    slot = lane_ids((ranks, slots))
+    owner = lax.broadcasted_iota(jnp.int32, (ranks, slots), 0)
+    count = jnp.broadcast_to(counts[...].astype(jnp.float32), (ranks, ranks)).T.astype(jnp.int32)
+    target = targets[0]
+    cell, col = target // cols_dev, target % cols_dev
+    outside = ((owner % n_new == n_new - 1) & (cell % rows_dev == rows_dev - 1)) | (
+        (owner // n_new == n_old - 1) & (col == cols_dev - 1)
+    )
+    used = (slot < count) & jnp.logical_not(outside)
+    weights_flat[...] = jnp.where(used, weights_in[0], 0.0)
+    load_weights = pltpu.make_async_copy(weights_flat, weights, local_sem.at[1])
+    load_weights.start()
+    where_to = jnp.where(used, FRONT + cell * width + col, FRONT + cols_dev + slot)
+    clash = jnp.zeros((ranks, slots), jnp.int32)
+    for gap in range(1, BATCH):
+        same = (where_to == pltpu.roll(where_to, 4 * gap, 1)) & (slot % (4 * BATCH) >= 4 * gap)
+        clash = clash | same.astype(jnp.int32)
+    notes[:, 0:slots] = where_to
+    notes[:, slots : slots + LANE] = jnp.broadcast_to(
+        jnp.max(clash, axis=1, keepdims=True), (ranks, LANE)
+    )
+
+    unroll = 8
 
     def flip(step, _):
-        start = pl.multiple_of(step * LANE, LANE)
-        part = values[:, pl.ds(start, LANE)]
-        table[pl.ds(start, LANE), :] = jnp.concatenate([part] * 4, axis=0).T
+        for at in range(unroll):
+            start = pl.multiple_of((step * unroll + at) * LANE, LANE)
+            part = values[:, pl.ds(start, LANE)]
+            table[pl.ds(start, LANE), :] = jnp.concatenate([part] * 4, axis=0).T
         return 0
 
-    lax.fori_loop(0, total // LANE, flip, 0)
+    lax.fori_loop(0, total // (LANE * unroll), flip, 0)
+    load_rows.wait()
+    load_weights.wait()
+    pl.semaphore_wait(barrier, ranks - 1)
+
+    left, right = lax.rem(old + n_old - 1, n_old), lax.rem(old + 1, n_old)
+    below, above = lax.rem(new + n_new - 1, n_new), lax.rem(new + 1, n_new)
+    top, low = pl.ds(rows_dev - 8, 8), pl.ds(0, 8)
+    near, far = pl.ds(0, LANE), pl.ds(cols_dev - LANE, LANE)
+    halo = [
+        (body.at[:, top, :], s_dn, (old, above)),
+        (body.at[:, low, :], s_up, (old, below)),
+        (body.at[:, :, far], s_l, (right, new)),
+        (body.at[:, :, near], s_r, (left, new)),
+        (body.at[:, top, far], s_dl, (right, above)),
+        (body.at[:, top, near], s_dr, (left, above)),
+        (body.at[:, low, far], s_ul, (right, below)),
+        (body.at[:, low, near], s_ur, (left, below)),
+    ]
+    halo = [
+        pltpu.make_async_remote_copy(
+            src_ref=source,
+            dst_ref=target,
+            send_sem=near_send.at[at],
+            recv_sem=near_recv.at[at],
+            device_id=device,
+            device_id_type=MESH,
+        )
+        for at, (source, target, device) in enumerate(halo)
+    ]
+    for copy in halo:
+        copy.start()
+
     lane = lane_ids((1, LANE))
     first, second, third = lane < 32, lane < 64, lane < 96
 
-    def one_owner(owner, _):
-        blocks = (counts[owner] + 31) // 32
-        for block in range(per // 32):
-
-            @pl.when(block < blocks)
-            def _():
-                for row in range(8):
-                    base = owner * per + block * 32 + row * 4
-                    part = [
-                        table[pl.ds(rows[base + g], 1), :] * weights[base + g] for g in range(4)
-                    ]
-                    merged = jnp.where(
-                        first,
-                        part[0],
-                        jnp.where(second, part[1], jnp.where(third, part[2], part[3])),
-                    )
-                    out[owner, pl.ds(block * 8 + row, 1), :] = merged
-
-            @pl.when(block >= blocks)
-            def _():
-                out[owner, pl.ds(block * 8, 8), :] = jnp.zeros((8, LANE), jnp.float32)
-
+    def fill(owner):
+        for row in range(payload):
+            part = [
+                table[pl.ds(rows[0, owner, row * 4 + g], 1), :] * weights[owner, row * 4 + g]
+                for g in range(4)
+            ]
+            merged = jnp.where(
+                first, part[0], jnp.where(second, part[1], jnp.where(third, part[2], part[3]))
+            )
+            picked[owner, pl.ds(row, 1), :] = merged
+        ids[owner] = notes[pl.ds(owner, 1), :]
+
+    def one_owner(step, _):
+        shift = lax.rem(step * STRIDE, ranks)
+        to_old = lax.rem(old + shift // n_new, n_old)
+        to_new = lax.rem(new + shift % n_new, n_new)
+        owner = to_old * n_new + to_new
+        fill(owner)
+        for at, (source, target) in enumerate(((picked, arrived), (ids, arrived_ids))):
+            pltpu.make_async_remote_copy(
+                src_ref=source.at[owner],
+                dst_ref=target.at[me],
+                send_sem=pair_sem.at[2 * at],
+                recv_sem=pair_sem.at[2 * at + 1],
+                device_id=(to_old, to_new),
+                device_id_type=MESH,
+            ).start()
         return 0
 
-    lax.fori_loop(0, ranks, one_owner, 0)
-
-
-def gather(counts, rows, weights, values):
-    ranks, per = rows.shape
-    return pl.pallas_call(
-        gather_kernel,
-        out_shape=jax.ShapeDtypeStruct((ranks, per // 4, LANE), jnp.float32),
-        in_specs=[SMEM, SMEM, SMEM, VMEM],
-        out_specs=VMEM,
-        scratch_shapes=[pltpu.VMEM((values.shape[1], LANE), jnp.float32)],
-        compiler_params=pltpu.CompilerParams(vmem_limit_bytes=24 * MIB),
-        name="gather",
-    )(counts, rows.reshape(-1), weights.reshape(-1), values)
-
-
-def scatter_kernel(rows_dev, cols_dev, ids, clash, data, part, right_tile, acc):
+    lax.fori_loop(1, ranks, one_owner, 0)
+    fill(me)
+    for at, (source, target) in enumerate(((picked, arrived), (ids, arrived_ids))):
+        pltpu.make_async_copy(source.at[me], target.at[me], pair_sem.at[2 * at + 1]).start()
+    for copy in halo:
+        copy.wait()
+    for at, (source, target) in enumerate(((picked, arrived), (ids, arrived_ids))):
+        rest = pl.ds(0, ranks - 1)
+        pltpu.make_async_copy(source.at[rest], source.at[rest], pair_sem.at[2 * at]).wait()
+        pltpu.make_async_copy(source, target, pair_sem.at[2 * at + 1]).wait()
+
+
+def send(counts, rows, targets, weights, values, body):
+    ranks, slots = rows.shape[1:]
+    payload = slots // 4
+    fields, rows_dev, cols_dev = body.shape
+    shapes = (
+        [(ranks, payload, LANE)]
+        + [(fields, 8, cols_dev)] * 2
+        + [(fields, rows_dev, LANE)] * 2
+        + [(fields, 8, LANE)] * 4
+    )
+    shapes = [jax.ShapeDtypeStruct(shape, jnp.float32) for shape in shapes]
+    shapes.insert(1, jax.ShapeDtypeStruct((ranks, 1, slots + LANE), jnp.int32))
+    result = pl.pallas_call(
+        functools.partial(send_kernel, rows_dev, cols_dev),
+        out_shape=tuple(shapes),
+        in_specs=[VMEM, ANY, VMEM, VMEM, VMEM, ANY],
+        out_specs=(ANY,) * len(shapes),
+        scratch_shapes=[
+            pltpu.VMEM((values.shape[1], LANE), jnp.float32),
+            pltpu.VMEM((ranks, payload, LANE), jnp.float32),
+            pltpu.VMEM((ranks, 1, slots + LANE), jnp.int32),
+            pltpu.VMEM((ranks, slots + LANE), jnp.int32),
+            pltpu.VMEM((ranks, slots), jnp.float32),
+            pltpu.SMEM((1, ranks, slots), jnp.int32),
+            pltpu.SMEM((ranks, slots), jnp.float32),
+            pltpu.SemaphoreType.DMA((2,)),
+            pltpu.SemaphoreType.DMA((4,)),
+            pltpu.SemaphoreType.DMA((8,)),
+            pltpu.SemaphoreType.DMA((8,)),
+        ],
+        compiler_params=pltpu.CompilerParams(
+            vmem_limit_bytes=24 * MIB, collective_id=1, has_side_effects=True
+        ),
+        name="send",
+    )(counts, rows, targets, weights, values, body)
+    return result[0], result[1], result[2:]
+
+
+def scatter_kernel(rows_dev, cols_dev, ids_in, data_in, part, right_tile, acc, carry, data, ids, sem):
     width = cols_dev + LANE
     ranks, payload, _ = data.shape
-    per = payload * 4
     size = acc.shape[0]
     chunk = width // 8
+    load_ids = pltpu.make_async_copy(ids_in, ids, sem.at[0])
+    load_data = pltpu.make_async_copy(data_in, data, sem.at[1])
+    load_ids.start()
+    load_data.start()
     zeros = jnp.zeros((chunk, LANE), jnp.float32)
     acc[pl.ds(0, FRONT), :] = jnp.zeros((FRONT, LANE), jnp.float32)
+    carry[...] = jnp.zeros_like(carry)
 
     def clear(step, _):
         acc[pl.ds(pl.multiple_of(FRONT + step * chunk, 8), chunk), :] = zeros
         return 0
 
     lax.fori_loop(0, (size - FRONT) // chunk, clear, 0)
+    load_ids.wait()
+    load_data.wait()
 
     lane = lane_ids((1, LANE))
     masks = [(lane >= 32 * g) & (lane < 32 * g + 32) for g in range(4)]
 
     def add_rows(source, first, count):
         slots = [(r, g) for r in range(count) for g in range(4)]
-        where_to = [ids[source * per + (first + r) * 4 + g] for r, g in slots]
+        where_to = [ids[source, 0, (first + r) * 4 + g] for r, g in slots]
         new = [data[source, pl.ds(first + r, 1), :] for r in range(count)]
         old = [acc[pl.ds(row, 1), :] for row in where_to]
         for (r, g), row, have in zip(slots, where_to, old):
             pltpu.store(acc.at[pl.ds(row, 1), :], have + new[r], mask=masks[g])
 
     def one_source(source, _):
-        @pl.when(clash[source] == 0)
+        clash = ids[source, 0, payload * 4]
+
+        @pl.when(clash == 0)
         def _():
             for first in range(0, payload, BATCH):
                 add_rows(source, first, BATCH)
 
-        @pl.when(clash[source] != 0)
+        @pl.when(clash != 0)
         def _():
             def slow(row, _):
                 add_rows(source, row, 1)
@@ -135,36 +288,40 @@
 
     def fold(total):
         flipped = total.T
-        return flipped[0:32] + flipped[32:64] + flipped[64:96] + flipped[96:128]
+        return (flipped[0:32] + flipped[32:64]) + (flipped[64:96] + flipped[96:128])
 
     upper_base = rows_dev * width
-    for tile in range(width // LANE):
-
-        def one_row(i, carry, tile=tile):
-            base = i * width + tile * LANE + FRONT
+    edge = lane_ids((part.shape[1], LANE))
+
+    def pack(i, own, ghost):
+        right_tile[i] = jnp.where(edge >= 64, own, jnp.where(edge == 0, ghost, 0.0))
+
+    tiles = width // LANE
+
+    def one_row(i, _):
+        done = []
+        for tile in range(tiles):
+            span = slice(tile * LANE, (tile + 1) * LANE)
+            base = pl.multiple_of(i * width + tile * LANE + FRONT, 8)
             lower = acc[pl.ds(base, LANE), :]
-            upper = acc[pl.ds(base + upper_base, LANE), :]
-            lower_left = acc[pl.ds(base - 1, LANE), :]
-            upper_left = acc[pl.ds(base + upper_base - 1, LANE), :]
-            shared = upper + lower_left
-            part[i, :, tile * LANE : (tile + 1) * LANE] = fold(lower + shared + carry)
-            return shared + upper_left
-
-        last = lax.fori_loop(0, rows_dev, one_row, jnp.zeros((LANE, LANE), jnp.float32))
-        part[rows_dev, :, tile * LANE : (tile + 1) * LANE] = fold(last)
-
-    edge = lane_ids((part.shape[1], LANE))
-
-    def pack(i, _):
-        own = part[i, :, cols_dev - LANE : cols_dev]
-        ghost = part[i, :, cols_dev:width]
-        right_tile[i] = jnp.where(edge >= 64, own, jnp.where(edge == 0, ghost, 0.0))
+            upper = acc[pl.ds(pl.multiple_of(base + upper_base, 8), LANE), :]
+            shared = upper + acc[pl.ds(base - 1, LANE), :]
+            summed = lower + shared + carry[span, :]
+            carry[span, :] = shared + acc[pl.ds(base + upper_base - 1, LANE), :]
+            folded = fold(summed)
+            part[i, :, span] = folded
+            done.append(folded)
+        pack(i, done[-2], done[-1])
         return 0
 
-    lax.fori_loop(0, rows_dev + 1, pack, 0)
-
-
-def scatter(ids, clash, data, rows_dev, cols_dev):
+    lax.fori_loop(0, rows_dev, one_row, 0)
+    done = [fold(carry[tile * LANE : (tile + 1) * LANE, :]) for tile in range(tiles)]
+    for tile in range(tiles):
+        part[rows_dev, :, tile * LANE : (tile + 1) * LANE] = done[tile]
+    pack(rows_dev, done[-2], done[-1])
+
+
+def scatter(ids, data, rows_dev, cols_dev):
     channels = LANE // 4
     width = cols_dev + LANE
     return pl.pallas_call(
@@ -173,12 +330,18 @@
             jax.ShapeDtypeStruct((rows_dev + 1, channels, width), jnp.float32),
             jax.ShapeDtypeStruct((rows_dev + 1, channels, LANE), jnp.float32),
         ),
-        in_specs=[SMEM, SMEM, VMEM],
+        in_specs=[ANY, ANY],
         out_specs=(VMEM, VMEM),
-        scratch_shapes=[pltpu.VMEM((FRONT + 2 * rows_dev * width, LANE), jnp.float32)],
+        scratch_shapes=[
+            pltpu.VMEM((FRONT + 2 * rows_dev * width, LANE), jnp.float32),
+            pltpu.VMEM((width, LANE), jnp.float32),
+            pltpu.VMEM(data.shape, jnp.float32),
+            pltpu.SMEM(ids.shape, jnp.int32),
+            pltpu.SemaphoreType.DMA((2,)),
+        ],
         compiler_params=pltpu.CompilerParams(vmem_limit_bytes=56 * MIB),
         name="scatter",
-    )(ids.reshape(-1), clash, data)
+    )(ids, data)
 
 
 def exchange_kernel(pick, body, edge, *refs):
@@ -230,22 +393,6 @@
         body.at[top, :, near],
         edge.at[low],
         body.at[low, :, near],
-    ]
-
-
-def pick_fields(body, edge):
-    rows, cols = body.shape[1:]
-    top, low = pl.ds(rows - 8, 8), pl.ds(0, 8)
-    near, far = pl.ds(0, LANE), pl.ds(cols - LANE, LANE)
-    return [
-        body.at[:, top, :],
-        body.at[:, low, :],
-        body.at[:, :, far],
-        body.at[:, :, near],
-        body.at[:, top, far],
-        body.at[:, top, near],
-        body.at[:, low, far],
-        body.at[:, low, near],
     ]
 
 
@@ -521,42 +668,14 @@
     velocity,
 ):
     channels = old_values.shape[0]
-    ranks, slots = pair_rows.shape[1:]
     rows_dev, cols_dev = cell_area.shape[1:]
     n_old, n_new = lax.axis_size("old"), lax.axis_size("new")
     width = cols_dev + LANE
-
-    slot = jnp.arange(slots, dtype=jnp.int32)[None, :]
-    owner = jnp.arange(ranks, dtype=jnp.int32)[:, None]
-    cell = pair_targets[0] // cols_dev
-    col = pair_targets[0] % cols_dev
-    outside = ((owner % n_new == n_new - 1) & (cell % rows_dev == rows_dev - 1)) | (
-        (owner // n_new == n_old - 1) & (col == cols_dev - 1)
+    body = jnp.concatenate([cell_area, thickness, displacement], axis=0)
+    arrived, ids, body_halo = send(
+        pair_counts, pair_rows, pair_targets, pair_weights, old_values, body
     )
-    used = (slot < pair_counts[0][:, None]) & ~outside
-    slot_weight = jnp.where(used, pair_weights[0], 0.0)
-    slot_row = jnp.where(used, FRONT + cell * width + col, FRONT + cols_dev + slot)
-
-    picked = gather(pair_counts[0], pair_rows[0], slot_weight, old_values)
-    ids = lax.all_to_all(slot_row, ("old", "new"), split_axis=0, concat_axis=0, tiled=True)
-    arrived = lax.all_to_all(picked, ("old", "new"), split_axis=0, concat_axis=0, tiled=True)
-
-    batches = ids.reshape(ranks, slots // (4 * BATCH), BATCH, 4)
-    clash = jnp.zeros((ranks,), jnp.bool_)
-    for a in range(BATCH):
-        for b in range(a):
-            clash = clash | jnp.any(batches[:, :, a] == batches[:, :, b], axis=(1, 2))
-
-    body = jnp.concatenate([cell_area, thickness, displacement], axis=0)
-    fields = body.shape[0]
-    body_halo = exchange(
-        pick_fields,
-        [(fields, 8, cols_dev)] * 2 + [(fields, rows_dev, LANE)] * 2 + [(fields, 8, LANE)] * 4,
-        body,
-        body,
-        1,
-    )
-    part, edge = scatter(ids, clash.astype(jnp.int32), arrived, rows_dev, cols_dev)
+    part, edge = scatter(ids, arrived, rows_dev, cols_dev)
     part_halo = exchange(
         pick_partial,
         [(HALO + 1, channels, width), (HALO, channels, width)]

time: 210 us -> 155 us (0.74)
  Pallas kernels: 176 us -> 139 us
  starting transfers between devices: 21.4 us -> 0 us
  local copies, waits for them, and re-layouts: 7.06 us -> 14.4 us
  other arithmetic: 4.17 us -> 0 us
    pallas_call x2 -> x1, Pallas kernels: 59.2 us -> 26.4 us  [exchange(): pl.pallas_call(functools.partial(exchange_kernel, pick), out_shape=tuple(...]
    pallas_call x1, Pallas kernels: 62 us -> 37.6 us  [scatter(): pl.pallas_call(functools.partial(scatter_kernel, rows_dev, cols_dev), out...]
    all_to_all x2 -> x0, starting transfers between devices: 21.4 us -> none  [the longest x1 11.5 us: local(): lax.all_to_all(slot_row, ('old', 'new'), split_axis=0, concat_axis=0, til...]
    pallas_call x1, Pallas kernels: 25.9 us -> 46.2 us  [send(): pl.pallas_call(functools.partial(send_kernel, rows_dev, cols_dev), out_sh...]
    unnamed x16 -> x34, local copies, waits for them, and re-layouts: 6.95 us -> 13.4 us
    select_n x2 -> x0, other arithmetic: 3.54 us -> none  [the longest x1 2.54 us: local(): jnp.where(used, FRONT + cell * width + col, FRONT + cols_dev + slot)]
  transfers between devices with their start and end apart: 2 -> 0, of which waited for: 0 -> 0; matrix products, arithmetic and copies ran while one was open for 2% -> 0% of each run, Pallas kernels for 28% -> 0%
where the time goes in v2:
time: 155 us; the launch traced here: 154 us
  Pallas kernels  139 us (90%)
  local copies, waits for them, and re-layouts  14.4 us (9%)
    pallas_call x1, Pallas kernels, send(): pl.pallas_call(functools.partial(send_kernel, rows_dev, cols_dev), out_sh...  46.2 us
    pallas_call x1, Pallas kernels, scatter(): pl.pallas_call(functools.partial(scatter_kernel, rows_dev, cols_dev), out...  37.6 us
    pallas_call x1, Pallas kernels, sheet(): pl.pallas_call(functools.partial(sheet_kernel, n_rows, n_cols), out_shape...  29 us
    pallas_call x1, Pallas kernels, exchange(): pl.pallas_call(functools.partial(exchange_kernel, pick), out_shape=tuple(...  26.4 us
    unnamed x34, local copies, waits for them, and re-layouts  13.4 us

profile of v2, /device:TPU:1, one launch (start us, length us, event | category | flops | bytes accessed | tf_op | source)
XLA Modules:
  0.0 154.4 jit_solution(5179432228188524839)
XLA Ops:
  0.6 1.0 constant_dynamic-update-slice_fusion.2
  1.6 1.0 constant_dynamic-update-slice_fusion.1
  2.6 1.0 constant_dynamic-update-slice_fusion.body.refs_9_
  3.6 0.0 copy-start.2
  3.6 1.2 copy-done.2
  4.8 0.0 copy-start.8
  4.8 0.8 copy-done.8
  5.7 0.0 copy-start.9
  5.7 0.8 copy-done.9
  6.5 0.0 copy-start.10
  6.5 0.8 copy-done.10
  7.4 0.0 copy-start.15
  7.4 0.7 copy-done.15
  8.0 0.0 copy-start
  8.0 46.2 %send.1 = (f32[128,32,128]{2,1,0:T(8,128)S(1)}, s32[128,1,256]{2,1,0:T(1,128)S(1)}, f32[7,8,1024]{2,1,0:T(8,128)S(1)}, f32[7,8,1024]{2,1,0:T(8,128)S(1)}, f32[7,...) custom-call(s32[1,128]{1,0:T(1,128)S(1)} %copy-done.15, ...), custom_call_target="tpu_custom_call" | custom-call | tf_op jit(solution)/shard_map/send/pallas_call | solution.py:211
  54.2 0.0 copy-start.1
  54.2 1.3 copy-done.1
  55.5 0.0 copy-start.3
  55.5 0.7 copy-done.3
  56.2 0.0 copy-start.4
  56.2 0.7 copy-done.4
  56.9 0.0 copy-start.5
  56.9 0.7 copy-done.5
  57.6 0.0 copy-start.6
  57.6 0.6 copy-done.6
  58.2 0.0 copy-start.7
  58.2 0.6 copy-done.7
  58.9 0.0 copy-start.11
  58.9 0.6 copy-done.11
  59.5 0.0 copy-start.12
  59.5 0.6 copy-done.12
  60.1 0.0 copy-start.13
  60.1 0.6 copy-done.13
  60.7 0.0 copy-start.14
  60.7 0.6 copy-done.14
  61.3 37.6 %scatter.1 = (f32[33,32,1152]{2,1,0:T(8,128)}, f32[33,32,128]{2,1,0:T(8,128)}) custom-call(s32[128,1,256]{2,1,0:T(1,128)} %copy-done.5, f32[128,32,128]{2,1,0:T(8,128)} %copy-done.1), custom_call_target="tpu_custom_call" | custom-call | tf_op jit(solution)/shard_map/scatter/pallas_call | solution.py:327
  98.9 26.4 %exchange.1 = (f32[5,32,1152]{2,1,0:T(8,128)}, f32[4,32,1152]{2,1,0:T(8,128)}, f32[33,32,128]{2,1,0:T(8,128)}, f32[33,32,128]{2,1,0:T(8,128)}, f32[5,32,128]{2,1...) custom-call(f32[33,32,1152]{2,1,0:T(8,128)} %get-tuple-element.24.body.refs_0_, ...), custom_call_target="tpu_custom_call" | custom-call | tf_op jit(solution)/shard_map/exchange/pallas_call | solution.py:400
  125.3 0.0 copy-done
  125.3 29.0 %sheet.1 = (f32[32,32,1024]{2,1,0:T(8,128)}, f32[3,32,1024]{2,1,0:T(8,128)}) custom-call(f32[33,32,1152]{2,1,0:T(8,128)} %get-tuple-element.24.body.refs_0_, f32[5,32,1152]{2,1,0:T(8,128)} %get-tuple-element.26.refs_1_, f32[4,32,1152]{2,1,0:T(8,128)} %get-tuple-element.27.refs_2_, f32[33,32,128]{2,1,0:T(8,128)} %get-tuple-element.28.refs_3_, ...), custom_call_target="tpu_custom_call" | custom-call | tf_op jit(solution)/shard_map/sheet/pallas_call | solution.py:636
Async XLA Ops:
  3.6 1.2 copy-start.2
  4.8 0.8 copy-start.8
  5.7 0.8 copy-start.9
  6.5 0.8 copy-start.10
  7.4 0.7 copy-start.15
  8.0 117.3 %copy-start = (f32[7,32,1024]{2,1,0:T(8,128)}, f32[7,32,1024]{2,1,0:T(8,128)S(1)}, u32[]{:S(2)}) copy-start(f32[7,32,1024]{2,1,0:T(8,128)S(1)} %constant_dynamic-update-slice_fusion.body.refs_9_) | copy-start | bytes 2752516
  54.2 1.3 copy-start.1
  55.5 0.7 copy-start.3
  56.2 0.7 copy-start.4
  56.9 0.7 copy-start.5
  57.6 0.6 copy-start.6
  58.2 0.6 copy-start.7
  58.9 0.6 copy-start.11
  59.5 0.6 copy-start.12
  60.1 0.6 copy-start.13
  60.7 0.6 copy-start.14

commit v3 on v2

v3 whole, which is shorter than its diff:
```python
import functools

import jax
import jax.numpy as jnp
from jax import lax
from jax.experimental import pallas as pl
from jax.experimental.pallas import tpu as pltpu
from jax.sharding import PartitionSpec as P

POINTS = 4
COMP = 8
ITERS = 3
MU_BASE = 10.0
LAMBDA_BULK = 20.0
PRESTRESS = 4.0
TIME_STEP = 1.0
GRAVITY = -1.0
EIG_LOW = 0.5
EIG_HIGH = 2.0

LANE = 128
FRONT = 8
BATCH = 4
HALO = 4
STRIDE = 37
MESH = pl.DeviceIdType.MESH
MIB = 1024 * 1024

VMEM = pl.BlockSpec(memory_space=pltpu.VMEM)
SMEM = pl.BlockSpec(memory_space=pltpu.SMEM)
HBM = pl.BlockSpec(memory_space=pltpu.HBM)


def lane_ids(shape):
    return lax.broadcasted_iota(jnp.int32, shape, len(shape) - 1)


def neighbours():
    n_old, n_new = lax.axis_size("old"), lax.axis_size("new")
    old, new = lax.axis_index("old"), lax.axis_index("new")
    left, right = lax.rem(old + n_old - 1, n_old), lax.rem(old + 1, n_old)
    below, above = lax.rem(new + n_new - 1, n_new), lax.rem(new + 1, n_new)
    return [
        (old, above),
        (old, below),
        (right, new),
        (left, new),
        (right, above),
        (left, above),
        (right, below),
        (left, below),
    ]


def to_neighbours(sources, targets, send_sem, recv_sem):
    return [
        pltpu.make_async_remote_copy(
            src_ref=source,
            dst_ref=target,
            send_sem=send_sem.at[at],
            recv_sem=recv_sem.at[at],
            device_id=device,
            device_id_type=MESH,
        )
        for at, (source, target, device) in enumerate(zip(sources, targets, neighbours()))
    ]


def send_kernel(
    rows_dev,
    cols_dev,
    counts,
    rows_in,
    targets_in,
    weights_in,
    values_in,
    area,
    thick,
    shift_in,
    arrived,
    arrived_ids,
    s_dn,
    s_up,
    s_l,
    s_r,
    s_dl,
    s_dr,
    s_ul,
    s_ur,
    table,
    picked,
    ids,
    notes,
    weights_flat,
    targets,
    weights_raw,
    values,
    rim_low,
    rim_high,
    rim_left,
    rim_right,
    pack_up,
    pack_down,
    pack_right,
    pack_left,
    rows,
    weights,
    local_sem,
    pair_sem,
    near_send,
    near_recv,
):
    n_old, n_new = lax.axis_size("old"), lax.axis_size("new")
    old, new = lax.axis_index("old"), lax.axis_index("new")
    ranks, payload, _ = picked.shape
    slots = payload * 4
    width = cols_dev + LANE
    total = values.shape[1]
    me = old * n_new + new
    top, low = pl.ds(rows_dev - 8, 8), pl.ds(0, 8)
    near, far = pl.ds(0, LANE), pl.ds(cols_dev - LANE, LANE)

    loads = [
        (targets_in, targets),
        (weights_in, weights_raw),
        (values_in, values),
        (rows_in, rows),
    ]
    for source, at, count in ((area, 0, 2), (thick, 2, 2), (shift_in, 4, 3)):
        into = pl.ds(at, count)
        loads.append((source.at[:, top, :], rim_high.at[into]))
        loads.append((source.at[:, low, :], rim_low.at[into]))
        loads.append((source.at[:, :, far], rim_right.at[into]))
        loads.append((source.at[:, :, near], rim_left.at[into]))
    loads = [
        pltpu.make_async_copy(source, target, local_sem.at[at])
        for at, (source, target) in enumerate(loads)
    ]
    for load in loads:
        load.start()

    barrier = pltpu.get_barrier_semaphore()

    def greet(step, _):
        other = lax.rem(me + step, ranks)
        pl.semaphore_signal(
            barrier, inc=1, device_id=(other // n_new, other % n_new), device_id_type=MESH
        )
        return 0

    lax.fori_loop(1, ranks, greet, 0)

    slot = lane_ids((ranks, slots))
    owner = lax.broadcasted_iota(jnp.int32, (ranks, slots), 0)
    count = jnp.broadcast_to(counts[...].astype(jnp.float32), (ranks, ranks)).T.astype(jnp.int32)
    loads[0].wait()
    loads[1].wait()
    target = targets[0]
    cell, col = target // cols_dev, target % cols_dev
    outside = ((owner % n_new == n_new - 1) & (cell % rows_dev == rows_dev - 1)) | (
        (owner // n_new == n_old - 1) & (col == cols_dev - 1)
    )
    used = (slot < count) & jnp.logical_not(outside)
    weights_flat[...] = jnp.where(used, weights_raw[0], 0.0)
    load_weights = pltpu.make_async_copy(weights_flat, weights, local_sem.at[len(loads)])
    load_weights.start()
    where_to = jnp.where(used, FRONT + cell * width + col, FRONT + cols_dev + slot)
    clash = jnp.zeros((ranks, slots), jnp.int32)
    for gap in range(1, BATCH):
        same = (where_to == pltpu.roll(where_to, 4 * gap, 1)) & (slot % (4 * BATCH) >= 4 * gap)
        clash = clash | same.astype(jnp.int32)
    notes[:, 0:slots] = where_to
    notes[:, slots : slots + LANE] = jnp.broadcast_to(
        jnp.max(clash, axis=1, keepdims=True), (ranks, LANE)
    )

    unroll = 8
    loads[2].wait()

    def flip(step, _):
        for at in range(unroll):
            start = pl.multiple_of((step * unroll + at) * LANE, LANE)
            part = values[:, pl.ds(start, LANE)]
            table[pl.ds(start, LANE), :] = jnp.concatenate([part] * 4, axis=0).T
        return 0

    lax.fori_loop(0, total // (LANE * unroll), flip, 0)

    for load in loads[3:]:
        load.wait()
    pack_up[...] = jnp.zeros_like(pack_up)
    pack_down[...] = jnp.zeros_like(pack_down)
    lane = lane_ids((rows_dev, LANE))
    to_right = jnp.zeros((rows_dev, LANE), jnp.float32)
    to_left = jnp.zeros((rows_dev, LANE), jnp.float32)
    for f in range(7):
        if f < 2:
            pack_up[5 * f : 5 * f + 5, :] = rim_high[f, 3:8, :]
            pack_down[4 * f : 4 * f + 4, :] = rim_low[f, 0:4, :]
        else:
            pack_up[8 + f : 9 + f, :] = rim_high[f, 7:8, :]
            if f >= 4:
                pack_down[4 + f : 5 + f, :] = rim_low[f, 0:1, :]
        mine = lane // 8 == f
        to_right = jnp.where(mine, pltpu.roll(rim_right[f], 8 * f + 5, 1), to_right)
        to_left = jnp.where(mine, pltpu.roll(rim_left[f], 8 * f, 1), to_left)
    pack_right[...] = to_right
    pack_left[...] = to_left
    load_weights.wait()
    pl.semaphore_wait(barrier, ranks - 1)

    halo = to_neighbours(
        [
            pack_up,
            pack_down,
            pack_right,
            pack_left,
            pack_right.at[top],
            pack_left.at[top],
            pack_right.at[low],
            pack_left.at[low],
        ],
        [s_dn, s_up, s_l, s_r, s_dl, s_dr, s_ul, s_ur],
        near_send,
        near_recv,
    )
    for copy in halo:
        copy.start()

    lane = lane_ids((1, LANE))
    first, second, third = lane < 32, lane < 64, lane < 96

    def fill(owner):
        for row in range(payload):
            part = [
                table[pl.ds(rows[0, owner, row * 4 + g], 1), :] * weights[owner, row * 4 + g]
                for g in range(4)
            ]
            merged = jnp.where(
                first, part[0], jnp.where(second, part[1], jnp.where(third, part[2], part[3]))
            )
            picked[owner, pl.ds(row, 1), :] = merged
        ids[owner] = notes[pl.ds(owner, 1), :]

    def one_owner(step, _):
        shift = lax.rem(step * STRIDE, ranks)
        to_old = lax.rem(old + shift // n_new, n_old)
        to_new = lax.rem(new + shift % n_new, n_new)
        owner = to_old * n_new + to_new
        fill(owner)
        for at, (source, target) in enumerate(((picked, arrived), (ids, arrived_ids))):
            pltpu.make_async_remote_copy(
                src_ref=source.at[owner],
                dst_ref=target.at[me],
                send_sem=pair_sem.at[2 * at],
                recv_sem=pair_sem.at[2 * at + 1],
                device_id=(to_old, to_new),
                device_id_type=MESH,
            ).start()
        return 0

    lax.fori_loop(1, ranks, one_owner, 0)
    fill(me)
    for at, (source, target) in enumerate(((picked, arrived), (ids, arrived_ids))):
        pltpu.make_async_copy(source.at[me], target.at[me], pair_sem.at[2 * at + 1]).start()
    for copy in halo:
        copy.wait()
    for at, (source, target) in enumerate(((picked, arrived), (ids, arrived_ids))):
        rest = pl.ds(0, ranks - 1)
        pltpu.make_async_copy(source.at[rest], source.at[rest], pair_sem.at[2 * at]).wait()
        pltpu.make_async_copy(source, target, pair_sem.at[2 * at + 1]).wait()


def send(counts, rows, targets, weights, values, area, thick, shift):
    ranks, slots = rows.shape[1:]
    payload = slots // 4
    rows_dev, cols_dev = area.shape[1:]
    halo = [(16, cols_dev)] * 2 + [(rows_dev, LANE)] * 2 + [(8, LANE)] * 4
    shapes = [jax.ShapeDtypeStruct(shape, jnp.float32) for shape in [(ranks, payload, LANE)] + halo]
    shapes.insert(1, jax.ShapeDtypeStruct((ranks, 1, slots + LANE), jnp.int32))

    def scratch(*shape):
        return pltpu.VMEM(shape, jnp.float32)

    result = pl.pallas_call(
        functools.partial(send_kernel, rows_dev, cols_dev),
        out_shape=tuple(shapes),
        in_specs=[VMEM] + [HBM] * 7,
        out_specs=(HBM,) * len(shapes),
        scratch_shapes=[
            scratch(values.shape[1], LANE),
            scratch(ranks, payload, LANE),
            pltpu.VMEM((ranks, 1, slots + LANE), jnp.int32),
            pltpu.VMEM((ranks, slots + LANE), jnp.int32),
            scratch(ranks, slots),
            pltpu.VMEM(targets.shape, jnp.int32),
            scratch(*weights.shape),
            scratch(*values.shape),
            scratch(7, 8, cols_dev),
            scratch(7, 8, cols_dev),
            scratch(7, rows_dev, LANE),
            scratch(7, rows_dev, LANE),
            scratch(16, cols_dev),
            scratch(16, cols_dev),
            scratch(rows_dev, LANE),
            scratch(rows_dev, LANE),
            pltpu.SMEM(rows.shape, jnp.int32),
            pltpu.SMEM((ranks, slots), jnp.float32),
            pltpu.SemaphoreType.DMA((17,)),
            pltpu.SemaphoreType.DMA((4,)),
            pltpu.SemaphoreType.DMA((8,)),
            pltpu.SemaphoreType.DMA((8,)),
        ],
        compiler_params=pltpu.CompilerParams(
            vmem_limit_bytes=24 * MIB, collective_id=1, has_side_effects=True
        ),
        name="send",
    )(counts, rows, targets, weights, values, area, thick, shift)
    return result[0], result[1], result[2:]


def scatter_kernel(rows_dev, cols_dev, ids_in, data_in, part, cols_right, cols_left, acc, carry, data, ids, sem):
    width = cols_dev + LANE
    ranks, payload, _ = data.shape
    size = acc.shape[0]
    chunk = width // 8
    load_ids = pltpu.make_async_copy(ids_in, ids, sem.at[0])
    load_data = pltpu.make_async_copy(data_in, data, sem.at[1])
    load_ids.start()
    load_data.start()
    zeros = jnp.zeros((chunk, LANE), jnp.float32)
    acc[pl.ds(0, FRONT), :] = jnp.zeros((FRONT, LANE), jnp.float32)
    carry[...] = jnp.zeros_like(carry)

    def clear(step, _):
        acc[pl.ds(pl.multiple_of(FRONT + step * chunk, 8), chunk), :] = zeros
        return 0

    lax.fori_loop(0, (size - FRONT) // chunk, clear, 0)
    load_ids.wait()
    load_data.wait()

    lane = lane_ids((1, LANE))
    masks = [(lane >= 32 * g) & (lane < 32 * g + 32) for g in range(4)]

    def add_rows(source, first, count):
        slots = [(r, g) for r in range(count) for g in range(4)]
        where_to = [ids[source, 0, (first + r) * 4 + g] for r, g in slots]
        new = [data[source, pl.ds(first + r, 1), :] for r in range(count)]
        old = [acc[pl.ds(row, 1), :] for row in where_to]
        for (r, g), row, have in zip(slots, where_to, old):
            pltpu.store(acc.at[pl.ds(row, 1), :], have + new[r], mask=masks[g])

    def one_source(source, _):
        clash = ids[source, 0, payload * 4]

        @pl.when(clash == 0)
        def _():
            for first in range(0, payload, BATCH):
                add_rows(source, first, BATCH)

        @pl.when(clash != 0)
        def _():
            def slow(row, _):
                add_rows(source, row, 1)
                return 0

            lax.fori_loop(0, payload, slow, 0)

        return 0

    lax.fori_loop(0, ranks, one_source, 0)

    def fold(total):
        flipped = total.T
        return (flipped[0:32] + flipped[32:64]) + (flipped[64:96] + flipped[96:128])

    upper_base = rows_dev * width
    lane = lane_ids((part.shape[1], LANE))

    def pack(i, own_near, own_far, ghost):
        tile, place = i // 16, i % 16
        mine = lane // 8 == place
        ends = pltpu.roll(jnp.where(lane == 0, ghost, own_far), 8 * place + 4, 1)
        cols_right[tile] = jnp.where(mine, ends, cols_right[tile])
        cols_left[tile] = jnp.where(mine, pltpu.roll(own_near, 8 * place, 1), cols_left[tile])

    cols_right[...] = jnp.zeros_like(cols_right)
    cols_left[...] = jnp.zeros_like(cols_left)
    tiles = width // LANE

    def one_row(i, _):
        done = []
        for tile in range(tiles):
            span = slice(tile * LANE, (tile + 1) * LANE)
            base = pl.multiple_of(i * width + tile * LANE + FRONT, 8)
            lower = acc[pl.ds(base, LANE), :]
            upper = acc[pl.ds(pl.multiple_of(base + upper_base, 8), LANE), :]
            shared = upper + acc[pl.ds(base - 1, LANE), :]
            summed = lower + shared + carry[span, :]
            carry[span, :] = shared + acc[pl.ds(base + upper_base - 1, LANE), :]
            folded = fold(summed)
            part[i, :, span] = folded
            done.append(folded)
        pack(i, done[0], done[-2], done[-1])
        return 0

    lax.fori_loop(0, rows_dev, one_row, 0)
    done = [fold(carry[tile * LANE : (tile + 1) * LANE, :]) for tile in range(tiles)]
    for tile in range(tiles):
        part[rows_dev, :, tile * LANE : (tile + 1) * LANE] = done[tile]
    pack(rows_dev, done[0], done[-2], done[-1])


def scatter(ids, data, rows_dev, cols_dev):
    channels = LANE // 4
    width = cols_dev + LANE
    return pl.pallas_call(
        functools.partial(scatter_kernel, rows_dev, cols_dev),
        out_shape=(
            jax.ShapeDtypeStruct((rows_dev + 1, channels, width), jnp.float32),
            jax.ShapeDtypeStruct((rows_dev // 16 + 1, channels, LANE), jnp.float32),
            jax.ShapeDtypeStruct((rows_dev // 16 + 1, channels, LANE), jnp.float32),
        ),
        in_specs=[HBM, HBM],
        out_specs=(VMEM, VMEM, VMEM),
        scratch_shapes=[
            pltpu.VMEM((FRONT + 2 * rows_dev * width, LANE), jnp.float32),
            pltpu.VMEM((width, LANE), jnp.float32),
            pltpu.VMEM(data.shape, jnp.float32),
            pltpu.SMEM(ids.shape, jnp.int32),
            pltpu.SemaphoreType.DMA((2,)),
        ],
        compiler_params=pltpu.CompilerParams(vmem_limit_bytes=56 * MIB),
        name="scatter",
    )(ids, data)


def first_piola(stretch_x, stretch_y, fields):
    gram_xx = sum(x * x for x in stretch_x)
    gram_xy = sum(x * y for x, y in zip(stretch_x, stretch_y))
    gram_yy = sum(y * y for y in stretch_y)
    determinant = gram_xx * gram_yy - gram_xy * gram_xy
    inverse = 1.0 / determinant
    inv_xx = gram_yy * inverse
    inv_xy = -gram_xy * inverse
    inv_yy = gram_xx * inverse
    shear_mod = MU_BASE * (1.5 + jnp.tanh(fields[3]))
    bulk = LAMBDA_BULK * 0.5 * jnp.log(determinant)
    piola_x, piola_y = [], []
    for along_x, along_y in zip(stretch_x, stretch_y):
        push_x = along_x * inv_xx + along_y * inv_xy
        push_y = along_x * inv_xy + along_y * inv_yy
        piola_x.append(
            shear_mod * (along_x - push_x)
            + bulk * push_x
            + PRESTRESS * (along_x * fields[0] + along_y * fields[2])
        )
        piola_y.append(
            shear_mod * (along_y - push_y)
            + bulk * push_y
            + PRESTRESS * (along_x * fields[2] + along_y * fields[1])
        )
    return piola_x, piola_y


def sheet_kernel(n_rows, n_cols, *refs):
    part_in, cols_right, cols_left, area_in, thick_in, shift_in = refs[:6]
    s_in = refs[6:14]
    total_out, speed_out = refs[14:16]
    p_halo, s_halo, refs = refs[16:24], refs[24:32], refs[32:]
    part, resid, dir_a, dir_b, dir_c, total, field, mem, mass, coef, speed = refs[:11]
    load_sem, save_sem, send_sem, recv_sem = refs[11:]
    p_dn, p_up, p_l, p_r, p_dl, p_dr, p_ul, p_ur = p_halo
    s_dn, s_up, s_l, s_r, s_dl, s_dr, s_ul, s_ur = s_halo
    rows_dev, cols_dev = area_in.shape[1:]
    channels, width = part.shape[1:]
    tall = rows_dev + 16
    middle, main = pl.ds(8, rows_dev), pl.ds(0, cols_dev)

    barrier = pltpu.get_barrier_semaphore()
    for device in neighbours():
        pl.semaphore_signal(barrier, inc=1, device_id=device, device_id_type=MESH)

    field[:, 0:8, :] = jnp.zeros((7, 8, width), jnp.float32)
    field[:, 8 + rows_dev : tall, :] = jnp.zeros((7, 8, width), jnp.float32)
    loads = [
        (area_in, field.at[pl.ds(0, 2), middle, main]),
        (thick_in, field.at[pl.ds(2, 2), middle, main]),
        (shift_in, field.at[pl.ds(4, 3), middle, main]),
    ] + list(zip(s_in, s_halo))
    loads.append((part_in, part))
    loads = [
        pltpu.make_async_copy(source, target, load_sem.at[at])
        for at, (source, target) in enumerate(loads)
    ]
    for load in loads:
        load.start()

    high, low = pl.ds(part_in.shape[0] - HALO - 1, HALO + 1), pl.ds(0, HALO)
    tiles_high, tiles_low = pl.ds((rows_dev - 1) // 16, 2), pl.ds(0, 1)
    pl.semaphore_wait(barrier, 8)
    copies = to_neighbours(
        [
            part_in.at[high],
            part_in.at[low],
            cols_right,
            cols_left,
            cols_right.at[tiles_high],
            cols_left.at[tiles_high],
            cols_right.at[tiles_low],
            cols_left.at[tiles_low],
        ],
        p_halo,
        send_sem,
        recv_sem,
    )
    for copy in copies[2:] + copies[:2]:
        copy.start()

    for load in loads[:-1]:
        load.wait()
    sides = []
    for left, right, size in ((s_l, s_r, rows_dev), (s_dl, s_dr, 8), (s_ul, s_ur, 8)):
        sides.append((left[...], right[...], lane_ids((size, LANE))))
    for f in range(7):
        if f < 2:
            field[f, 3:8, 0:cols_dev] = s_dn[5 * f : 5 * f + 5, :]
            field[f, 8 + rows_dev : 12 + rows_dev, 0:cols_dev] = s_up[4 * f : 4 * f + 4, :]
        else:
            field[f, 7:8, 0:cols_dev] = s_dn[8 + f : 9 + f, :]
            if f >= 4:
                field[f, 8 + rows_dev : 9 + rows_dev, 0:cols_dev] = s_up[4 + f : 5 + f, :]
        wide, narrow = (5, 4) if f < 2 else (1, 0 if f < 4 else 1)
        back = 5 if f < 2 else 5
        made = []
        for left, right, lane in sides:
            from_l = pltpu.roll(left, LANE - back - 8 * f, 1)
            from_r = pltpu.roll(right, (LANE - 8 * f) % LANE, 1)
            made.append(
                jnp.where(lane >= LANE - wide, from_l, jnp.where(lane < narrow, from_r, 0.0))
            )
        field[f, 8 : 8 + rows_dev, cols_dev:width] = made[0]
        row8 = lax.broadcasted_iota(jnp.int32, (8, LANE), 0)
        under = row8 >= 8 - wide
        over = row8 < narrow
        field[f, 0:8, cols_dev:width] = jnp.where(under, made[1], 0.0)
        field[f, 8 + rows_dev : tall, cols_dev:width] = jnp.where(over, made[2], 0.0)

    shape = (tall, width)
    row = lax.broadcasted_iota(jnp.int32, shape, 0) - 8 + lax.axis_index("new") * rows_dev
    lane = lax.broadcasted_iota(jnp.int32, shape, 1)
    col = jnp.where(lane < cols_dev + 64, lane, lane - width) + lax.axis_index("old") * cols_dev
    valid = (row >= 0) & (row < n_rows - 1) & (col >= 0) & (col < n_cols - 1)

    def from_left(x):
        return pltpu.roll(x, 1, 1)

    def from_right(x):
        return pltpu.roll(x, width - 1, 1)

    def from_below(x):
        return pltpu.roll(x, 1, 0)

    def from_above(x):
        return pltpu.roll(x, tall - 1, 0)

    area_low = jnp.where(valid, field[0], 0.0)
    area_up = jnp.where(valid, field[1], 0.0)
    field[2] = field[2] * area_low
    field[3] = field[3] * area_up
    lower, upper = area_low / 12.0, area_up / 12.0
    both = lower + upper
    lower_left, upper_below = from_left(lower), from_below(upper)
    weight = both + lower_left + upper_below + from_below(from_left(both))
    inv = jnp.where(weight > 0.0, 1.0 / (2.0 * weight), 0.0)
    inv_right = from_right(inv)
    east, north = lower + upper_below, upper + lower_left
    coef[0] = inv * (1.0 / 3.0)
    coef[1] = inv * north
    coef[2] = inv * from_below(north)
    coef[3] = from_left(inv * east)
    coef[4] = from_left(inv * both)
    coef[5] = inv_right * east
    coef[6] = inv_right * from_below(both)
    vol_low, vol_up = field[2], field[3]
    mass[...] = (
        vol_low
        + vol_up
        + from_left(vol_low)
        + from_below(vol_up)
        + from_below(from_left(vol_low + vol_up))
    ) * (1.0 / 3.0)
    mem[...] = jnp.zeros_like(mem)

    centre = 0.5 * (EIG_HIGH + EIG_LOW)
    half_width = 0.5 * (EIG_HIGH - EIG_LOW)
    ratio_eig = centre / half_width
    edge = lane_ids((channels, LANE))

    def widen(inner, left, right, place):
        left = pltpu.roll(left, lax.rem(2 * LANE - 4 - 8 * place, LANE), 1)
        right = pltpu.roll(right, lax.rem(LANE - 8 * place, LANE), 1)
        first = inner[:, 0:LANE] + jnp.where(edge == 0, left, 0.0)
        last = inner[:, cols_dev:width] + jnp.where(
            edge >= LANE - HALO, left, jnp.where(edge < HALO, right, 0.0)
        )
        return jnp.concatenate([first, inner[:, LANE:cols_dev], last], axis=1)

    def begin(e, rhs):
        scaled = rhs * coef[0, pl.ds(e + 4, 1), :]
        resid[e] = scaled
        dir_a[e] = scaled * (1.0 / centre)

    def own(i):
        i = jnp.int32(i)
        return widen(part[i], p_l[i // 16], p_r[i // 16], i % 16)

    def under(k):
        i = rows_dev - HALO + k
        tile = i // 16 - (rows_dev - 1) // 16
        return widen(p_dn[k], p_dl[tile], p_dr[tile], jnp.int32(i % 16))

    def over(k):
        return widen(p_up[k], p_ul[0], p_ur[0], jnp.int32(k))

    rhos = [1.0 / ratio_eig]
    for _ in range(ITERS):
        rhos.append(1.0 / (2.0 * ratio_eig - rhos[-1]))
    directions = [dir_a, dir_b, dir_c]

    def sweep_row(sweep, e):
        keep = rhos[sweep + 1] * rhos[sweep]
        gain = 2.0 * rhos[sweep + 1] / half_width
        final = sweep == ITERS - 1
        source = directions[sweep]
        k = [coef[c, pl.ds(e + 4, 1), :] for c in range(1, 7)]
        through = None
        for group in range(0, channels, 8):
            at = slice(group, group + 8)
            here, up, down = source[e, at, :], source[e + 1, at, :], source[e - 1, at, :]
            to_left = k[2] * here + k[3] * up
            to_right = k[4] * here + k[5] * down
            left = resid[e, at, :] - (
                here
                + k[0] * up
                + k[1] * down
                + pltpu.roll(to_left, width - 1, 1)
                + pltpu.roll(to_right, 1, 1)
            )
            new = keep * here + gain * left
            if final:
                summed = (dir_a[e, at, :] + dir_b[e, at, :]) + (here + new)
                total[e, at, :] = summed
                through = summed if through is None else through + summed
            else:
                resid[e, at, :] = left
                directions[sweep + 1][e, at, :] = new
        if final:
            through = through * (1.0 / POINTS)
            for at, value in enumerate((0, 1, 5, 7)):
                mem[at, pl.ds(e + 4, 1), :] = through[value : value + 1, :]

    for copy in copies[2:]:
        copy.wait()
    loads[-1].wait()

    def inner_row(i, _):
        begin(i + HALO, own(i))
        return 0

    lax.fori_loop(1, rows_dev, inner_row, 0)
    for sweep in range(ITERS):

        def inner_sweep(e, _, sweep=sweep):
            sweep_row(sweep, e)
            return 0

        lax.fori_loop(HALO + 2 + sweep, rows_dev + HALO - 1 - sweep, inner_sweep, 0)

    for copy in copies[:2]:
        copy.wait()
    for e in range(HALO):
        begin(e, under(e))
    begin(HALO, own(0) + under(HALO))
    begin(rows_dev + HALO, own(rows_dev) + over(0))
    for e in range(1, HALO):
        begin(rows_dev + HALO + e, over(e))
    for sweep in range(ITERS):
        def outer_sweep(k, _, sweep=sweep):
            low_end = HALO + 1
            sweep_row(
                sweep,
                jnp.where(k < low_end, 1 + sweep + k, rows_dev + HALO - 1 - sweep + k - low_end),
            )
            return 0

        lax.fori_loop(0, 2 * HALO + 1, outer_sweep, 0)

    saves = [pltpu.make_async_copy(total.at[pl.ds(HALO, rows_dev)], total_out, save_sem.at[0])]
    saves[0].start()

    anchor = [field[4 + c] for c in range(3)]
    beside = [from_right(x) for x in anchor]
    upward = [from_above(x) for x in anchor]
    across = [from_above(x) for x in beside]
    m_anchor = [mem[c] for c in range(4)]
    m_beside = [from_right(x) for x in m_anchor]
    m_upward = [from_above(x) for x in m_anchor]
    m_across = [from_above(x) for x in m_beside]
    third = 1.0 / 3.0
    m_low = [(a + b + x) * third for a, b, x in zip(m_anchor, m_beside, m_across)]
    m_up = [(a + x + u) * third for a, x, u in zip(m_anchor, m_across, m_upward)]
    low_x = [b - a for a, b in zip(anchor, beside)]
    low_y = [x - b for b, x in zip(beside, across)]
    up_x = [x - u for u, x in zip(upward, across)]
    up_y = [u - a for a, u in zip(anchor, upward)]
    low_x[0], up_x[0] = 1.0 + low_x[0], 1.0 + up_x[0]
    low_y[1], up_y[1] = 1.0 + low_y[1], 1.0 + up_y[1]
    piola_lx, piola_ly = first_piola(low_x, low_y, m_low)
    piola_ux, piola_uy = first_piola(up_x, up_y, m_up)
    vol_low, vol_up = field[2], field[3]
    node_mass = mass[8 : 8 + rows_dev, 0:cols_dev]
    for c in range(3):
        f_beside = -vol_low * (piola_lx[c] - piola_ly[c])
        f_across_low = -vol_low * piola_ly[c]
        f_across_up = -vol_up * piola_ux[c]
        f_upward = -vol_up * (piola_uy[c] - piola_ux[c])
        f_anchor = -(f_beside + f_across_low) - (f_across_up + f_upward)
        force = (
            f_anchor
            + from_left(f_beside)
            + from_below(f_upward)
            + from_below(from_left(f_across_low + f_across_up))
        )
        speed_up = force[8 : 8 + rows_dev, 0:cols_dev] / node_mass
        speed[c] = speed_up + GRAVITY if c == 2 else speed_up
    saves.append(pltpu.make_async_copy(speed, speed_out, save_sem.at[1]))
    saves[1].start()
    for save in saves:
        save.wait()


def sheet(part, cols_right, cols_left, fields, halo, n_rows, n_cols):
    channels, width = part.shape[1:]
    rows_dev, cols_dev = fields[0].shape[1:]
    tall, long = rows_dev + 16, rows_dev + 2 * HALO
    tiles = cols_right.shape[0]

    def scratch(*shape):
        return pltpu.VMEM(shape, jnp.float32)

    block = scratch(long, channels, width)
    part_halo = [(HALO + 1, channels, width), (HALO, channels, width)]
    part_halo += [(tiles, channels, LANE)] * 2 + [(2, channels, LANE)] * 2
    part_halo += [(1, channels, LANE)] * 2
    return pl.pallas_call(
        functools.partial(sheet_kernel, n_rows, n_cols),
        out_shape=(
            jax.ShapeDtypeStruct((rows_dev, channels, width), jnp.float32),
            jax.ShapeDtypeStruct((3, rows_dev, cols_dev), jnp.float32),
        ),
        in_specs=[HBM] * 14,
        out_specs=(HBM, HBM),
        scratch_shapes=[scratch(*shape) for shape in part_halo]
        + [scratch(*x.shape) for x in halo]
        + [
            scratch(*part.shape),
            block,
            block,
            block,
            block,
            block,
            scratch(7, tall, width),
            scratch(4, tall, width),
            scratch(tall, width),
            scratch(7, tall, width),
            scratch(3, rows_dev, cols_dev),
            pltpu.SemaphoreType.DMA((12,)),
            pltpu.SemaphoreType.DMA((2,)),
            pltpu.SemaphoreType.DMA((8,)),
            pltpu.SemaphoreType.DMA((8,)),
        ],
        compiler_params=pltpu.CompilerParams(
            vmem_limit_bytes=58 * MIB, collective_id=2, has_side_effects=True
        ),
        name="sheet",
    )(part, cols_right, cols_left, *fields, *halo)


def finish_kernel(total, speed_up, velocity, out, vel_out):
    rows, channels, _ = total.shape
    cols = out.shape[2]
    for channel in range(channels):
        out[channel] = total[:, channel, 0:cols]
    vel_out[...] = velocity[...] + TIME_STEP * speed_up[...]


def finish(total, speed_up, velocity):
    rows_dev, channels, width = total.shape
    cols_dev = velocity.shape[2]

    def plane(count):
        return pl.BlockSpec((count, 8, cols_dev), lambda i: (0, i, 0))

    return pl.pallas_call(
        finish_kernel,
        grid=(rows_dev // 8,),
        out_shape=(
            jax.ShapeDtypeStruct((channels, rows_dev, cols_dev), jnp.float32),
            jax.ShapeDtypeStruct(velocity.shape, jnp.float32),
        ),
        in_specs=[pl.BlockSpec((8, channels, width), lambda i: (i, 0, 0)), plane(3), plane(3)],
        out_specs=(plane(channels), plane(3)),
        compiler_params=pltpu.CompilerParams(vmem_limit_bytes=24 * MIB),
        name="finish",
    )(total, speed_up, velocity)


def local(
    old_values,
    pair_rows,
    pair_targets,
    pair_weights,
    pair_counts,
    cell_area,
    thickness,
    displacement,
    velocity,
):
    rows_dev, cols_dev = cell_area.shape[1:]
    n_old, n_new = lax.axis_size("old"), lax.axis_size("new")
    arrived, ids, halo = send(
        pair_counts,
        pair_rows,
        pair_targets,
        pair_weights,
        old_values,
        cell_area,
        thickness,
        displacement,
    )
    part, cols_right, cols_left = scatter(ids, arrived, rows_dev, cols_dev)
    fields = (cell_area, thickness, displacement)
    total, speed_up = sheet(
        part, cols_right, cols_left, fields, halo, n_new * rows_dev, n_old * cols_dev
    )
    return finish(total, speed_up, velocity)


def solution(mesh):
    return jax.shard_map(
        local,
        mesh=mesh,
        in_specs=(
            P(None, ("old", "new")),
            P(("old", "new"), None, None),
            P(("old", "new"), None, None),
            P(("old", "new"), None, None),
            P(("old", "new"), None),
            P(None, "new", "old"),
            P(None, "new", "old"),
            P(None, "new", "old"),
            P(None, "new", "old"),
        ),
        out_specs=(P(None, "new", "old"), P(None, "new", "old")),
        check_vma=False,
    )
```

time: 155 us -> 137 us (0.88)
  Pallas kernels: 139 us -> 118 us
  local copies, waits for them, and re-layouts: 14.4 us -> 17.3 us
    pallas_call x1, Pallas kernels: 26.4 us -> 2.88 us  [finish(): pl.pallas_call(finish_kernel, grid=(rows_dev // 8,), out_shape=(jax.Shape...]
    pallas_call x1, Pallas kernels: 29 us -> 34.4 us  [sheet(): pl.pallas_call(functools.partial(sheet_kernel, n_rows, n_cols), out_shape...]
    unnamed x34 -> x42, local copies, waits for them, and re-layouts: 13.4 us -> 17.3 us
    pallas_call x1, Pallas kernels: 46.2 us -> 42.4 us  [send(): pl.pallas_call(functools.partial(send_kernel, rows_dev, cols_dev), out_sh...]
where the time goes in v3:
time: 137 us; the launch traced here: 136 us
  Pallas kernels  118 us (86%)
  local copies, waits for them, and re-layouts  17.3 us (13%)
    pallas_call x1, Pallas kernels, send(): pl.pallas_call(functools.partial(send_kernel, rows_dev, cols_dev), out_sh...  42.4 us
    pallas_call x1, Pallas kernels, scatter(): pl.pallas_call(functools.partial(scatter_kernel, rows_dev, cols_dev), out...  38.5 us
    pallas_call x1, Pallas kernels, sheet(): pl.pallas_call(functools.partial(sheet_kernel, n_rows, n_cols), out_shape...  34.4 us
    unnamed x42, local copies, waits for them, and re-layouts  17.3 us
    pallas_call x1, Pallas kernels, finish(): pl.pallas_call(finish_kernel, grid=(rows_dev // 8,), out_shape=(jax.Shape...  2.88 us

profile of v3, /device:TPU:1, one launch (start us, length us, event | category | flops | bytes accessed | tf_op | source)
XLA Modules:
  0.0 136.2 jit_solution(12780388197952081267)
XLA Ops:
  0.6 0.0 copy-start.2
  0.6 1.0 copy-done.2
  1.6 0.0 copy-start.3
  1.6 0.9 copy-done.3
  2.6 0.0 copy-start.4
  2.6 0.9 copy-done.4
  3.5 0.0 copy-start.5
  3.5 1.2 copy-done.5
  4.8 0.0 copy-start.11
  4.8 0.8 copy-done.11
  5.6 0.0 copy-start.12
  5.6 0.8 copy-done.12
  6.4 0.0 copy-start.13
  6.4 0.8 copy-done.13
  7.3 0.0 copy-start.20
  7.3 0.7 copy-done.20
  7.9 0.0 copy-start.6
  7.9 42.4 %send.1 = (f32[128,32,128]{2,1,0:T(8,128)S(1)}, s32[128,1,256]{2,1,0:T(1,128)S(1)}, f32[16,1024]{1,0:T(8,128)S(1)}, f32[16,1024]{1,0:T(8,128)S(1)}, f32[32,128]{...) custom-call(s32[1,128]{1,0:T(1,128)S(1)} %copy-done.20, ...), custom_call_target="tpu_custom_call" | custom-call | tf_op jit(solution)/shard_map/send/pallas_call | solution.py:285
  50.3 0.0 copy-start.1
  50.3 1.3 copy-done.1
  51.6 0.0 copy-start.8
  51.6 0.7 copy-done.8
  52.3 0.0 copy-start.9
  52.3 0.6 copy-done.9
  52.9 0.0 copy-start.10
  52.9 0.6 copy-done.10
  53.5 0.0 copy-start.14
  53.5 0.6 copy-done.14
  54.1 0.0 copy-start.15
  54.1 0.6 copy-done.15
  54.7 0.0 copy-start.16
  54.7 0.6 copy-done.16
  55.3 0.0 copy-start.17
  55.3 0.6 copy-done.17
  55.9 0.0 copy-start.18
  55.9 0.6 copy-done.18
  56.5 0.0 copy-start.19
  56.5 0.6 copy-done.19
  57.0 38.5 %scatter.1 = (f32[33,32,1152]{2,1,0:T(8,128)}, f32[3,32,128]{2,1,0:T(8,128)}, f32[3,32,128]{2,1,0:T(8,128)}) custom-call(s32[128,1,256]{2,1,0:T(1,128)} %copy-done.8, f32[128,32,128]{2,1,0:T(8,128)} %copy-done.1), custom_call_target="tpu_custom_call" | custom-call | tf_op jit(solution)/shard_map/scatter/pallas_call | solution.py:418
  95.5 34.4 %sheet.1 = (f32[32,32,1152]{2,1,0:T(8,128)}, f32[3,32,1024]{2,1,0:T(8,128)}) custom-call(f32[33,32,1152]{2,1,0:T(8,128)} %get-tuple-element.19.refs_0_, f32[3,32,128]{2,1,0:T(8,128)} %get-tuple-element.20.refs_1_, f32[3,32,128]{2,1,0:T(8,128)} %get-tuple-element.21.refs_2_, f32[2,32,1024]{2,1,0:T(8,128)} %refs_3_.1, f32[2,32,1024]{2,1,0:T(8,128)} %refs_4_.1, ...), custom_call_target="tpu_custom_call" | custom-call | tf_op jit(solution)/shard_map/sheet/pallas_call | solution.py:757
  129.9 0.0 copy-done.6
  129.9 0.0 copy-start
  130.0 2.3 %copy-done = f32[32,32,1152]{2,1,0:T(8,128)S(1)} copy-done((f32[32,32,1152]{2,1,0:T(8,128)S(1)}, f32[32,32,1152]{2,1,0:T(8,128)}, u32[]{:S(2)}) %copy-start) | copy-done | bytes 4718616
  132.3 0.0 copy-start.7
  132.3 1.0 copy-done.7
  133.3 2.9 %finish.1 = (f32[32,32,1024]{2,1,0:T(8,128)}, f32[3,32,1024]{2,1,0:T(8,128)}) custom-call(f32[32,32,1152]{2,1,0:T(8,128)S(1)} %copy-done, f32[3,32,1024]{2,1,0:T(8,128)S(1)} %copy-done.7, f32[3,32,1024]{2,1,0:T(8,128)S(1)} %copy-done.6), custom_call_target="tpu_custom_call" | custom-call | tf_op jit(solution)/shard_map/finish/pallas_call | solution.py:806
Async XLA Ops:
  0.6 1.0 copy-start.2
  1.6 0.9 copy-start.3
  2.6 0.9 copy-start.4
  3.5 1.2 copy-start.5
  4.8 0.8 copy-start.11
  5.6 0.8 copy-start.12
  6.4 0.8 copy-start.13
  7.3 0.7 copy-start.20
  7.9 122.0 %copy-start.6 = (f32[3,32,1024]{2,1,0:T(8,128)S(1)}, f32[3,32,1024]{2,1,0:T(8,128)}, u32[]{:S(2)}) copy-start(f32[3,32,1024]{2,1,0:T(8,128)} %velocity.1) | copy-start | bytes 1179652
  50.3 1.3 copy-start.1
  51.6 0.7 copy-start.8
  52.3 0.6 copy-start.9
  52.9 0.6 copy-start.10
  53.5 0.6 copy-start.14
  54.1 0.6 copy-start.15
  54.7 0.6 copy-start.16
  55.3 0.6 copy-start.17
  55.9 0.6 copy-start.18
  56.5 0.6 copy-start.19
  129.9 2.3 %copy-start = (f32[32,32,1152]{2,1,0:T(8,128)S(1)}, f32[32,32,1152]{2,1,0:T(8,128)}, u32[]{:S(2)}) copy-start(f32[32,32,1152]{2,1,0:T(8,128)} %get-tuple-element.30.total) | copy-start | bytes 14155780
  132.3 1.0 copy-start.7

commit v4 on v3

--- a/solution.py
+++ b/solution.py
@@ -312,7 +312,7 @@
             pltpu.SemaphoreType.DMA((8,)),
         ],
         compiler_params=pltpu.CompilerParams(
-            vmem_limit_bytes=24 * MIB, collective_id=1, has_side_effects=True
+            vmem_limit_bytes=60 * MIB, collective_id=1, has_side_effects=True
         ),
         name="send",
     )(counts, rows, targets, weights, values, area, thick, shift)
@@ -431,7 +431,7 @@
             pltpu.SMEM(ids.shape, jnp.int32),
             pltpu.SemaphoreType.DMA((2,)),
         ],
-        compiler_params=pltpu.CompilerParams(vmem_limit_bytes=56 * MIB),
+        compiler_params=pltpu.CompilerParams(vmem_limit_bytes=60 * MIB),
         name="scatter",
     )(ids, data)
 
@@ -782,7 +782,7 @@
             pltpu.SemaphoreType.DMA((8,)),
         ],
         compiler_params=pltpu.CompilerParams(
-            vmem_limit_bytes=58 * MIB, collective_id=2, has_side_effects=True
+            vmem_limit_bytes=60 * MIB, collective_id=2, has_side_effects=True
         ),
         name="sheet",
     )(part, cols_right, cols_left, *fields, *halo)
@@ -812,7 +812,7 @@
         ),
         in_specs=[pl.BlockSpec((8, channels, width), lambda i: (i, 0, 0)), plane(3), plane(3)],
         out_specs=(plane(channels), plane(3)),
-        compiler_params=pltpu.CompilerParams(vmem_limit_bytes=24 * MIB),
+        compiler_params=pltpu.CompilerParams(vmem_limit_bytes=60 * MIB),
         name="finish",
     )(total, speed_up, velocity)
 

time: 137 us -> 122 us (0.89)
  local copies, waits for them, and re-layouts: 17.3 us -> 0 us
  Pallas kernels: 118 us -> 121 us
    unnamed x42 -> x0, local copies, waits for them, and re-layouts: 17.3 us -> none
    pallas_call x1, Pallas kernels: 2.88 us -> 5.38 us  [finish(): pl.pallas_call(finish_kernel, grid=(rows_dev // 8,), out_shape=(jax.Shape...]
where the time goes in v4:
time: 122 us
  Pallas kernels  121 us (99%)
    pallas_call x1, Pallas kernels, send(): pl.pallas_call(functools.partial(send_kernel, rows_dev, cols_dev), out_sh...  42.6 us
    pallas_call x1, Pallas kernels, scatter(): pl.pallas_call(functools.partial(scatter_kernel, rows_dev, cols_dev), out...  38.5 us
    pallas_call x1, Pallas kernels, sheet(): pl.pallas_call(functools.partial(sheet_kernel, n_rows, n_cols), out_shape...  34.4 us
    pallas_call x1, Pallas kernels, finish(): pl.pallas_call(finish_kernel, grid=(rows_dev // 8,), out_shape=(jax.Shape...  5.38 us

profile of v4, /device:TPU:1, one launch (start us, length us, event | category | flops | bytes accessed | tf_op | source)
XLA Modules:
  0.0 121.5 jit_solution(6526112900275387966)
XLA Ops:
  0.6 42.6 %send.1 = (f32[128,32,128]{2,1,0:T(8,128)}, s32[128,1,256]{2,1,0:T(1,128)}, f32[16,1024]{1,0:T(8,128)}, f32[16,1024]{1,0:T(8,128)}, f32[32,128]{1,0:T(8,128)}, /...) custom-call(s32[1,128]{1,0:T(1,128)} %counts.1, ...), custom_call_target="tpu_custom_call" | custom-call | tf_op jit(solution)/shard_map/send/pallas_call | solution.py:285
  43.2 38.5 %scatter.1 = (f32[33,32,1152]{2,1,0:T(8,128)}, f32[3,32,128]{2,1,0:T(8,128)}, f32[3,32,128]{2,1,0:T(8,128)}) custom-call(s32[128,1,256]{2,1,0:T(1,128)} %get-tuple-element.17.ids_in, f32[128,32,128]{2,1,0:T(8,128)} %get-tuple-element.18.data_in), custom_call_target="tpu_custom_call" | custom-call | tf_op jit(solution)/shard_map/scatter/pallas_call | solution.py:418
  81.8 34.4 %sheet.1 = (f32[32,32,1152]{2,1,0:T(8,128)}, f32[3,32,1024]{2,1,0:T(8,128)}) custom-call(f32[33,32,1152]{2,1,0:T(8,128)} %get-tuple-element.19.refs_0_, f32[3,32,128]{2,1,0:T(8,128)} %get-tuple-element.20.refs_1_, f32[3,32,128]{2,1,0:T(8,128)} %get-tuple-element.21.refs_2_, f32[2,32,1024]{2,1,0:T(8,128)} %refs_3_.1, f32[2,32,1024]{2,1,0:T(8,128)} %refs_4_.1, ...), custom_call_target="tpu_custom_call" | custom-call | tf_op jit(solution)/shard_map/sheet/pallas_call | solution.py:757
  116.1 5.4 %finish.1 = (f32[32,32,1024]{2,1,0:T(8,128)}, f32[3,32,1024]{2,1,0:T(8,128)}) custom-call(f32[32,32,1152]{2,1,0:T(8,128)} %get-tuple-element.30.total, f32[3,32,1024]{2,1,0:T(8,128)} %get-tuple-element.31.speed_up, f32[3,32,1024]{2,1,0:T(8,128)} %velocity.1), custom_call_target="tpu_custom_call" | custom-call | tf_op jit(solution)/shard_map/finish/pallas_call | solution.py:806

commit v5 on v3

--- a/solution.py
+++ b/solution.py
@@ -87,6 +87,7 @@
     s_dr,
     s_ul,
     s_ur,
+    acc,
     table,
     picked,
     ids,
@@ -242,12 +243,22 @@
             picked[owner, pl.ds(row, 1), :] = merged
         ids[owner] = notes[pl.ds(owner, 1), :]
 
+    chunk = (acc.shape[0] - FRONT) // ranks
+
+    def clear(step):
+        start = pl.multiple_of(FRONT + step * chunk, 8)
+        acc[pl.ds(start, chunk), :] = jnp.zeros((chunk, LANE), jnp.float32)
+
+    acc[pl.ds(0, FRONT), :] = jnp.zeros((FRONT, LANE), jnp.float32)
+    clear(0)
+
     def one_owner(step, _):
         shift = lax.rem(step * STRIDE, ranks)
         to_old = lax.rem(old + shift // n_new, n_old)
         to_new = lax.rem(new + shift % n_new, n_new)
         owner = to_old * n_new + to_new
         fill(owner)
+        clear(step)
         for at, (source, target) in enumerate(((picked, arrived), (ids, arrived_ids))):
             pltpu.make_async_remote_copy(
                 src_ref=source.at[owner],
@@ -276,8 +287,10 @@
     payload = slots // 4
     rows_dev, cols_dev = area.shape[1:]
     halo = [(16, cols_dev)] * 2 + [(rows_dev, LANE)] * 2 + [(8, LANE)] * 4
-    shapes = [jax.ShapeDtypeStruct(shape, jnp.float32) for shape in [(ranks, payload, LANE)] + halo]
+    shapes = [jax.ShapeDtypeStruct(shape, jnp.float32) for shape in halo]
+    shapes.insert(0, jax.ShapeDtypeStruct((ranks, payload, LANE), jnp.float32))
     shapes.insert(1, jax.ShapeDtypeStruct((ranks, 1, slots + LANE), jnp.int32))
+    shapes.append(pltpu.VMEM((FRONT + 2 * rows_dev * (cols_dev + LANE), LANE), jnp.float32))
 
     def scratch(*shape):
         return pltpu.VMEM(shape, jnp.float32)
@@ -286,7 +299,7 @@
         functools.partial(send_kernel, rows_dev, cols_dev),
         out_shape=tuple(shapes),
         in_specs=[VMEM] + [HBM] * 7,
-        out_specs=(HBM,) * len(shapes),
+        out_specs=(HBM,) * (len(shapes) - 1) + (VMEM,),
         scratch_shapes=[
             scratch(values.shape[1], LANE),
             scratch(ranks, payload, LANE),
@@ -316,29 +329,36 @@
         ),
         name="send",
     )(counts, rows, targets, weights, values, area, thick, shift)
-    return result[0], result[1], result[2:]
-
-
-def scatter_kernel(rows_dev, cols_dev, ids_in, data_in, part, cols_right, cols_left, acc, carry, data, ids, sem):
+    return result[0], result[1], result[2:-1], result[-1]
+
+
+def scatter_kernel(
+    rows_dev,
+    cols_dev,
+    ids_in,
+    data_in,
+    _,
+    part,
+    cols_right,
+    cols_left,
+    acc,
+    carry,
+    data,
+    ids,
+    ids_sem,
+    data_sem,
+):
     width = cols_dev + LANE
     ranks, payload, _ = data.shape
-    size = acc.shape[0]
-    chunk = width // 8
-    load_ids = pltpu.make_async_copy(ids_in, ids, sem.at[0])
-    load_data = pltpu.make_async_copy(data_in, data, sem.at[1])
-    load_ids.start()
-    load_data.start()
-    zeros = jnp.zeros((chunk, LANE), jnp.float32)
-    acc[pl.ds(0, FRONT), :] = jnp.zeros((FRONT, LANE), jnp.float32)
+    quarter = ranks // 4
+    loads = []
+    for at in range(4):
+        some = pl.ds(at * quarter, quarter)
+        for source, target, sem in ((ids_in, ids, ids_sem), (data_in, data, data_sem)):
+            loads.append(pltpu.make_async_copy(source.at[some], target.at[some], sem.at[at]))
+    for load in loads:
+        load.start()
     carry[...] = jnp.zeros_like(carry)
-
-    def clear(step, _):
-        acc[pl.ds(pl.multiple_of(FRONT + step * chunk, 8), chunk), :] = zeros
-        return 0
-
-    lax.fori_loop(0, (size - FRONT) // chunk, clear, 0)
-    load_ids.wait()
-    load_data.wait()
 
     lane = lane_ids((1, LANE))
     masks = [(lane >= 32 * g) & (lane < 32 * g + 32) for g in range(4)]
@@ -369,7 +389,10 @@
 
         return 0
 
-    lax.fori_loop(0, ranks, one_source, 0)
+    for at in range(4):
+        loads[2 * at].wait()
+        loads[2 * at + 1].wait()
+        lax.fori_loop(at * quarter, (at + 1) * quarter, one_source, 0)
 
     def fold(total):
         flipped = total.T
@@ -412,7 +435,7 @@
     pack(rows_dev, done[0], done[-2], done[-1])
 
 
-def scatter(ids, data, rows_dev, cols_dev):
+def scatter(ids, data, acc, rows_dev, cols_dev):
     channels = LANE // 4
     width = cols_dev + LANE
     return pl.pallas_call(
@@ -421,19 +444,21 @@
             jax.ShapeDtypeStruct((rows_dev + 1, channels, width), jnp.float32),
             jax.ShapeDtypeStruct((rows_dev // 16 + 1, channels, LANE), jnp.float32),
             jax.ShapeDtypeStruct((rows_dev // 16 + 1, channels, LANE), jnp.float32),
+            pltpu.VMEM(acc.shape, jnp.float32),
         ),
-        in_specs=[HBM, HBM],
-        out_specs=(VMEM, VMEM, VMEM),
+        in_specs=[HBM, HBM, VMEM],
+        out_specs=(VMEM, VMEM, VMEM, VMEM),
+        input_output_aliases={2: 3},
         scratch_shapes=[
-            pltpu.VMEM((FRONT + 2 * rows_dev * width, LANE), jnp.float32),
             pltpu.VMEM((width, LANE), jnp.float32),
             pltpu.VMEM(data.shape, jnp.float32),
             pltpu.SMEM(ids.shape, jnp.int32),
-            pltpu.SemaphoreType.DMA((2,)),
+            pltpu.SemaphoreType.DMA((4,)),
+            pltpu.SemaphoreType.DMA((4,)),
         ],
-        compiler_params=pltpu.CompilerParams(vmem_limit_bytes=56 * MIB),
+        compiler_params=pltpu.CompilerParams(vmem_limit_bytes=24 * MIB),
         name="scatter",
-    )(ids, data)
+    )(ids, data, acc)[:3]
 
 
 def first_piola(stretch_x, stretch_y, fields):
@@ -467,10 +492,10 @@
 def sheet_kernel(n_rows, n_cols, *refs):
     part_in, cols_right, cols_left, area_in, thick_in, shift_in = refs[:6]
     s_in = refs[6:14]
-    total_out, speed_out = refs[14:16]
+    total, speed = refs[14:16]
     p_halo, s_halo, refs = refs[16:24], refs[24:32], refs[32:]
-    part, resid, dir_a, dir_b, dir_c, total, field, mem, mass, coef, speed = refs[:11]
-    load_sem, save_sem, send_sem, recv_sem = refs[11:]
+    part, resid, dir_a, dir_b, dir_c, field, mem, mass, coef = refs[:9]
+    load_sem, send_sem, recv_sem = refs[9:]
     p_dn, p_up, p_l, p_r, p_dl, p_dr, p_ul, p_ur = p_halo
     s_dn, s_up, s_l, s_r, s_dl, s_dr, s_ul, s_ur = s_halo
     rows_dev, cols_dev = area_in.shape[1:]
@@ -696,9 +721,6 @@
             return 0
 
         lax.fori_loop(0, 2 * HALO + 1, outer_sweep, 0)
-
-    saves = [pltpu.make_async_copy(total.at[pl.ds(HALO, rows_dev)], total_out, save_sem.at[0])]
-    saves[0].start()
 
     anchor = [field[4 + c] for c in range(3)]
     beside = [from_right(x) for x in anchor]
@@ -735,10 +757,6 @@
         )
         speed_up = force[8 : 8 + rows_dev, 0:cols_dev] / node_mass
         speed[c] = speed_up + GRAVITY if c == 2 else speed_up
-    saves.append(pltpu.make_async_copy(speed, speed_out, save_sem.at[1]))
-    saves[1].start()
-    for save in saves:
-        save.wait()
 
 
 def sheet(part, cols_right, cols_left, fields, halo, n_rows, n_cols):
@@ -757,11 +775,11 @@
     return pl.pallas_call(
         functools.partial(sheet_kernel, n_rows, n_cols),
         out_shape=(
-            jax.ShapeDtypeStruct((rows_dev, channels, width), jnp.float32),
-            jax.ShapeDtypeStruct((3, rows_dev, cols_dev), jnp.float32),
+            block,
+            scratch(3, rows_dev, cols_dev),
         ),
         in_specs=[HBM] * 14,
-        out_specs=(HBM, HBM),
+        out_specs=(VMEM, VMEM),
         scratch_shapes=[scratch(*shape) for shape in part_halo]
         + [scratch(*x.shape) for x in halo]
         + [
@@ -770,35 +788,32 @@
             block,
             block,
             block,
-            block,
             scratch(7, tall, width),
             scratch(4, tall, width),
             scratch(tall, width),
             scratch(7, tall, width),
-            scratch(3, rows_dev, cols_dev),
             pltpu.SemaphoreType.DMA((12,)),
-            pltpu.SemaphoreType.DMA((2,)),
             pltpu.SemaphoreType.DMA((8,)),
             pltpu.SemaphoreType.DMA((8,)),
         ],
         compiler_params=pltpu.CompilerParams(
-            vmem_limit_bytes=58 * MIB, collective_id=2, has_side_effects=True
+            vmem_limit_bytes=54 * MIB, collective_id=2, has_side_effects=True
         ),
         name="sheet",
     )(part, cols_right, cols_left, *fields, *halo)
 
 
 def finish_kernel(total, speed_up, velocity, out, vel_out):
-    rows, channels, _ = total.shape
-    cols = out.shape[2]
+    channels, rows, cols = out.shape
+    here = pl.ds(HALO + pl.program_id(0) * rows, rows)
     for channel in range(channels):
-        out[channel] = total[:, channel, 0:cols]
+        out[channel] = total[here, channel, 0:cols]
     vel_out[...] = velocity[...] + TIME_STEP * speed_up[...]
 
 
 def finish(total, speed_up, velocity):
-    rows_dev, channels, width = total.shape
-    cols_dev = velocity.shape[2]
+    channels = total.shape[1]
+    rows_dev, cols_dev = velocity.shape[1:]
 
     def plane(count):
         return pl.BlockSpec((count, 8, cols_dev), lambda i: (0, i, 0))
@@ -810,9 +825,9 @@
             jax.ShapeDtypeStruct((channels, rows_dev, cols_dev), jnp.float32),
             jax.ShapeDtypeStruct(velocity.shape, jnp.float32),
         ),
-        in_specs=[pl.BlockSpec((8, channels, width), lambda i: (i, 0, 0)), plane(3), plane(3)],
+        in_specs=[VMEM, plane(3), plane(3)],
         out_specs=(plane(channels), plane(3)),
-        compiler_params=pltpu.CompilerParams(vmem_limit_bytes=24 * MIB),
+        compiler_params=pltpu.CompilerParams(vmem_limit_bytes=40 * MIB),
         name="finish",
     )(total, speed_up, velocity)
 
@@ -830,7 +845,7 @@
 ):
     rows_dev, cols_dev = cell_area.shape[1:]
     n_old, n_new = lax.axis_size("old"), lax.axis_size("new")
-    arrived, ids, halo = send(
+    arrived, ids, halo, acc = send(
         pair_counts,
         pair_rows,
         pair_targets,
@@ -840,7 +855,7 @@
         thickness,
         displacement,
     )
-    part, cols_right, cols_left = scatter(ids, arrived, rows_dev, cols_dev)
+    part, cols_right, cols_left = scatter(ids, arrived, acc, rows_dev, cols_dev)
     fields = (cell_area, thickness, displacement)
     total, speed_up = sheet(
         part, cols_right, cols_left, fields, halo, n_new * rows_dev, n_old * cols_dev

time: 137 us -> 117 us (0.85)
  local copies, waits for them, and re-layouts: 17.3 us -> 0.01 us
  Pallas kernels: 118 us -> 116 us
    unnamed x42 -> x2, local copies, waits for them, and re-layouts: 17.3 us -> 0.01 us
    pallas_call x1, Pallas kernels: 34.4 us -> 32.2 us  [sheet(): pl.pallas_call(functools.partial(sheet_kernel, n_rows, n_cols), out_shape...]
where the time goes in v5:
time: 117 us
  Pallas kernels  116 us (99%)
    pallas_call x1, Pallas kernels, send(): pl.pallas_call(functools.partial(send_kernel, rows_dev, cols_dev), out_sh...  42.6 us
    pallas_call x1, Pallas kernels, scatter(): pl.pallas_call(functools.partial(scatter_kernel, rows_dev, cols_dev), out...  38.5 us
    pallas_call x1, Pallas kernels, sheet(): pl.pallas_call(functools.partial(sheet_kernel, n_rows, n_cols), out_shape...  32.2 us
    pallas_call x1, Pallas kernels, finish(): pl.pallas_call(finish_kernel, grid=(rows_dev // 8,), out_shape=(jax.Shape...  2.89 us

profile of v5, /device:TPU:1, one launch (start us, length us, event | category | flops | bytes accessed | tf_op | source)
XLA Modules:
  0.0 116.8 jit_solution(5765518731964476518)
XLA Ops:
  0.6 42.6 %send.1 = (f32[128,32,128]{2,1,0:T(8,128)}, s32[128,1,256]{2,1,0:T(1,128)}, f32[16,1024]{1,0:T(8,128)}, f32[16,1024]{1,0:T(8,128)}, f32[32,128]{1,0:T(8,128)}, /...) custom-call(s32[1,128]{1,0:T(1,128)} %counts.1, ...), custom_call_target="tpu_custom_call" | custom-call | tf_op jit(solution)/shard_map/send/pallas_call | solution.py:298
  43.2 38.5 %scatter.1 = (f32[33,32,1152]{2,1,0:T(8,128)}, f32[3,32,128]{2,1,0:T(8,128)}, f32[3,32,128]{2,1,0:T(8,128)}, f32[73736,128]{1,0:T(8,128)S(1)}) custom-call(s32[128,1,256]{2,1,0:T(1,128)} %get-tuple-element.18.ids_in, f32[128,32,128]{2,1,0:T(8,128)} %get-tuple-element.19.data_in, f32[73736,128]{1,0:T(8,128)S(1)} %get-tuple-element.20._), custom_call_target="tpu_custom_call", output_to_operand_aliasing={{3}: (2, {})} | custom-call | tf_op jit(solution)/shard_map/scatter/pallas_call | solution.py:441
  81.7 0.0 copy-start
  81.7 32.2 %sheet.1 = (f32[40,32,1152]{2,1,0:T(8,128)S(1)}, f32[3,32,1024]{2,1,0:T(8,128)S(1)}) custom-call(f32[33,32,1152]{2,1,0:T(8,128)} %get-tuple-element.21.refs_0_, f32[3,32,128]{2,1,0:T(8,128)} %get-tuple-element.22.refs_1_, f32[3,32,128]{2,1,0:T(8,128)} %get-tuple-element.23.refs_2_, f32[2,32,1024]{2,1,0:T(8,128)} %refs_3_.1, f32[2,32,1024]{2,1,0:T(8,128)} %refs_4_.1, ...), custom_call_target="tpu_custom_call" | custom-call | tf_op jit(solution)/shard_map/sheet/pallas_call | solution.py:775
  113.9 0.0 copy-done
  113.9 2.9 %finish.1 = (f32[32,32,1024]{2,1,0:T(8,128)}, f32[3,32,1024]{2,1,0:T(8,128)}) custom-call(f32[40,32,1152]{2,1,0:T(8,128)S(1)} %get-tuple-element.32.total, f32[3,32,1024]{2,1,0:T(8,128)S(1)} %get-tuple-element.33.speed_up, f32[3,32,1024]{2,1,0:T(8,128)S(1)} %copy-done), custom_call_target="tpu_custom_call" | custom-call | tf_op jit(solution)/shard_map/finish/pallas_call | solution.py:821
Async XLA Ops:
  81.7 32.2 %copy-start = (f32[3,32,1024]{2,1,0:T(8,128)S(1)}, f32[3,32,1024]{2,1,0:T(8,128)}, u32[]{:S(2)}) copy-start(f32[3,32,1024]{2,1,0:T(8,128)} %velocity.1) | copy-start | bytes 1179652

commit v6 on v5

--- a/solution.py
+++ b/solution.py
@@ -53,6 +53,7 @@
 
 
 def to_neighbours(sources, targets, send_sem, recv_sem):
+    around = neighbours()
     return [
         pltpu.make_async_remote_copy(
             src_ref=source,
@@ -62,7 +63,7 @@
             device_id=device,
             device_id_type=MESH,
         )
-        for at, (source, target, device) in enumerate(zip(sources, targets, neighbours()))
+        for at, (source, target, device) in enumerate(zip(sources, targets, around + around))
     ]
 
 
@@ -115,7 +116,6 @@
     old, new = lax.axis_index("old"), lax.axis_index("new")
     ranks, payload, _ = picked.shape
     slots = payload * 4
-    width = cols_dev + LANE
     total = values.shape[1]
     me = old * n_new + new
     top, low = pl.ds(rows_dev - 8, 8), pl.ds(0, 8)
@@ -165,15 +165,15 @@
     weights_flat[...] = jnp.where(used, weights_raw[0], 0.0)
     load_weights = pltpu.make_async_copy(weights_flat, weights, local_sem.at[len(loads)])
     load_weights.start()
-    where_to = jnp.where(used, FRONT + cell * width + col, FRONT + cols_dev + slot)
+    spare = slot // 4 % FRONT
+    where_to = jnp.where(used, FRONT + target, spare)
     clash = jnp.zeros((ranks, slots), jnp.int32)
     for gap in range(1, BATCH):
         same = (where_to == pltpu.roll(where_to, 4 * gap, 1)) & (slot % (4 * BATCH) >= 4 * gap)
         clash = clash | same.astype(jnp.int32)
-    notes[:, 0:slots] = where_to
-    notes[:, slots : slots + LANE] = jnp.broadcast_to(
-        jnp.max(clash, axis=1, keepdims=True), (ranks, LANE)
-    )
+    found = jnp.broadcast_to(jnp.max(clash, axis=1, keepdims=True), (ranks, slots))
+    notes[:, 0:slots] = jnp.where(clash > 0, spare, where_to)
+    notes[:, slots : 2 * slots] = jnp.where(slot == 0, found, clash * where_to)
 
     unroll = 8
     loads[2].wait()
@@ -243,13 +243,14 @@
             picked[owner, pl.ds(row, 1), :] = merged
         ids[owner] = notes[pl.ds(owner, 1), :]
 
-    chunk = (acc.shape[0] - FRONT) // ranks
+    chunk = (acc.shape[0] - 2 * FRONT) // ranks
 
     def clear(step):
         start = pl.multiple_of(FRONT + step * chunk, 8)
         acc[pl.ds(start, chunk), :] = jnp.zeros((chunk, LANE), jnp.float32)
 
-    acc[pl.ds(0, FRONT), :] = jnp.zeros((FRONT, LANE), jnp.float32)
+    for end in (0, acc.shape[0] - FRONT):
+        acc[pl.ds(end, FRONT), :] = jnp.zeros((FRONT, LANE), jnp.float32)
     clear(0)
 
     def one_owner(step, _):
@@ -289,8 +290,8 @@
     halo = [(16, cols_dev)] * 2 + [(rows_dev, LANE)] * 2 + [(8, LANE)] * 4
     shapes = [jax.ShapeDtypeStruct(shape, jnp.float32) for shape in halo]
     shapes.insert(0, jax.ShapeDtypeStruct((ranks, payload, LANE), jnp.float32))
-    shapes.insert(1, jax.ShapeDtypeStruct((ranks, 1, slots + LANE), jnp.int32))
-    shapes.append(pltpu.VMEM((FRONT + 2 * rows_dev * (cols_dev + LANE), LANE), jnp.float32))
+    shapes.insert(1, jax.ShapeDtypeStruct((ranks, 1, 2 * slots), jnp.int32))
+    shapes.append(pltpu.VMEM((2 * FRONT + 2 * rows_dev * cols_dev, LANE), jnp.float32))
 
     def scratch(*shape):
         return pltpu.VMEM(shape, jnp.float32)
@@ -303,8 +304,8 @@
         scratch_shapes=[
             scratch(values.shape[1], LANE),
             scratch(ranks, payload, LANE),
-            pltpu.VMEM((ranks, 1, slots + LANE), jnp.int32),
-            pltpu.VMEM((ranks, slots + LANE), jnp.int32),
+            pltpu.VMEM((ranks, 1, 2 * slots), jnp.int32),
+            pltpu.VMEM((ranks, 2 * slots), jnp.int32),
             scratch(ranks, slots),
             pltpu.VMEM(targets.shape, jnp.int32),
             scratch(*weights.shape),
@@ -332,24 +333,53 @@
     return result[0], result[1], result[2:-1], result[-1]
 
 
+def fold(total):
+    flipped = total.T
+    return (flipped[0:32] + flipped[32:64]) + (flipped[64:96] + flipped[96:128])
+
+
+def node_parts(acc, rows_dev, cols_dev, i, first, size, cells, below):
+    upper = rows_dev * cols_dev
+    base = i * cols_dev + (FRONT + first)
+    here, left = [], []
+    if cells:
+        here += [base, base + upper]
+        left += [base - 1]
+    if below:
+        here += [base + upper - cols_dev]
+        left += [base - cols_dev - 1, base + upper - cols_dev - 1]
+    here, left = ([acc[pl.ds(at, size), :] for at in some] for some in (here, left))
+    return functools.reduce(jnp.add, here), functools.reduce(jnp.add, left)
+
+
+def node_tile(acc, rows_dev, cols_dev, i, tile, cells=True, below=True):
+    here, left = node_parts(acc, rows_dev, cols_dev, i, tile * LANE, LANE, cells, below)
+    if tile == 0:
+        rows = lax.broadcasted_iota(jnp.int32, (LANE, LANE), 0)
+        left = jnp.where(rows == 0, 0.0, left)
+    return fold(here + left)
+
+
 def scatter_kernel(
     rows_dev,
     cols_dev,
     ids_in,
     data_in,
     _,
-    part,
+    rim_high,
+    rim_low,
     cols_right,
     cols_left,
     acc,
-    carry,
+    flat_right,
+    flat_left,
     data,
     ids,
     ids_sem,
     data_sem,
 ):
-    width = cols_dev + LANE
     ranks, payload, _ = data.shape
+    slots = payload * 4
     quarter = ranks // 4
     loads = []
     for at in range(4):
@@ -358,35 +388,22 @@
             loads.append(pltpu.make_async_copy(source.at[some], target.at[some], sem.at[at]))
     for load in loads:
         load.start()
-    carry[...] = jnp.zeros_like(carry)
+    flat_right[...] = jnp.zeros_like(flat_right)
+    flat_left[...] = jnp.zeros_like(flat_left)
 
     lane = lane_ids((1, LANE))
-    masks = [(lane >= 32 * g) & (lane < 32 * g + 32) for g in range(4)]
-
-    def add_rows(source, first, count):
-        slots = [(r, g) for r in range(count) for g in range(4)]
-        where_to = [ids[source, 0, (first + r) * 4 + g] for r, g in slots]
-        new = [data[source, pl.ds(first + r, 1), :] for r in range(count)]
+    masks = [lane // 32 == g for g in range(4)]
+
+    def add_rows(source, first):
+        where_to = [ids[source, 0, first * 4 + k] for k in range(4 * BATCH)]
+        new = [data[source, pl.ds(first + r, 1), :] for r in range(BATCH)]
         old = [acc[pl.ds(row, 1), :] for row in where_to]
-        for (r, g), row, have in zip(slots, where_to, old):
-            pltpu.store(acc.at[pl.ds(row, 1), :], have + new[r], mask=masks[g])
+        for k, (row, have) in enumerate(zip(where_to, old)):
+            pltpu.store(acc.at[pl.ds(row, 1), :], have + new[k // 4], mask=masks[k % 4])
 
     def one_source(source, _):
-        clash = ids[source, 0, payload * 4]
-
-        @pl.when(clash == 0)
-        def _():
-            for first in range(0, payload, BATCH):
-                add_rows(source, first, BATCH)
-
-        @pl.when(clash != 0)
-        def _():
-            def slow(row, _):
-                add_rows(source, row, 1)
-                return 0
-
-            lax.fori_loop(0, payload, slow, 0)
-
+        for first in range(0, payload, BATCH):
+            add_rows(source, first)
         return 0
 
     for at in range(4):
@@ -394,63 +411,86 @@
         loads[2 * at + 1].wait()
         lax.fori_loop(at * quarter, (at + 1) * quarter, one_source, 0)
 
-    def fold(total):
-        flipped = total.T
-        return (flipped[0:32] + flipped[32:64]) + (flipped[64:96] + flipped[96:128])
-
-    upper_base = rows_dev * width
-    lane = lane_ids((part.shape[1], LANE))
-
-    def pack(i, own_near, own_far, ghost):
-        tile, place = i // 16, i % 16
-        mine = lane // 8 == place
-        ends = pltpu.roll(jnp.where(lane == 0, ghost, own_far), 8 * place + 4, 1)
-        cols_right[tile] = jnp.where(mine, ends, cols_right[tile])
-        cols_left[tile] = jnp.where(mine, pltpu.roll(own_near, 8 * place, 1), cols_left[tile])
-
-    cols_right[...] = jnp.zeros_like(cols_right)
-    cols_left[...] = jnp.zeros_like(cols_left)
-    tiles = width // LANE
-
-    def one_row(i, _):
-        done = []
+    def late(source, _):
+        def one_slot(k, _):
+            row = ids[source, 0, slots + k]
+
+            @pl.when(row > 0)
+            def _():
+                new = data[source, pl.ds(k // 4, 1), :]
+                acc[pl.ds(row, 1), :] += jnp.where(lane // 32 == k % 4, new, 0.0)
+
+            return 0
+
+        @pl.when(ids[source, 0, slots] > 0)
+        def _():
+            lax.fori_loop(1, slots, one_slot, 0)
+
+        return 0
+
+    def late_group(group, _):
+        found = sum(ids[group * 8 + k, 0, slots] for k in range(8))
+
+        @pl.when(found > 0)
+        def _():
+            lax.fori_loop(group * 8, group * 8 + 8, late, 0)
+
+        return 0
+
+    lax.fori_loop(0, ranks // 8, late_group, 0)
+
+    tiles = cols_dev // LANE
+    for at in range(HALO):
         for tile in range(tiles):
             span = slice(tile * LANE, (tile + 1) * LANE)
-            base = pl.multiple_of(i * width + tile * LANE + FRONT, 8)
-            lower = acc[pl.ds(base, LANE), :]
-            upper = acc[pl.ds(pl.multiple_of(base + upper_base, 8), LANE), :]
-            shared = upper + acc[pl.ds(base - 1, LANE), :]
-            summed = lower + shared + carry[span, :]
-            carry[span, :] = shared + acc[pl.ds(base + upper_base - 1, LANE), :]
-            folded = fold(summed)
-            part[i, :, span] = folded
-            done.append(folded)
-        pack(i, done[0], done[-2], done[-1])
+            rim_low[at, :, span] = node_tile(acc, rows_dev, cols_dev, at, tile, True, at > 0)
+    for at in range(HALO + 1):
+        i = rows_dev - HALO + at
+        for tile in range(tiles):
+            span = slice(tile * LANE, (tile + 1) * LANE)
+            rim_high[at, :, span] = node_tile(acc, rows_dev, cols_dev, i, tile, i < rows_dev)
+
+    row8 = lax.broadcasted_iota(jnp.int32, (8, LANE), 0)
+
+    def rim_columns(i, cells, below):
+        into = pl.ds(pl.multiple_of(i * 8, 8), 8)
+        here, left = node_parts(acc, rows_dev, cols_dev, i, cols_dev - HALO, 8, cells, below)
+        flat_right[into, :] = jnp.where(row8 < HALO, here, 0.0) + jnp.where(
+            row8 < HALO + 1, left, 0.0
+        )
+        here, left = node_parts(acc, rows_dev, cols_dev, i, 0, 8, cells, below)
+        flat_left[into, :] = jnp.where(
+            row8 < HALO, here + jnp.where(row8 > 0, left, 0.0), 0.0
+        )
+
+    def inner_columns(i, _):
+        rim_columns(i, True, True)
         return 0
 
-    lax.fori_loop(0, rows_dev, one_row, 0)
-    done = [fold(carry[tile * LANE : (tile + 1) * LANE, :]) for tile in range(tiles)]
-    for tile in range(tiles):
-        part[rows_dev, :, tile * LANE : (tile + 1) * LANE] = done[tile]
-    pack(rows_dev, done[0], done[-2], done[-1])
+    rim_columns(jnp.int32(0), True, False)
+    lax.fori_loop(1, rows_dev, inner_columns, 0)
+    rim_columns(jnp.int32(rows_dev), False, True)
+    for tile in range(cols_right.shape[0]):
+        span = slice(tile * LANE, (tile + 1) * LANE)
+        cols_right[tile] = fold(flat_right[span, :])
+        cols_left[tile] = fold(flat_left[span, :])
 
 
 def scatter(ids, data, acc, rows_dev, cols_dev):
     channels = LANE // 4
-    width = cols_dev + LANE
+    tiles = rows_dev // 16 + 1
+    shapes = [(HALO + 1, channels, cols_dev), (HALO, channels, cols_dev)]
+    shapes += [(tiles, channels, LANE)] * 2
     return pl.pallas_call(
         functools.partial(scatter_kernel, rows_dev, cols_dev),
-        out_shape=(
-            jax.ShapeDtypeStruct((rows_dev + 1, channels, width), jnp.float32),
-            jax.ShapeDtypeStruct((rows_dev // 16 + 1, channels, LANE), jnp.float32),
-            jax.ShapeDtypeStruct((rows_dev // 16 + 1, channels, LANE), jnp.float32),
-            pltpu.VMEM(acc.shape, jnp.float32),
-        ),
+        out_shape=tuple(jax.ShapeDtypeStruct(shape, jnp.float32) for shape in shapes)
+        + (pltpu.VMEM(acc.shape, jnp.float32),),
         in_specs=[HBM, HBM, VMEM],
-        out_specs=(VMEM, VMEM, VMEM, VMEM),
-        input_output_aliases={2: 3},
+        out_specs=(VMEM,) * 5,
+        input_output_aliases={2: 4},
         scratch_shapes=[
-            pltpu.VMEM((width, LANE), jnp.float32),
+            pltpu.VMEM((tiles * LANE, LANE), jnp.float32),
+            pltpu.VMEM((tiles * LANE, LANE), jnp.float32),
             pltpu.VMEM(data.shape, jnp.float32),
             pltpu.SMEM(ids.shape, jnp.int32),
             pltpu.SemaphoreType.DMA((4,)),
@@ -458,7 +498,7 @@
         ],
         compiler_params=pltpu.CompilerParams(vmem_limit_bytes=24 * MIB),
         name="scatter",
-    )(ids, data, acc)[:3]
+    )(ids, data, acc)
 
 
 def first_piola(stretch_x, stretch_y, fields):
@@ -490,16 +530,16 @@
 
 
 def sheet_kernel(n_rows, n_cols, *refs):
-    part_in, cols_right, cols_left, area_in, thick_in, shift_in = refs[:6]
-    s_in = refs[6:14]
-    total, speed = refs[14:16]
-    p_halo, s_halo, refs = refs[16:24], refs[24:32], refs[32:]
-    part, resid, dir_a, dir_b, dir_c, field, mem, mass, coef = refs[:9]
-    load_sem, send_sem, recv_sem = refs[9:]
-    p_dn, p_up, p_l, p_r, p_dl, p_dr, p_ul, p_ur = p_halo
+    acc, rim_high, rim_low, cols_right, cols_left, area_in, thick_in, shift_in = refs[:8]
+    s_in = refs[8:16]
+    total, speed = refs[16:18]
+    p_halo, s_halo, refs = refs[18:28], refs[28:36], refs[36:]
+    resid, first_sum, field, mem, mass, coef, p_own = refs[:7]
+    load_sem, send_sem, recv_sem = refs[7:]
+    p_dn, p_up, p_l, p_r, p_dl, p_dr, p_ul, p_ur, p_d, p_u = p_halo
     s_dn, s_up, s_l, s_r, s_dl, s_dr, s_ul, s_ur = s_halo
     rows_dev, cols_dev = area_in.shape[1:]
-    channels, width = part.shape[1:]
+    channels, width = resid.shape[1:]
     tall = rows_dev + 16
     middle, main = pl.ds(8, rows_dev), pl.ds(0, cols_dev)
 
@@ -514,7 +554,11 @@
         (thick_in, field.at[pl.ds(2, 2), middle, main]),
         (shift_in, field.at[pl.ds(4, 3), middle, main]),
     ] + list(zip(s_in, s_halo))
-    loads.append((part_in, part))
+    loads += [
+        (cols_right, p_own),
+        (rim_low, resid.at[pl.ds(HALO, HALO), :, main]),
+        (rim_high, resid.at[pl.ds(rows_dev, HALO + 1), :, main]),
+    ]
     loads = [
         pltpu.make_async_copy(source, target, load_sem.at[at])
         for at, (source, target) in enumerate(loads)
@@ -522,19 +566,20 @@
     for load in loads:
         load.start()
 
-    high, low = pl.ds(part_in.shape[0] - HALO - 1, HALO + 1), pl.ds(0, HALO)
     tiles_high, tiles_low = pl.ds((rows_dev - 1) // 16, 2), pl.ds(0, 1)
     pl.semaphore_wait(barrier, 8)
     copies = to_neighbours(
         [
-            part_in.at[high],
-            part_in.at[low],
+            rim_high,
+            rim_low,
             cols_right,
             cols_left,
             cols_right.at[tiles_high],
             cols_left.at[tiles_high],
             cols_right.at[tiles_low],
             cols_left.at[tiles_low],
+            cols_right.at[tiles_high],
+            cols_right.at[tiles_low],
         ],
         p_halo,
         send_sem,
@@ -543,7 +588,15 @@
     for copy in copies[2:] + copies[:2]:
         copy.start()
 
-    for load in loads[:-1]:
+    def inner_fold(i, _):
+        for tile in range(cols_dev // LANE):
+            span = slice(tile * LANE, (tile + 1) * LANE)
+            resid[i + HALO, :, span] = node_tile(acc, rows_dev, cols_dev, i, tile)
+        return 0
+
+    lax.fori_loop(HALO, rows_dev - HALO, inner_fold, 0)
+
+    for load in loads:
         load.wait()
     sides = []
     for left, right, size in ((s_l, s_r, rows_dev), (s_dl, s_dr, 8), (s_ul, s_ur, 8)):
@@ -623,42 +676,46 @@
     ratio_eig = centre / half_width
     edge = lane_ids((channels, LANE))
 
-    def widen(inner, left, right, place):
+    def widen(inner, ends, left, right, place):
+        ends = pltpu.roll(ends, lax.rem(2 * LANE - 4 - 8 * place, LANE), 1)
         left = pltpu.roll(left, lax.rem(2 * LANE - 4 - 8 * place, LANE), 1)
         right = pltpu.roll(right, lax.rem(LANE - 8 * place, LANE), 1)
         first = inner[:, 0:LANE] + jnp.where(edge == 0, left, 0.0)
-        last = inner[:, cols_dev:width] + jnp.where(
-            edge >= LANE - HALO, left, jnp.where(edge < HALO, right, 0.0)
+        last = jnp.where(
+            edge >= LANE - HALO,
+            left,
+            jnp.where(edge < HALO, right + jnp.where(edge == 0, ends, 0.0), 0.0),
         )
-        return jnp.concatenate([first, inner[:, LANE:cols_dev], last], axis=1)
+        return jnp.concatenate([first, inner[:, LANE:], last], axis=1)
 
     def begin(e, rhs):
         scaled = rhs * coef[0, pl.ds(e + 4, 1), :]
         resid[e] = scaled
-        dir_a[e] = scaled * (1.0 / centre)
+        first_sum[e] = scaled * (1.0 / centre)
 
     def own(i):
         i = jnp.int32(i)
-        return widen(part[i], p_l[i // 16], p_r[i // 16], i % 16)
+        tile = i // 16
+        return widen(resid[i + HALO, :, 0:cols_dev], p_own[tile], p_l[tile], p_r[tile], i % 16)
 
     def under(k):
         i = rows_dev - HALO + k
         tile = i // 16 - (rows_dev - 1) // 16
-        return widen(p_dn[k], p_dl[tile], p_dr[tile], jnp.int32(i % 16))
+        return widen(p_dn[k], p_d[tile], p_dl[tile], p_dr[tile], jnp.int32(i % 16))
 
     def over(k):
-        return widen(p_up[k], p_ul[0], p_ur[0], jnp.int32(k))
+        return widen(p_up[k], p_u[0], p_ul[0], p_ur[0], jnp.int32(k))
 
     rhos = [1.0 / ratio_eig]
     for _ in range(ITERS):
         rhos.append(1.0 / (2.0 * ratio_eig - rhos[-1]))
-    directions = [dir_a, dir_b, dir_c]
+    iterates = [first_sum, total]
 
     def sweep_row(sweep, e):
         keep = rhos[sweep + 1] * rhos[sweep]
         gain = 2.0 * rhos[sweep + 1] / half_width
         final = sweep == ITERS - 1
-        source = directions[sweep]
+        source, other = iterates[sweep % 2], iterates[(sweep + 1) % 2]
         k = [coef[c, pl.ds(e + 4, 1), :] for c in range(1, 7)]
         through = None
         for group in range(0, channels, 8):
@@ -667,20 +724,15 @@
             to_left = k[2] * here + k[3] * up
             to_right = k[4] * here + k[5] * down
             left = resid[e, at, :] - (
-                here
-                + k[0] * up
-                + k[1] * down
-                + pltpu.roll(to_left, width - 1, 1)
-                + pltpu.roll(to_right, 1, 1)
+                (k[0] * up + k[1] * down)
+                + (pltpu.roll(to_left, width - 1, 1) + pltpu.roll(to_right, 1, 1))
             )
-            new = keep * here + gain * left
+            new = (1.0 + keep - gain) * here + gain * left
+            if sweep > 0:
+                new = new - keep * other[e, at, :]
+            other[e, at, :] = new
             if final:
-                summed = (dir_a[e, at, :] + dir_b[e, at, :]) + (here + new)
-                total[e, at, :] = summed
-                through = summed if through is None else through + summed
-            else:
-                resid[e, at, :] = left
-                directions[sweep + 1][e, at, :] = new
+                through = new if through is None else through + new
         if final:
             through = through * (1.0 / POINTS)
             for at, value in enumerate((0, 1, 5, 7)):
@@ -688,7 +740,6 @@
 
     for copy in copies[2:]:
         copy.wait()
-    loads[-1].wait()
 
     def inner_row(i, _):
         begin(i + HALO, own(i))
@@ -759,48 +810,46 @@
         speed[c] = speed_up + GRAVITY if c == 2 else speed_up
 
 
-def sheet(part, cols_right, cols_left, fields, halo, n_rows, n_cols):
-    channels, width = part.shape[1:]
+def sheet(acc, rims, fields, halo, n_rows, n_cols):
     rows_dev, cols_dev = fields[0].shape[1:]
+    width = cols_dev + LANE
     tall, long = rows_dev + 16, rows_dev + 2 * HALO
-    tiles = cols_right.shape[0]
+    tiles, channels, _ = rims[2].shape
 
     def scratch(*shape):
         return pltpu.VMEM(shape, jnp.float32)
 
     block = scratch(long, channels, width)
-    part_halo = [(HALO + 1, channels, width), (HALO, channels, width)]
-    part_halo += [(tiles, channels, LANE)] * 2 + [(2, channels, LANE)] * 2
-    part_halo += [(1, channels, LANE)] * 2
+    part_halo = [rims[0].shape, rims[1].shape, rims[2].shape, rims[3].shape]
+    part_halo += [(2, channels, LANE)] * 2 + [(1, channels, LANE)] * 2
+    part_halo += [(2, channels, LANE), (1, channels, LANE)]
     return pl.pallas_call(
         functools.partial(sheet_kernel, n_rows, n_cols),
         out_shape=(
             block,
             scratch(3, rows_dev, cols_dev),
         ),
-        in_specs=[HBM] * 14,
+        in_specs=[VMEM] + [HBM] * 15,
         out_specs=(VMEM, VMEM),
         scratch_shapes=[scratch(*shape) for shape in part_halo]
         + [scratch(*x.shape) for x in halo]
         + [
-            scratch(*part.shape),
-            block,
-            block,
             block,
             block,
             scratch(7, tall, width),
             scratch(4, tall, width),
             scratch(tall, width),
             scratch(7, tall, width),
-            pltpu.SemaphoreType.DMA((12,)),
-            pltpu.SemaphoreType.DMA((8,)),
-            pltpu.SemaphoreType.DMA((8,)),
+            scratch(tiles, channels, LANE),
+            pltpu.SemaphoreType.DMA((14,)),
+            pltpu.SemaphoreType.DMA((10,)),
+            pltpu.SemaphoreType.DMA((10,)),
         ],
         compiler_params=pltpu.CompilerParams(
-            vmem_limit_bytes=54 * MIB, collective_id=2, has_side_effects=True
+            vmem_limit_bytes=24 * MIB, collective_id=2, has_side_effects=True
         ),
         name="sheet",
-    )(part, cols_right, cols_left, *fields, *halo)
+    )(acc, *rims, *fields, *halo)
 
 
 def finish_kernel(total, speed_up, velocity, out, vel_out):
@@ -855,11 +904,10 @@
         thickness,
         displacement,
     )
-    part, cols_right, cols_left = scatter(ids, arrived, acc, rows_dev, cols_dev)
+    *rims, acc = scatter(ids, arrived, acc, rows_dev, cols_dev)
     fields = (cell_area, thickness, displacement)
-    total, speed_up = sheet(
-        part, cols_right, cols_left, fields, halo, n_new * rows_dev, n_old * cols_dev
-    )
+    acc = pltpu.with_memory_space_constraint(acc, pltpu.VMEM)
+    total, speed_up = sheet(acc, rims, fields, halo, n_new * rows_dev, n_old * cols_dev)
     return finish(total, speed_up, velocity)
 
 

time: 117 us -> 106 us (0.906)
  Pallas kernels: 116 us -> 105 us
    pallas_call x1, Pallas kernels: 38.5 us -> 25.7 us  [scatter(): pl.pallas_call(functools.partial(scatter_kernel, rows_dev, cols_dev), out...]
    pallas_call x1, Pallas kernels: 32.2 us -> 34.3 us  [sheet(): pl.pallas_call(functools.partial(sheet_kernel, n_rows, n_cols), out_shape...]
where the time goes in v6:
time: 106 us
  Pallas kernels  105 us (99%)
    pallas_call x1, Pallas kernels, send(): pl.pallas_call(functools.partial(send_kernel, rows_dev, cols_dev), out_sh...  42.6 us
    pallas_call x1, Pallas kernels, sheet(): pl.pallas_call(functools.partial(sheet_kernel, n_rows, n_cols), out_shape...  34.3 us
    pallas_call x1, Pallas kernels, scatter(): pl.pallas_call(functools.partial(scatter_kernel, rows_dev, cols_dev), out...  25.7 us
    pallas_call x1, Pallas kernels, finish(): pl.pallas_call(finish_kernel, grid=(rows_dev // 8,), out_shape=(jax.Shape...  2.89 us

profile of v6, /device:TPU:1, one launch (start us, length us, event | category | flops | bytes accessed | tf_op | source)
XLA Modules:
  0.0 106.1 jit_solution(2583303957924737520)
XLA Ops:
  0.6 42.6 %send.1 = (f32[128,32,128]{2,1,0:T(8,128)}, s32[128,1,256]{2,1,0:T(1,128)}, f32[16,1024]{1,0:T(8,128)}, f32[16,1024]{1,0:T(8,128)}, f32[32,128]{1,0:T(8,128)}, /...) custom-call(s32[1,128]{1,0:T(1,128)} %counts.1, ...), custom_call_target="tpu_custom_call" | custom-call | tf_op jit(solution)/shard_map/send/pallas_call | solution.py:299
  43.2 25.7 %scatter.1 = (f32[5,32,1024]{2,1,0:T(8,128)}, f32[4,32,1024]{2,1,0:T(8,128)}, f32[3,32,128]{2,1,0:T(8,128)}, f32[3,32,128]{2,1,0:T(8,128)}, f32[65552,128]{1,0:T(8,128)S(1)}) custom-call(s32[128,1,256]{2,1,0:T(1,128)} %get-tuple-element.20.ids_in, f32[128,32,128]{2,1,0:T(8,128)} %get-tuple-element.21.data_in, ...), custom_call_target="tpu_custom_call", output_to_operand_aliasing={{4}: (2, {})} | custom-call | tf_op jit(solution)/shard_map/scatter/pallas_call | solution.py:484
  68.9 0.0 copy-start
  68.9 34.3 %sheet.1 = (f32[40,32,1152]{2,1,0:T(8,128)S(1)}, f32[3,32,1024]{2,1,0:T(8,128)S(1)}) custom-call(f32[65552,128]{1,0:T(8,128)S(1)} %get-tuple-element.23.refs_0_, f32[5,32,1024]{2,1,0:T(8,128)} %get-tuple-element.24.refs_1_, f32[4,32,1024]{2,1,0:T(8,128)} %get-tuple-element.25.refs_2_, f32[3,32,128]{2,1,0:T(8,128)} %get-tuple-element.26.refs_3_, ...), custom_call_target="tpu_custom_call" | custom-call | tf_op jit(solution)/shard_map/sheet/pallas_call | solution.py:826
  103.2 0.0 copy-done
  103.2 2.9 %finish.1 = (f32[32,32,1024]{2,1,0:T(8,128)}, f32[3,32,1024]{2,1,0:T(8,128)}) custom-call(f32[40,32,1152]{2,1,0:T(8,128)S(1)} %get-tuple-element.36.total, f32[3,32,1024]{2,1,0:T(8,128)S(1)} %get-tuple-element.37.speed_up, f32[3,32,1024]{2,1,0:T(8,128)S(1)} %copy-done), custom_call_target="tpu_custom_call" | custom-call | tf_op jit(solution)/shard_map/finish/pallas_call | solution.py:870
Async XLA Ops:
  68.9 34.3 %copy-start = (f32[3,32,1024]{2,1,0:T(8,128)S(1)}, f32[3,32,1024]{2,1,0:T(8,128)}, u32[]{:S(2)}) copy-start(f32[3,32,1024]{2,1,0:T(8,128)} %velocity.1) | copy-start | bytes 1179652

commit v7 on v6

--- a/solution.py
+++ b/solution.py
@@ -23,12 +23,26 @@
 BATCH = 4
 HALO = 4
 STRIDE = 37
+UNROLL = 4
 MESH = pl.DeviceIdType.MESH
 MIB = 1024 * 1024
 
 VMEM = pl.BlockSpec(memory_space=pltpu.VMEM)
 SMEM = pl.BlockSpec(memory_space=pltpu.SMEM)
 HBM = pl.BlockSpec(memory_space=pltpu.HBM)
+
+
+def rows_loop(start, stop, one_row, unroll=UNROLL):
+    steps = (stop - start) // unroll
+
+    def some(step, _):
+        for k in range(unroll):
+            one_row(start + step * unroll + k)
+        return 0
+
+    lax.fori_loop(0, steps, some, 0)
+    for i in range(start + steps * unroll, stop):
+        one_row(jnp.int32(i))
 
 
 def lane_ids(shape):
@@ -422,9 +436,18 @@
 
             return 0
 
+        def eight_slots(some, _):
+            noted = sum(ids[source, 0, slots + some * 8 + k] for k in range(8))
+
+            @pl.when(noted > 0)
+            def _():
+                lax.fori_loop(jnp.maximum(some * 8, 1), some * 8 + 8, one_slot, 0)
+
+            return 0
+
         @pl.when(ids[source, 0, slots] > 0)
         def _():
-            lax.fori_loop(1, slots, one_slot, 0)
+            lax.fori_loop(0, slots // 8, eight_slots, 0)
 
         return 0
 
@@ -588,13 +611,12 @@
     for copy in copies[2:] + copies[:2]:
         copy.start()
 
-    def inner_fold(i, _):
+    def inner_fold(i):
         for tile in range(cols_dev // LANE):
             span = slice(tile * LANE, (tile + 1) * LANE)
             resid[i + HALO, :, span] = node_tile(acc, rows_dev, cols_dev, i, tile)
-        return 0
-
-    lax.fori_loop(HALO, rows_dev - HALO, inner_fold, 0)
+
+    rows_loop(HALO, rows_dev - HALO, inner_fold, 2)
 
     for load in loads:
         load.wait()
@@ -710,49 +732,59 @@
     for _ in range(ITERS):
         rhos.append(1.0 / (2.0 * ratio_eig - rhos[-1]))
     iterates = [first_sum, total]
+    lane8 = lane_ids((8, LANE))
+    first_lane, last_lane = lane8 == 0, lane8 == LANE - 1
 
     def sweep_row(sweep, e):
         keep = rhos[sweep + 1] * rhos[sweep]
         gain = 2.0 * rhos[sweep + 1] / half_width
         final = sweep == ITERS - 1
         source, other = iterates[sweep % 2], iterates[(sweep + 1) % 2]
-        k = [coef[c, pl.ds(e + 4, 1), :] for c in range(1, 7)]
-        through = None
-        for group in range(0, channels, 8):
-            at = slice(group, group + 8)
-            here, up, down = source[e, at, :], source[e + 1, at, :], source[e - 1, at, :]
-            to_left = k[2] * here + k[3] * up
-            to_right = k[4] * here + k[5] * down
-            left = resid[e, at, :] - (
-                (k[0] * up + k[1] * down)
-                + (pltpu.roll(to_left, width - 1, 1) + pltpu.roll(to_right, 1, 1))
-            )
-            new = (1.0 + keep - gain) * here + gain * left
-            if sweep > 0:
-                new = new - keep * other[e, at, :]
-            other[e, at, :] = new
-            if final:
-                through = new if through is None else through + new
+        k_row = [coef[c, pl.ds(e + 4, 1), :] for c in range(1, 7)]
+        tiles, groups = width // LANE, range(channels // 8)
+        rest = [[None] * tiles for _ in groups]
+        west = [[None] * tiles for _ in groups]
+        east = [[None] * tiles for _ in groups]
+        sums = [None] * tiles
+
+        def close(t):
+            span = slice(t * LANE, (t + 1) * LANE)
+            for g in groups:
+                from_east = jnp.where(last_lane, east[g][(t + 1) % tiles], east[g][t])
+                from_west = jnp.where(first_lane, west[g][t - 1], west[g][t])
+                new = rest[g][t] - gain * (from_east + from_west)
+                other[e, 8 * g : 8 * g + 8, span] = new
+                if final:
+                    sums[t] = new if g == 0 else sums[t] + new
+
+        for t in range(tiles):
+            span = slice(t * LANE, (t + 1) * LANE)
+            k = [jnp.broadcast_to(x[:, span], (8, LANE)) for x in k_row]
+            for g in groups:
+                at = slice(8 * g, 8 * g + 8)
+                here, up, down = source[e, at, span], source[e + 1, at, span], source[e - 1, at, span]
+                east[g][t] = pltpu.roll(k[2] * here + k[3] * up, LANE - 1, 1)
+                west[g][t] = pltpu.roll(k[4] * here + k[5] * down, 1, 1)
+                kept = (1.0 + keep - gain) * here
+                kept = kept + gain * (resid[e, at, span] - (k[0] * up + k[1] * down))
+                rest[g][t] = kept if sweep == 0 else kept - keep * other[e, at, span]
+            if t > 1:
+                close(t - 1)
+        close(tiles - 1)
+        close(0)
         if final:
-            through = through * (1.0 / POINTS)
+            through = jnp.concatenate(sums, axis=1) * (1.0 / POINTS)
             for at, value in enumerate((0, 1, 5, 7)):
                 mem[at, pl.ds(e + 4, 1), :] = through[value : value + 1, :]
 
     for copy in copies[2:]:
         copy.wait()
 
-    def inner_row(i, _):
-        begin(i + HALO, own(i))
-        return 0
-
-    lax.fori_loop(1, rows_dev, inner_row, 0)
+    rows_loop(1, rows_dev, lambda i: begin(i + HALO, own(i)))
     for sweep in range(ITERS):
-
-        def inner_sweep(e, _, sweep=sweep):
-            sweep_row(sweep, e)
-            return 0
-
-        lax.fori_loop(HALO + 2 + sweep, rows_dev + HALO - 1 - sweep, inner_sweep, 0)
+        rows_loop(
+            HALO + 2 + sweep, rows_dev + HALO - 1 - sweep, functools.partial(sweep_row, sweep)
+        )
 
     for copy in copies[:2]:
         copy.wait()
@@ -763,15 +795,14 @@
     for e in range(1, HALO):
         begin(rows_dev + HALO + e, over(e))
     for sweep in range(ITERS):
-        def outer_sweep(k, _, sweep=sweep):
+        def outer_row(k, sweep=sweep):
             low_end = HALO + 1
             sweep_row(
                 sweep,
                 jnp.where(k < low_end, 1 + sweep + k, rows_dev + HALO - 1 - sweep + k - low_end),
             )
-            return 0
-
-        lax.fori_loop(0, 2 * HALO + 1, outer_sweep, 0)
+
+        rows_loop(0, 2 * HALO + 1, outer_row, 3)
 
     anchor = [field[4 + c] for c in range(3)]
     beside = [from_right(x) for x in anchor]

time: 106 us -> 100 us (0.943)
  Pallas kernels: 105 us -> 99.3 us
    pallas_call x1, Pallas kernels: 34.3 us -> 28.2 us  [sheet(): pl.pallas_call(functools.partial(sheet_kernel, n_rows, n_cols), out_shape...]
where the time goes in v7:
time: 100 us
  Pallas kernels  99.3 us (99%)
    pallas_call x1, Pallas kernels, send(): pl.pallas_call(functools.partial(send_kernel, rows_dev, cols_dev), out_sh...  42.6 us
    pallas_call x1, Pallas kernels, sheet(): pl.pallas_call(functools.partial(sheet_kernel, n_rows, n_cols), out_shape...  28.2 us
    pallas_call x1, Pallas kernels, scatter(): pl.pallas_call(functools.partial(scatter_kernel, rows_dev, cols_dev), out...  25.7 us
    pallas_call x1, Pallas kernels, finish(): pl.pallas_call(finish_kernel, grid=(rows_dev // 8,), out_shape=(jax.Shape...  2.89 us

profile of v7, /device:TPU:1, one launch (start us, length us, event | category | flops | bytes accessed | tf_op | source)
XLA Modules:
  0.0 100.0 jit_solution(14171508181101127307)
XLA Ops:
  0.6 42.6 %send.1 = (f32[128,32,128]{2,1,0:T(8,128)}, s32[128,1,256]{2,1,0:T(1,128)}, f32[16,1024]{1,0:T(8,128)}, f32[16,1024]{1,0:T(8,128)}, f32[32,128]{1,0:T(8,128)}, /...) custom-call(s32[1,128]{1,0:T(1,128)} %counts.1, ...), custom_call_target="tpu_custom_call" | custom-call | tf_op jit(solution)/shard_map/send/pallas_call | solution.py:313
  43.2 25.7 %scatter.1 = (f32[5,32,1024]{2,1,0:T(8,128)}, f32[4,32,1024]{2,1,0:T(8,128)}, f32[3,32,128]{2,1,0:T(8,128)}, f32[3,32,128]{2,1,0:T(8,128)}, f32[65552,128]{1,0:T(8,128)S(1)}) custom-call(s32[128,1,256]{2,1,0:T(1,128)} %get-tuple-element.20.ids_in, f32[128,32,128]{2,1,0:T(8,128)} %get-tuple-element.21.data_in, ...), custom_call_target="tpu_custom_call", output_to_operand_aliasing={{4}: (2, {})} | custom-call | tf_op jit(solution)/shard_map/scatter/pallas_call | solution.py:507
  68.9 0.0 copy-start
  68.9 28.2 %sheet.1 = (f32[40,32,1152]{2,1,0:T(8,128)S(1)}, f32[3,32,1024]{2,1,0:T(8,128)S(1)}) custom-call(f32[65552,128]{1,0:T(8,128)S(1)} %get-tuple-element.23.refs_0_, f32[5,32,1024]{2,1,0:T(8,128)} %get-tuple-element.24.refs_1_, f32[4,32,1024]{2,1,0:T(8,128)} %get-tuple-element.25.refs_2_, f32[3,32,128]{2,1,0:T(8,128)} %get-tuple-element.26.refs_3_, ...), custom_call_target="tpu_custom_call" | custom-call | tf_op jit(solution)/shard_map/sheet/pallas_call | solution.py:857
  97.1 0.0 copy-done
  97.1 2.9 %finish.1 = (f32[32,32,1024]{2,1,0:T(8,128)}, f32[3,32,1024]{2,1,0:T(8,128)}) custom-call(f32[40,32,1152]{2,1,0:T(8,128)S(1)} %get-tuple-element.36.total, f32[3,32,1024]{2,1,0:T(8,128)S(1)} %get-tuple-element.37.speed_up, f32[3,32,1024]{2,1,0:T(8,128)S(1)} %copy-done), custom_call_target="tpu_custom_call" | custom-call | tf_op jit(solution)/shard_map/finish/pallas_call | solution.py:901
Async XLA Ops:
  68.9 28.2 %copy-start = (f32[3,32,1024]{2,1,0:T(8,128)S(1)}, f32[3,32,1024]{2,1,0:T(8,128)}, u32[]{:S(2)}) copy-start(f32[3,32,1024]{2,1,0:T(8,128)} %velocity.1) | copy-start | bytes 1179652

commit v8 on v7

--- a/solution.py
+++ b/solution.py
@@ -47,6 +47,88 @@
 
 def lane_ids(shape):
     return lax.broadcasted_iota(jnp.int32, shape, len(shape) - 1)
+
+
+def shifters(tall, width):
+    def from_left(x):
+        return pltpu.roll(x, 1, 1)
+
+    def from_right(x):
+        return pltpu.roll(x, width - 1, 1)
+
+    def from_below(x):
+        return pltpu.roll(x, 1, 0)
+
+    def from_above(x):
+        return pltpu.roll(x, tall - 1, 0)
+
+    return from_left, from_right, from_below, from_above
+
+
+def cell_planes(n_rows, n_cols, field, coef, mass, s_halo):
+    s_dn, s_up, s_l, s_r, s_dl, s_dr, s_ul, s_ur = s_halo
+    tall, width = mass.shape
+    rows_dev, cols_dev = tall - 16, width - LANE
+    sides = []
+    for left, right, size in ((s_l, s_r, rows_dev), (s_dl, s_dr, 8), (s_ul, s_ur, 8)):
+        sides.append((left[...], right[...], lane_ids((size, LANE))))
+    for f in range(7):
+        if f < 2:
+            field[f, 3:8, 0:cols_dev] = s_dn[5 * f : 5 * f + 5, :]
+            field[f, 8 + rows_dev : 12 + rows_dev, 0:cols_dev] = s_up[4 * f : 4 * f + 4, :]
+        else:
+            field[f, 7:8, 0:cols_dev] = s_dn[8 + f : 9 + f, :]
+            if f >= 4:
+                field[f, 8 + rows_dev : 9 + rows_dev, 0:cols_dev] = s_up[4 + f : 5 + f, :]
+        wide, narrow = (5, 4) if f < 2 else (1, 0 if f < 4 else 1)
+        back = 5 if f < 2 else 5
+        made = []
+        for left, right, lane in sides:
+            from_l = pltpu.roll(left, LANE - back - 8 * f, 1)
+            from_r = pltpu.roll(right, (LANE - 8 * f) % LANE, 1)
+            made.append(
+                jnp.where(lane >= LANE - wide, from_l, jnp.where(lane < narrow, from_r, 0.0))
+            )
+        field[f, 8 : 8 + rows_dev, cols_dev:width] = made[0]
+        row8 = lax.broadcasted_iota(jnp.int32, (8, LANE), 0)
+        under = row8 >= 8 - wide
+        over = row8 < narrow
+        field[f, 0:8, cols_dev:width] = jnp.where(under, made[1], 0.0)
+        field[f, 8 + rows_dev : tall, cols_dev:width] = jnp.where(over, made[2], 0.0)
+
+    shape = (tall, width)
+    row = lax.broadcasted_iota(jnp.int32, shape, 0) - 8 + lax.axis_index("new") * rows_dev
+    lane = lax.broadcasted_iota(jnp.int32, shape, 1)
+    col = jnp.where(lane < cols_dev + 64, lane, lane - width) + lax.axis_index("old") * cols_dev
+    valid = (row >= 0) & (row < n_rows - 1) & (col >= 0) & (col < n_cols - 1)
+
+    from_left, from_right, from_below, _ = shifters(tall, width)
+    area_low = jnp.where(valid, field[0], 0.0)
+    area_up = jnp.where(valid, field[1], 0.0)
+    field[2] = field[2] * area_low
+    field[3] = field[3] * area_up
+    lower, upper = area_low / 12.0, area_up / 12.0
+    both = lower + upper
+    lower_left, upper_below = from_left(lower), from_below(upper)
+    weight = both + lower_left + upper_below + from_below(from_left(both))
+    inv = jnp.where(weight > 0.0, 1.0 / (2.0 * weight), 0.0)
+    inv_right = from_right(inv)
+    east, north = lower + upper_below, upper + lower_left
+    coef[0] = inv * (1.0 / 3.0)
+    coef[1] = inv * north
+    coef[2] = inv * from_below(north)
+    coef[3] = from_left(inv * east)
+    coef[4] = from_left(inv * both)
+    coef[5] = inv_right * east
+    coef[6] = inv_right * from_below(both)
+    vol_low, vol_up = field[2], field[3]
+    mass[...] = (
+        vol_low
+        + vol_up
+        + from_left(vol_low)
+        + from_below(vol_up)
+        + from_below(from_left(vol_low + vol_up))
+    ) * (1.0 / 3.0)
 
 
 def neighbours():
@@ -94,6 +176,10 @@
     shift_in,
     arrived,
     arrived_ids,
+    field_out,
+    coef_out,
+    mass_out,
+    acc,
     s_dn,
     s_up,
     s_l,
@@ -102,7 +188,9 @@
     s_dr,
     s_ul,
     s_ur,
-    acc,
+    field,
+    coef,
+    mass,
     table,
     picked,
     ids,
@@ -147,10 +235,15 @@
         loads.append((source.at[:, low, :], rim_low.at[into]))
         loads.append((source.at[:, :, far], rim_right.at[into]))
         loads.append((source.at[:, :, near], rim_left.at[into]))
+        inner = field.at[into, pl.ds(8, rows_dev), pl.ds(0, cols_dev)]
+        loads.append((source, inner))
     loads = [
         pltpu.make_async_copy(source, target, local_sem.at[at])
         for at, (source, target) in enumerate(loads)
     ]
+    tall = rows_dev + 16
+    field[:, 0:8, :] = jnp.zeros((7, 8, cols_dev + LANE), jnp.float32)
+    field[:, 8 + rows_dev : tall, :] = jnp.zeros((7, 8, cols_dev + LANE), jnp.float32)
     for load in loads:
         load.start()
 
@@ -291,6 +384,18 @@
         pltpu.make_async_copy(source.at[me], target.at[me], pair_sem.at[2 * at + 1]).start()
     for copy in halo:
         copy.wait()
+    around = (s_dn, s_up, s_l, s_r, s_dl, s_dr, s_ul, s_ur)
+    cell_planes(n_new * rows_dev, n_old * cols_dev, field, coef, mass, around)
+    saves = [
+        pltpu.make_async_copy(source, target, near_send.at[at])
+        for at, (source, target) in enumerate(
+            ((field.at[pl.ds(2, 5)], field_out), (coef, coef_out), (mass, mass_out))
+        )
+    ]
+    for save in saves:
+        save.start()
+    for save in saves:
+        save.wait()
     for at, (source, target) in enumerate(((picked, arrived), (ids, arrived_ids))):
         rest = pl.ds(0, ranks - 1)
         pltpu.make_async_copy(source.at[rest], source.at[rest], pair_sem.at[2 * at]).wait()
@@ -302,8 +407,9 @@
     payload = slots // 4
     rows_dev, cols_dev = area.shape[1:]
     halo = [(16, cols_dev)] * 2 + [(rows_dev, LANE)] * 2 + [(8, LANE)] * 4
-    shapes = [jax.ShapeDtypeStruct(shape, jnp.float32) for shape in halo]
-    shapes.insert(0, jax.ShapeDtypeStruct((ranks, payload, LANE), jnp.float32))
+    tall, width = rows_dev + 16, cols_dev + LANE
+    shapes = [(ranks, payload, LANE), (5, tall, width), (7, tall, width), (tall, width)]
+    shapes = [jax.ShapeDtypeStruct(shape, jnp.float32) for shape in shapes]
     shapes.insert(1, jax.ShapeDtypeStruct((ranks, 1, 2 * slots), jnp.int32))
     shapes.append(pltpu.VMEM((2 * FRONT + 2 * rows_dev * cols_dev, LANE), jnp.float32))
 
@@ -315,7 +421,11 @@
         out_shape=tuple(shapes),
         in_specs=[VMEM] + [HBM] * 7,
         out_specs=(HBM,) * (len(shapes) - 1) + (VMEM,),
-        scratch_shapes=[
+        scratch_shapes=[scratch(*shape) for shape in halo]
+        + [
+            scratch(7, tall, width),
+            scratch(7, tall, width),
+            scratch(tall, width),
             scratch(values.shape[1], LANE),
             scratch(ranks, payload, LANE),
             pltpu.VMEM((ranks, 1, 2 * slots), jnp.int32),
@@ -334,7 +444,7 @@
             scratch(rows_dev, LANE),
             pltpu.SMEM(rows.shape, jnp.int32),
             pltpu.SMEM((ranks, slots), jnp.float32),
-            pltpu.SemaphoreType.DMA((17,)),
+            pltpu.SemaphoreType.DMA((20,)),
             pltpu.SemaphoreType.DMA((4,)),
             pltpu.SemaphoreType.DMA((8,)),
             pltpu.SemaphoreType.DMA((8,)),
@@ -552,32 +662,27 @@
     return piola_x, piola_y
 
 
-def sheet_kernel(n_rows, n_cols, *refs):
-    acc, rim_high, rim_low, cols_right, cols_left, area_in, thick_in, shift_in = refs[:8]
-    s_in = refs[8:16]
-    total, speed = refs[16:18]
-    p_halo, s_halo, refs = refs[18:28], refs[28:36], refs[36:]
+def sheet_kernel(*refs):
+    acc, rim_high, rim_low, cols_right, cols_left, field_in, coef_in, mass_in = refs[:8]
+    total, speed = refs[8:10]
+    p_halo, refs = refs[10:20], refs[20:]
     resid, first_sum, field, mem, mass, coef, p_own = refs[:7]
     load_sem, send_sem, recv_sem = refs[7:]
     p_dn, p_up, p_l, p_r, p_dl, p_dr, p_ul, p_ur, p_d, p_u = p_halo
-    s_dn, s_up, s_l, s_r, s_dl, s_dr, s_ul, s_ur = s_halo
-    rows_dev, cols_dev = area_in.shape[1:]
     channels, width = resid.shape[1:]
-    tall = rows_dev + 16
-    middle, main = pl.ds(8, rows_dev), pl.ds(0, cols_dev)
+    tall = mass.shape[0]
+    rows_dev, cols_dev = tall - 16, width - LANE
+    main = pl.ds(0, cols_dev)
+    from_left, from_right, from_below, from_above = shifters(tall, width)
 
     barrier = pltpu.get_barrier_semaphore()
     for device in neighbours():
         pl.semaphore_signal(barrier, inc=1, device_id=device, device_id_type=MESH)
 
-    field[:, 0:8, :] = jnp.zeros((7, 8, width), jnp.float32)
-    field[:, 8 + rows_dev : tall, :] = jnp.zeros((7, 8, width), jnp.float32)
     loads = [
-        (area_in, field.at[pl.ds(0, 2), middle, main]),
-        (thick_in, field.at[pl.ds(2, 2), middle, main]),
-        (shift_in, field.at[pl.ds(4, 3), middle, main]),
-    ] + list(zip(s_in, s_halo))
-    loads += [
+        (field_in, field),
+        (coef_in, coef),
+        (mass_in, mass),
         (cols_right, p_own),
         (rim_low, resid.at[pl.ds(HALO, HALO), :, main]),
         (rim_high, resid.at[pl.ds(rows_dev, HALO + 1), :, main]),
@@ -620,77 +725,6 @@
 
     for load in loads:
         load.wait()
-    sides = []
-    for left, right, size in ((s_l, s_r, rows_dev), (s_dl, s_dr, 8), (s_ul, s_ur, 8)):
-        sides.append((left[...], right[...], lane_ids((size, LANE))))
-    for f in range(7):
-        if f < 2:
-            field[f, 3:8, 0:cols_dev] = s_dn[5 * f : 5 * f + 5, :]
-            field[f, 8 + rows_dev : 12 + rows_dev, 0:cols_dev] = s_up[4 * f : 4 * f + 4, :]
-        else:
-            field[f, 7:8, 0:cols_dev] = s_dn[8 + f : 9 + f, :]
-            if f >= 4:
-                field[f, 8 + rows_dev : 9 + rows_dev, 0:cols_dev] = s_up[4 + f : 5 + f, :]
-        wide, narrow = (5, 4) if f < 2 else (1, 0 if f < 4 else 1)
-        back = 5 if f < 2 else 5
-        made = []
-        for left, right, lane in sides:
-            from_l = pltpu.roll(left, LANE - back - 8 * f, 1)
-            from_r = pltpu.roll(right, (LANE - 8 * f) % LANE, 1)
-            made.append(
-                jnp.where(lane >= LANE - wide, from_l, jnp.where(lane < narrow, from_r, 0.0))
-            )
-        field[f, 8 : 8 + rows_dev, cols_dev:width] = made[0]
-        row8 = lax.broadcasted_iota(jnp.int32, (8, LANE), 0)
-        under = row8 >= 8 - wide
-        over = row8 < narrow
-        field[f, 0:8, cols_dev:width] = jnp.where(under, made[1], 0.0)
-        field[f, 8 + rows_dev : tall, cols_dev:width] = jnp.where(over, made[2], 0.0)
-
-    shape = (tall, width)
-    row = lax.broadcasted_iota(jnp.int32, shape, 0) - 8 + lax.axis_index("new") * rows_dev
-    lane = lax.broadcasted_iota(jnp.int32, shape, 1)
-    col = jnp.where(lane < cols_dev + 64, lane, lane - width) + lax.axis_index("old") * cols_dev
-    valid = (row >= 0) & (row < n_rows - 1) & (col >= 0) & (col < n_cols - 1)
-
-    def from_left(x):
-        return pltpu.roll(x, 1, 1)
-
-    def from_right(x):
-        return pltpu.roll(x, width - 1, 1)
-
-    def from_below(x):
-        return pltpu.roll(x, 1, 0)
-
-    def from_above(x):
-        return pltpu.roll(x, tall - 1, 0)
-
-    area_low = jnp.where(valid, field[0], 0.0)
-    area_up = jnp.where(valid, field[1], 0.0)
-    field[2] = field[2] * area_low
-    field[3] = field[3] * area_up
-    lower, upper = area_low / 12.0, area_up / 12.0
-    both = lower + upper
-    lower_left, upper_below = from_left(lower), from_below(upper)
-    weight = both + lower_left + upper_below + from_below(from_left(both))
-    inv = jnp.where(weight > 0.0, 1.0 / (2.0 * weight), 0.0)
-    inv_right = from_right(inv)
-    east, north = lower + upper_below, upper + lower_left
-    coef[0] = inv * (1.0 / 3.0)
-    coef[1] = inv * north
-    coef[2] = inv * from_below(north)
-    coef[3] = from_left(inv * east)
-    coef[4] = from_left(inv * both)
-    coef[5] = inv_right * east
-    coef[6] = inv_right * from_below(both)
-    vol_low, vol_up = field[2], field[3]
-    mass[...] = (
-        vol_low
-        + vol_up
-        + from_left(vol_low)
-        + from_below(vol_up)
-        + from_below(from_left(vol_low + vol_up))
-    ) * (1.0 / 3.0)
     mem[...] = jnp.zeros_like(mem)
 
     centre = 0.5 * (EIG_HIGH + EIG_LOW)
@@ -804,7 +838,7 @@
 
         rows_loop(0, 2 * HALO + 1, outer_row, 3)
 
-    anchor = [field[4 + c] for c in range(3)]
+    anchor = [field[2 + c] for c in range(3)]
     beside = [from_right(x) for x in anchor]
     upward = [from_above(x) for x in anchor]
     across = [from_above(x) for x in beside]
@@ -823,7 +857,7 @@
     low_y[1], up_y[1] = 1.0 + low_y[1], 1.0 + up_y[1]
     piola_lx, piola_ly = first_piola(low_x, low_y, m_low)
     piola_ux, piola_uy = first_piola(up_x, up_y, m_up)
-    vol_low, vol_up = field[2], field[3]
+    vol_low, vol_up = field[0], field[1]
     node_mass = mass[8 : 8 + rows_dev, 0:cols_dev]
     for c in range(3):
         f_beside = -vol_low * (piola_lx[c] - piola_ly[c])
@@ -841,10 +875,10 @@
         speed[c] = speed_up + GRAVITY if c == 2 else speed_up
 
 
-def sheet(acc, rims, fields, halo, n_rows, n_cols):
-    rows_dev, cols_dev = fields[0].shape[1:]
-    width = cols_dev + LANE
-    tall, long = rows_dev + 16, rows_dev + 2 * HALO
+def sheet(acc, rims, planes):
+    tall, width = planes[2].shape
+    rows_dev, cols_dev = tall - 16, width - LANE
+    long = rows_dev + 2 * HALO
     tiles, channels, _ = rims[2].shape
 
     def scratch(*shape):
@@ -855,24 +889,23 @@
     part_halo += [(2, channels, LANE)] * 2 + [(1, channels, LANE)] * 2
     part_halo += [(2, channels, LANE), (1, channels, LANE)]
     return pl.pallas_call(
-        functools.partial(sheet_kernel, n_rows, n_cols),
+        sheet_kernel,
         out_shape=(
             block,
             scratch(3, rows_dev, cols_dev),
         ),
-        in_specs=[VMEM] + [HBM] * 15,
+        in_specs=[VMEM] + [HBM] * 7,
         out_specs=(VMEM, VMEM),
         scratch_shapes=[scratch(*shape) for shape in part_halo]
-        + [scratch(*x.shape) for x in halo]
         + [
             block,
             block,
-            scratch(7, tall, width),
+            scratch(5, tall, width),
             scratch(4, tall, width),
             scratch(tall, width),
             scratch(7, tall, width),
             scratch(tiles, channels, LANE),
-            pltpu.SemaphoreType.DMA((14,)),
+            pltpu.SemaphoreType.DMA((6,)),
             pltpu.SemaphoreType.DMA((10,)),
             pltpu.SemaphoreType.DMA((10,)),
         ],
@@ -880,7 +913,7 @@
             vmem_limit_bytes=24 * MIB, collective_id=2, has_side_effects=True
         ),
         name="sheet",
-    )(acc, *rims, *fields, *halo)
+    )(acc, *rims, *planes)
 
 
 def finish_kernel(total, speed_up, velocity, out, vel_out):
@@ -924,8 +957,7 @@
     velocity,
 ):
     rows_dev, cols_dev = cell_area.shape[1:]
-    n_old, n_new = lax.axis_size("old"), lax.axis_size("new")
-    arrived, ids, halo, acc = send(
+    arrived, ids, planes, acc = send(
         pair_counts,
         pair_rows,
         pair_targets,
@@ -936,9 +968,8 @@
         displacement,
     )
     *rims, acc = scatter(ids, arrived, acc, rows_dev, cols_dev)
-    fields = (cell_area, thickness, displacement)
     acc = pltpu.with_memory_space_constraint(acc, pltpu.VMEM)
-    total, speed_up = sheet(acc, rims, fields, halo, n_new * rows_dev, n_old * cols_dev)
+    total, speed_up = sheet(acc, rims, planes)
     return finish(total, speed_up, velocity)
 
 

time: 100 us -> 100 us (level)
  no operation moved by 1% of the time
where the time goes in v8:
time: 100 us
  Pallas kernels  99.4 us (99%)
    pallas_call x1, Pallas kernels, send(): pl.pallas_call(functools.partial(send_kernel, rows_dev, cols_dev), out_sh...  42.7 us
    pallas_call x1, Pallas kernels, sheet(): pl.pallas_call(sheet_kernel, out_shape=(block, scratch(3, rows_dev, cols_...  28.1 us
    pallas_call x1, Pallas kernels, scatter(): pl.pallas_call(functools.partial(scatter_kernel, rows_dev, cols_dev), out...  25.7 us
    pallas_call x1, Pallas kernels, finish(): pl.pallas_call(finish_kernel, grid=(rows_dev // 8,), out_shape=(jax.Shape...  2.89 us

profile of v8, /device:TPU:1, one launch (start us, length us, event | category | flops | bytes accessed | tf_op | source)
XLA Modules:
  0.0 100.1 jit_solution(5637984020300396712)
XLA Ops:
  0.6 42.7 %send.1 = (f32[128,32,128]{2,1,0:T(8,128)}, s32[128,1,256]{2,1,0:T(1,128)}, f32[5,48,1152]{2,1,0:T(8,128)}, f32[7,48,1152]{2,1,0:T(8,128)}, f32[48,1152]{1,0:T(8,128)}, /*index=5*/f32[65552,128]{1,0:T(8,128)S(1)}) custom-call(s32[1,128]{1,0:T(1,128)} %counts.1, s32[1,128,128]{2,1,0:T(8,128)} %rows_in.1, s32[1,128,128]{2,1,0:T(8,128)} %targets_in.1, ...), custom_call_target="tpu_custom_call" | custom-call | tf_op jit(solution)/shard_map/send/pallas_call | solution.py:419
  43.3 25.7 %scatter.1 = (f32[5,32,1024]{2,1,0:T(8,128)}, f32[4,32,1024]{2,1,0:T(8,128)}, f32[3,32,128]{2,1,0:T(8,128)}, f32[3,32,128]{2,1,0:T(8,128)}, f32[65552,128]{1,0:T(8,128)S(1)}) custom-call(s32[128,1,256]{2,1,0:T(1,128)} %get-tuple-element.15.ids_in, f32[128,32,128]{2,1,0:T(8,128)} %get-tuple-element.16.data_in, ...), custom_call_target="tpu_custom_call", output_to_operand_aliasing={{4}: (2, {})} | custom-call | tf_op jit(solution)/shard_map/scatter/pallas_call | solution.py:617
  69.0 0.0 copy-start
  69.0 28.1 %sheet.1 = (f32[40,32,1152]{2,1,0:T(8,128)S(1)}, f32[3,32,1024]{2,1,0:T(8,128)S(1)}) custom-call(f32[65552,128]{1,0:T(8,128)S(1)} %get-tuple-element.18.refs_0_, f32[5,32,1024]{2,1,0:T(8,128)} %get-tuple-element.19.refs_1_, f32[4,32,1024]{2,1,0:T(8,128)} %get-tuple-element.20.refs_2_, f32[3,32,128]{2,1,0:T(8,128)} %get-tuple-element.21.refs_3_, ...), custom_call_target="tpu_custom_call" | custom-call | tf_op jit(solution)/shard_map/sheet/pallas_call | solution.py:891
  97.2 0.0 copy-done
  97.2 2.9 %finish.1 = (f32[32,32,1024]{2,1,0:T(8,128)}, f32[3,32,1024]{2,1,0:T(8,128)}) custom-call(f32[40,32,1152]{2,1,0:T(8,128)S(1)} %get-tuple-element.26.total, f32[3,32,1024]{2,1,0:T(8,128)S(1)} %get-tuple-element.27.speed_up, f32[3,32,1024]{2,1,0:T(8,128)S(1)} %copy-done), custom_call_target="tpu_custom_call" | custom-call | tf_op jit(solution)/shard_map/finish/pallas_call | solution.py:934
Async XLA Ops:
  69.0 28.2 %copy-start = (f32[3,32,1024]{2,1,0:T(8,128)S(1)}, f32[3,32,1024]{2,1,0:T(8,128)}, u32[]{:S(2)}) copy-start(f32[3,32,1024]{2,1,0:T(8,128)} %velocity.1) | copy-start | bytes 1179652

commit v9 on v8

--- a/solution.py
+++ b/solution.py
@@ -667,7 +667,7 @@
     total, speed = refs[8:10]
     p_halo, refs = refs[10:20], refs[20:]
     resid, first_sum, field, mem, mass, coef, p_own = refs[:7]
-    load_sem, send_sem, recv_sem = refs[7:]
+    load_sem, send_sem, recv_sem, far_send, far_recv = refs[7:]
     p_dn, p_up, p_l, p_r, p_dl, p_dr, p_ul, p_ur, p_d, p_u = p_halo
     channels, width = resid.shape[1:]
     tall = mass.shape[0]
@@ -698,8 +698,8 @@
     pl.semaphore_wait(barrier, 8)
     copies = to_neighbours(
         [
-            rim_high,
-            rim_low,
+            rim_high.at[pl.ds(1, HALO)],
+            rim_low.at[pl.ds(0, HALO - 1)],
             cols_right,
             cols_left,
             cols_right.at[tiles_high],
@@ -709,9 +709,15 @@
             cols_right.at[tiles_high],
             cols_right.at[tiles_low],
         ],
-        p_halo,
+        [p_dn.at[pl.ds(1, HALO)], p_up.at[pl.ds(0, HALO - 1)]] + list(p_halo[2:]),
         send_sem,
         recv_sem,
+    )
+    far_copies = to_neighbours(
+        [rim_high.at[pl.ds(0, 1)], rim_low.at[pl.ds(HALO - 1, 1)]],
+        [p_dn.at[pl.ds(0, 1)], p_up.at[pl.ds(HALO - 1, 1)]],
+        far_send,
+        far_recv,
     )
     for copy in copies[2:] + copies[:2]:
         copy.start()
@@ -819,24 +825,34 @@
         rows_loop(
             HALO + 2 + sweep, rows_dev + HALO - 1 - sweep, functools.partial(sweep_row, sweep)
         )
+        if sweep == 0:
+            for copy in far_copies:
+                copy.start()
 
     for copy in copies[:2]:
         copy.wait()
-    for e in range(HALO):
+    for e in range(1, HALO):
         begin(e, under(e))
     begin(HALO, own(0) + under(HALO))
     begin(rows_dev + HALO, own(rows_dev) + over(0))
-    for e in range(1, HALO):
+    for e in range(1, HALO - 1):
         begin(rows_dev + HALO + e, over(e))
     for sweep in range(ITERS):
+
         def outer_row(k, sweep=sweep):
-            low_end = HALO + 1
             sweep_row(
-                sweep,
-                jnp.where(k < low_end, 1 + sweep + k, rows_dev + HALO - 1 - sweep + k - low_end),
+                sweep, jnp.where(k < HALO, 2 + sweep + k, rows_dev - 1 - sweep + k)
             )
 
-        rows_loop(0, 2 * HALO + 1, outer_row, 3)
+        rows_loop(0, 2 * HALO - 1, outer_row)
+
+    for copy in far_copies:
+        copy.wait()
+    begin(0, under(0))
+    begin(rows_dev + 2 * HALO - 1, over(HALO - 1))
+    for sweep in range(ITERS):
+        sweep_row(sweep, 1 + sweep)
+        sweep_row(sweep, rows_dev + 2 * HALO - 2 - sweep)
 
     anchor = [field[2 + c] for c in range(3)]
     beside = [from_right(x) for x in anchor]
@@ -908,6 +924,8 @@
             pltpu.SemaphoreType.DMA((6,)),
             pltpu.SemaphoreType.DMA((10,)),
             pltpu.SemaphoreType.DMA((10,)),
+            pltpu.SemaphoreType.DMA((2,)),
+            pltpu.SemaphoreType.DMA((2,)),
         ],
         compiler_params=pltpu.CompilerParams(
             vmem_limit_bytes=24 * MIB, collective_id=2, has_side_effects=True

time: 100 us -> 98.7 us (0.987)
  Pallas kernels: 99.4 us -> 97.2 us
    pallas_call x1, Pallas kernels: 28.1 us -> 26 us  [sheet(): pl.pallas_call(sheet_kernel, out_shape=(block, scratch(3, rows_dev, cols_...]
where the time goes in v9:
time: 98.7 us; the launch traced here: 97.9 us
  Pallas kernels  97.2 us (98%)
    pallas_call x1, Pallas kernels, send(): pl.pallas_call(functools.partial(send_kernel, rows_dev, cols_dev), out_sh...  42.7 us
    pallas_call x1, Pallas kernels, sheet(): pl.pallas_call(sheet_kernel, out_shape=(block, scratch(3, rows_dev, cols_...  26 us
    pallas_call x1, Pallas kernels, scatter(): pl.pallas_call(functools.partial(scatter_kernel, rows_dev, cols_dev), out...  25.7 us
    pallas_call x1, Pallas kernels, finish(): pl.pallas_call(finish_kernel, grid=(rows_dev // 8,), out_shape=(jax.Shape...  2.89 us

profile of v9, /device:TPU:1, one launch (start us, length us, event | category | flops | bytes accessed | tf_op | source)
XLA Modules:
  0.0 97.9 jit_solution(16392587946448404673)
XLA Ops:
  0.6 42.7 %send.1 = (f32[128,32,128]{2,1,0:T(8,128)}, s32[128,1,256]{2,1,0:T(1,128)}, f32[5,48,1152]{2,1,0:T(8,128)}, f32[7,48,1152]{2,1,0:T(8,128)}, f32[48,1152]{1,0:T(8,128)}, /*index=5*/f32[65552,128]{1,0:T(8,128)S(1)}) custom-call(s32[1,128]{1,0:T(1,128)} %counts.1, s32[1,128,128]{2,1,0:T(8,128)} %rows_in.1, s32[1,128,128]{2,1,0:T(8,128)} %targets_in.1, ...), custom_call_target="tpu_custom_call" | custom-call | tf_op jit(solution)/shard_map/send/pallas_call | solution.py:419
  43.3 25.7 %scatter.1 = (f32[5,32,1024]{2,1,0:T(8,128)}, f32[4,32,1024]{2,1,0:T(8,128)}, f32[3,32,128]{2,1,0:T(8,128)}, f32[3,32,128]{2,1,0:T(8,128)}, f32[65552,128]{1,0:T(8,128)S(1)}) custom-call(s32[128,1,256]{2,1,0:T(1,128)} %get-tuple-element.15.ids_in, f32[128,32,128]{2,1,0:T(8,128)} %get-tuple-element.16.data_in, ...), custom_call_target="tpu_custom_call", output_to_operand_aliasing={{4}: (2, {})} | custom-call | tf_op jit(solution)/shard_map/scatter/pallas_call | solution.py:617
  69.0 0.0 copy-start
  69.0 26.0 %sheet.1 = (f32[40,32,1152]{2,1,0:T(8,128)S(1)}, f32[3,32,1024]{2,1,0:T(8,128)S(1)}) custom-call(f32[65552,128]{1,0:T(8,128)S(1)} %get-tuple-element.18.refs_0_, f32[5,32,1024]{2,1,0:T(8,128)} %get-tuple-element.19.refs_1_, f32[4,32,1024]{2,1,0:T(8,128)} %get-tuple-element.20.refs_2_, f32[3,32,128]{2,1,0:T(8,128)} %get-tuple-element.21.refs_3_, ...), custom_call_target="tpu_custom_call" | custom-call | tf_op jit(solution)/shard_map/sheet/pallas_call | solution.py:907
  95.0 0.0 copy-done
  95.0 2.9 %finish.1 = (f32[32,32,1024]{2,1,0:T(8,128)}, f32[3,32,1024]{2,1,0:T(8,128)}) custom-call(f32[40,32,1152]{2,1,0:T(8,128)S(1)} %get-tuple-element.26.total, f32[3,32,1024]{2,1,0:T(8,128)S(1)} %get-tuple-element.27.speed_up, f32[3,32,1024]{2,1,0:T(8,128)S(1)} %copy-done), custom_call_target="tpu_custom_call" | custom-call | tf_op jit(solution)/shard_map/finish/pallas_call | solution.py:952
Async XLA Ops:
  69.0 26.0 %copy-start = (f32[3,32,1024]{2,1,0:T(8,128)S(1)}, f32[3,32,1024]{2,1,0:T(8,128)}, u32[]{:S(2)}) copy-start(f32[3,32,1024]{2,1,0:T(8,128)} %velocity.1) | copy-start | bytes 1179652
